TPU v7x, 32 devices: a whole 2x2x4 slice. The times are simulated.
32 devices in a mesh: groups: 2 (over x), ff: 8 (over z, y), var: 2 (over core).
Axes of the slice: x: 2, y: 2, z: 4, core: 2. Of those that a mesh axis runs over, the one named last changes fastest.
Arguments:
- tokens: bfloat16 [128, 8192], P(('groups', 'ff'), 'var'), parts along dimension 0, may hold values from -6 to 6
- gate_weight: bfloat16 [8192, 16384], P('var', 'ff'), may hold values from -0.0625 to 0.0625
- up_weight: bfloat16 [8192, 16384], P('var', 'ff'), may hold values from -0.0625 to 0.0625
- down_weight: bfloat16 [16384, 8192], P('ff', 'var'), may hold values from -0.046875 to 0.046875
- shrink_gu: bfloat16 [64, 32, 8192], P(('groups', 'ff'), None, 'var'), parts along dimension 0, may hold values from -0.0625 to 0.0625
- expand_gu: bfloat16 [64, 2, 16, 16384], P(('groups', 'ff'), None, 'var'), parts along dimension 0, may hold values from -1.5 to 1.5
- shrink_down: bfloat16 [64, 16, 16384], P(('groups', 'ff')), parts along dimension 0, may hold values from -0.046875 to 0.046875
- expand_down: bfloat16 [64, 16, 8192], P(('groups', 'ff'), None, 'var'), parts along dimension 0, may hold values from -1.5 to 1.5
- variant_ids: int32 [128, 1], P('groups'), parts along dimension 0, may hold values from 0 to 31; in each aligned block of 64 rows (0 to 63, 64 to 127, ...) at most 8 rows name the same one
- variant_slot: int32 [64], P('groups'), parts along dimension 0, may hold values from 0 to 31, each once
Outputs:
- mixed: bfloat16 [128, 8192], P(('groups', 'ff'), 'var'), parts along dimension 0
There are 2 independent parts, one for each index of `groups`. A program takes and returns all parts, laid end to end along the dimension named above; an argument that names none is the same for every part. Nothing has to cross between parts.
Inputs may be any that keep to these rules, and one draw needn't show every extreme that they name: `variant_ids`: no variant is used by more than 8 rows of a group and one variant by exactly 8; every variant is used by some row. `variant_slot`: each slot holds exactly one variant.
All inputs are finite; a program needn't handle non-finite values.
Results may differ from a plain program's by a relative error of at most 0.0063.
Values may be sent and summed in bfloat16 or wider, within the bound.
No kernel may reach another device: no remote copies, remote signals or barrier semaphores. Data moves between devices by JAX's collectives and lax.ppermute only.
A program may use at most 192 MiB of HBM per device.

v0:
```python
import functools

import jax
import jax.numpy as jnp
from jax import lax
from jax.experimental import pallas as pl
from jax.experimental.pallas import tpu as pltpu
from jax.sharding import PartitionSpec as P

MOST = 8
DIRECT = 8
MINE, NEXT, STEP, PLACE = range(4)
USUAL = 16
BF = jnp.bfloat16
F32 = jnp.float32
I32 = jnp.int32
MIB = 1024 * 1024


def dot(a, b):
    return jnp.dot(a, b, preferred_element_type=F32)


def dot_last(a, b):
    return lax.dot_general(a, b, (((1,), (1,)), ((), ())), preferred_element_type=F32)


def params(mib):
    return pltpu.CompilerParams(vmem_limit_bytes=int(mib * MIB))


def cost(flops, moved):
    return pl.CostEstimate(flops=flops, bytes_accessed=moved, transcendentals=0)


SCALARS = pl.BlockSpec(memory_space=pltpu.SMEM)
WHOLE = pl.BlockSpec(memory_space=pltpu.VMEM)
FAR = pl.BlockSpec(memory_space=pltpu.HBM)


def fixed(array):
    zeros = (0,) * array.ndim
    return pl.BlockSpec(array.shape, lambda *_: zeros)


def one_hot(count, cell):
    lines = lax.broadcasted_iota(I32, (count, cell.shape[1]), 0)
    return (lines == cell).astype(F32).astype(BF)


def dot_first(a, b):
    return lax.dot_general(a, b, (((0,), (0,)), ((), ())), preferred_element_type=F32)


class Ways:
    def __init__(self):
        self.shards = lax.axis_size("ff")
        self.fast = 2 if self.shards % 2 == 0 else 1
        self.slow = self.shards // self.fast
        self.direct = self.shards <= DIRECT
        me = lax.axis_index("ff").astype(I32)
        steps = jnp.arange(self.shards, dtype=I32)
        if self.direct:
            slow = (me // self.fast - steps % self.slow) % self.slow
            fast = (me % self.fast - steps // self.slow) % self.fast
            self.order = slow * self.fast + fast
        else:
            self.order = steps

    def arrival(self):
        steps = jnp.arange(self.shards, dtype=I32)
        if not self.direct:
            return steps
        return steps % self.slow * self.fast + steps // self.slow

    def back(self, a, c):
        S, F = self.slow, self.fast
        return [(s * F + f, (s - a) % S * F + (f - c) % F) for s in range(S) for f in range(F)]

    def gather(self, block):
        if not self.direct:
            return list(lax.all_gather(block, "ff"))
        got = [block] + [
            lax.ppermute(block, "ff", self.back(-a, 0)) for a in range(1, self.slow)
        ]
        for c in range(1, self.fast):
            got += [lax.ppermute(part, "ff", self.back(0, -c)) for part in got[: self.slow]]
        return got

    def spread(self, blocks):
        return lax.all_to_all(blocks, "ff", 0, 0, tiled=True)

    def slow_steps(self, blocks):
        got = [blocks[0]] + [None] * (self.slow - 1)
        for a in range(1, self.slow):
            got[(-a) % self.slow] = lax.ppermute(blocks[a], "ff", self.back(a, 0))
        return got


def stage_kernel(
    here_ref, there_ref, x_ref, expand_ref, shrink_ref, kept_ref, near_ref, far_ref, held_ref, sems
):
    half = near_ref.shape[1] // (sems.shape[0] - 1)
    copies = []
    for side, (at_ref, out) in enumerate(((there_ref, far_ref), (here_ref, near_ref))):
        for b in range(sems.shape[0] - 1):
            columns = pl.ds(pl.multiple_of(at_ref[b] * half, half), half)
            put = out.at[:, pl.ds(b * half, half)]
            copies.append(pltpu.make_async_copy(expand_ref.at[:, columns], put, sems.at[b, side]))
    copies.append(pltpu.make_async_copy(shrink_ref, held_ref, sems.at[sems.shape[0] - 1, 0]))
    copies.append(pltpu.make_async_copy(x_ref, kept_ref, sems.at[sems.shape[0] - 1, 1]))
    for copy in copies:
        copy.start()
    for copy in copies:
        copy.wait()


def stage(at_here, at_there, x, expand, shrink):
    depth, width = expand.shape
    shards = at_here.shape[0]
    out = jax.ShapeDtypeStruct((depth, width // 2), BF)
    return pl.pallas_call(
        stage_kernel,
        out_shape=(
            jax.ShapeDtypeStruct(x.shape, BF),
            out,
            out,
            jax.ShapeDtypeStruct(shrink.shape, BF),
        ),
        in_specs=[SCALARS, SCALARS, FAR, FAR, FAR],
        out_specs=(WHOLE,) * 4,
        scratch_shapes=[pltpu.SemaphoreType.DMA((shards + 1, 2))],
        compiler_params=params(51),
        cost_estimate=cost(0, 2 * (2 * expand.size + 2 * shrink.size)),
    )(at_here, at_there, x, expand, shrink)


def low_in_kernel(count, shrink_ref, mask_ref, *refs):
    parts, x_ref, out_ref = refs[:count], refs[count], refs[count + 1]
    x = jnp.concatenate([part[...].astype(F32) for part in parts], axis=0).astype(BF)
    x_ref[...] = x

    @pl.when(pl.program_id(0) == 0)
    def _():
        out_ref[...] = jnp.zeros_like(out_ref)

    out_ref[...] += jnp.where(mask_ref[...] > 0, dot_last(x, shrink_ref[...]), 0.0)


def low_in_pairs(parts, shrink, mask):
    count = len(parts)
    own_rows, width = parts[0].shape
    rows, block = count * own_rows, min(1024, width)
    return pl.pallas_call(
        lambda *refs: low_in_kernel(count, *refs),
        out_shape=(
            jax.ShapeDtypeStruct((rows, width), BF),
            jax.ShapeDtypeStruct(mask.shape, F32),
        ),
        grid=(width // block,),
        in_specs=[pl.BlockSpec((shrink.shape[0], block), lambda n: (0, n)), fixed(mask)]
        + [pl.BlockSpec((own_rows, block), lambda n: (0, n))] * count,
        out_specs=(pl.BlockSpec((rows, block), lambda n: (0, n)), fixed(mask)),
        compiler_params=params(16),
        cost_estimate=cost(2 * rows * width * shrink.shape[0], 2 * shrink.size + 4 * rows * width),
    )(shrink, mask, *parts)


def expand_kernel(
    cap, fast, own_ref, got_ref, marks_ref, cols_ref, near_ref, far_ref, *out_refs
):
    low = (own_ref[...] + got_ref[...]).astype(BF)
    picked = dot(one_hot(cap, marks_ref[MINE : MINE + 1]), low).astype(BF)
    lhs = jnp.concatenate([dot(picked, cols_ref[kind]) for kind in range(2)], axis=0).astype(BF)
    tall = lhs.shape[0]
    half = out_refs[0].shape[1]
    count = near_ref.shape[1] // half
    for b in range(count):
        here = pl.ds(b * half, half)
        both = jnp.concatenate([near_ref[:, here], far_ref[:, here]], axis=0)
        at = b % (count // fast)
        out_refs[b * fast // count][pl.ds(at * tall, tall)] = dot(lhs, both).astype(BF)


def expand_rows(own, got, marks, cols, near, far, shards, cap, fast):
    depth, width = near.shape
    out = jax.ShapeDtypeStruct((2 * cap * shards // fast, width // shards), BF)
    return pl.pallas_call(
        functools.partial(expand_kernel, cap, fast),
        out_shape=(out,) * fast,
        compiler_params=params(16),
        cost_estimate=cost(8 * cap * depth * width, 4 * (depth + cap) * width),
    )(own, got, marks, cols, near, far)


def base_kernel(side_ref, x_ref, gate_ref, up_ref, out_ref, held, sums, sems):
    half = held.shape[2]
    chunks = sems.shape[1]
    depth = held.shape[1] // chunks
    columns = pl.ds(pl.multiple_of(side_ref[0] * half, half), half)
    copies = []
    for c in range(chunks):
        here = pl.ds(c * depth, depth)
        for kind, weight in enumerate((gate_ref, up_ref)):
            copy = pltpu.make_async_copy(
                weight.at[here, columns], held.at[kind, here], sems.at[kind, c]
            )
            copy.start()
            copies.append((kind, here, copy))
    for kind, here, copy in copies:
        copy.wait()
        part = dot(x_ref[:, here], held[kind, here])
        sums[kind] = part if here.start == 0 else sums[kind] + part
    out_ref[...] = sums[...].astype(out_ref.dtype)


def base_half(side, x, gate_weight, up_weight, half, kind):
    rows, width = x.shape
    chunks = max(width // 512, 1)
    return pl.pallas_call(
        base_kernel,
        out_shape=jax.ShapeDtypeStruct((2, rows, half), kind),
        in_specs=[SCALARS, WHOLE, FAR, FAR],
        out_specs=WHOLE,
        scratch_shapes=[
            pltpu.VMEM((2, width, half), BF),
            pltpu.VMEM((2, rows, half), F32),
            pltpu.SemaphoreType.DMA((2, chunks)),
        ],
        compiler_params=params(48),
        cost_estimate=cost(4 * rows * width * half, 4 * width * half + 2 * rows * width),
    )(side, x, gate_weight, up_weight)


def hidden_kernel(cap, count, own_ref, got_ref, marks_ref, arrive_ref, *refs):
    parts, hid_ref, out_refs = refs[:count], refs[count], refs[count + 1 :]
    rows, half = hid_ref.shape
    cells = sum(part.shape[0] for part in parts)
    place = one_hot(cells, arrive_ref[0:1] * cap + arrive_ref[1:2])
    tall = out_refs[0].shape[0]
    leave = marks_ref[STEP : STEP + 1] * cap + marks_ref[PLACE : PLACE + 1]
    send = one_hot(tall * len(out_refs), leave)
    block = min(256, half)
    for first in range(0, half, block):
        here = pl.ds(first, block)
        delta = dot_first(place, jnp.concatenate([part[:, here] for part in parts], axis=0))
        gate = own_ref[0, :, here] + got_ref[0, :, here].astype(F32) + delta[:rows]
        up = own_ref[1, :, here] + got_ref[1, :, here].astype(F32) + delta[rows:]
        hidden = (gate / (1.0 + jnp.exp(-gate)) * up).astype(BF)
        hid_ref[:, here] = hidden
        sent = dot(send, hidden).astype(BF)
        for n, out_ref in enumerate(out_refs):
            out_ref[:, here] = sent[n * tall : (n + 1) * tall]


def hidden_half(own, got, parts, marks, arrive, cap, shards, count):
    rows, half = own.shape[1:]
    cells = shards * cap
    return pl.pallas_call(
        functools.partial(hidden_kernel, cap, len(parts)),
        out_shape=(jax.ShapeDtypeStruct((rows, half), BF),)
        + (jax.ShapeDtypeStruct((cells // count, half), BF),) * count,
        compiler_params=params(40),
        cost_estimate=cost(10 * half * cells * rows, 2 * half * (6 * rows + 3 * cells)),
    )(own, got, marks, arrive, *parts)


def relay_kernel(own_ref, got_ref, *out_refs):
    cap = out_refs[0].shape[0] // 2
    for a, out_ref in enumerate(out_refs):
        here = pl.ds(a * cap, cap)
        out_ref[:cap] = own_ref[here]
        out_ref[cap:] = got_ref[here]


def relay(own, got, count):
    tall, half = own.shape
    return pl.pallas_call(
        relay_kernel,
        out_shape=(jax.ShapeDtypeStruct((2 * tall // count, half), BF),) * count,
        compiler_params=params(16),
        cost_estimate=cost(0, 8 * tall * half),
    )(own, got)


def down_kernel(core_ref, near_ref, far_ref, weight_ref, *refs):
    out_refs, held, sems = refs[:-2], refs[-2], refs[-1]
    chunks = sems.shape[1]
    half, width = held.shape[1:]
    block = width // chunks
    tall = out_refs[0].shape[0]
    copies = []
    for c in range(chunks):
        here = pl.ds(c * block, block)
        for side, at in enumerate((core_ref[0], 1 - core_ref[0])):
            lines = pl.ds(pl.multiple_of(at * half, half), half)
            copy = pltpu.make_async_copy(
                weight_ref.at[lines, here], held.at[side, :, here], sems.at[side, c]
            )
            copy.start()
            copies.append(copy)
    for c in range(chunks):
        here = pl.ds(c * block, block)
        copies[2 * c].wait()
        copies[2 * c + 1].wait()
        total = dot(near_ref[...], held[0, :, here]) + dot(far_ref[...], held[1, :, here])
        for n, out_ref in enumerate(out_refs):
            out_ref[:, here] = total[n * tall : (n + 1) * tall].astype(out_ref.dtype)


def down_base(core, near, far, weight, kinds):
    rows, half = near.shape
    width = weight.shape[1]
    chunks = max(width // 512, 1)
    outs = tuple(jax.ShapeDtypeStruct((rows // len(kinds), width), kind) for kind in kinds)
    return pl.pallas_call(
        down_kernel,
        out_shape=outs,
        in_specs=[SCALARS, WHOLE, WHOLE, FAR],
        out_specs=(WHOLE,) * len(outs),
        scratch_shapes=[
            pltpu.VMEM((2, half, width), BF),
            pltpu.SemaphoreType.DMA((2, chunks)),
        ],
        compiler_params=params(48),
        cost_estimate=cost(4 * rows * half * width, 4 * half * width + 4 * rows * width),
    )(core, near, far, weight)


def low_out_kernel(cap, count, at_ref, marks_ref, slot_ref, shrink_ref, *refs):
    parts, out_ref = refs[:count], refs[count]
    half = parts[0].shape[1]
    blocks = [part[r : r + cap] for r in range(0, parts[0].shape[0], cap) for part in parts]
    pairs = jnp.zeros(out_ref.shape, F32)
    for b, block in enumerate(blocks):
        columns = pl.ds(pl.multiple_of(at_ref[b] * half, half), half)
        pairs += dot_last(block, shrink_ref[:, columns])
    mask = dot(one_hot(cap, marks_ref[MINE : MINE + 1]), slot_ref[...])
    out_ref[...] = jnp.where(mask > 0.5, pairs, 0.0)


def low_out_pairs(at, marks, slot_mask, shrink, parts, cap):
    count = len(parts)
    half = parts[0].shape[1]
    depth = shrink.shape[0]
    return pl.pallas_call(
        functools.partial(low_out_kernel, cap, count),
        out_shape=jax.ShapeDtypeStruct((cap, depth), F32),
        in_specs=[SCALARS] + [WHOLE] * (3 + count),
        compiler_params=params(16),
        cost_estimate=cost(
            2 * cap * depth * at.shape[0] * half, 2 * at.shape[0] * half * (depth + cap)
        ),
    )(at, marks, slot_mask, shrink, *parts)


def add_kernel(owners, *refs):
    base_refs, refs = refs[:owners], refs[owners:]
    low_refs, refs = refs[: 2 * owners], refs[2 * owners :]
    marks_ref, expand_refs, out_refs = refs[0], refs[1 : owners + 1], refs[owners + 1 :]
    rows = base_refs[0].shape[0]
    spreads = []
    for n in range(owners):
        low = (low_refs[2 * n][...] + low_refs[2 * n + 1][...]).astype(BF)
        pick = one_hot(low.shape[0], marks_ref[MINE + n : MINE + n + 1, :rows])
        spreads.append(dot_first(pick, low).astype(BF))
    spread = jnp.concatenate(spreads, axis=1)
    own_rows, width = out_refs[0].shape
    block = min(1024, width)
    for first in range(0, width, block):
        here = pl.ds(first, block)
        expand = jnp.concatenate([ref[:, here] for ref in expand_refs], axis=0)
        total = dot(spread, expand)
        for base_ref in base_refs:
            total += base_ref[:, here].astype(F32)
        for b, out_ref in enumerate(out_refs):
            out_ref[:, here] = total[b * own_rows : (b + 1) * own_rows].astype(BF)


def add_delta(bases, lows, marks, expands, count):
    rows, width = bases[0].shape
    depth = expands[0].shape[0]
    return pl.pallas_call(
        functools.partial(add_kernel, len(bases)),
        out_shape=(jax.ShapeDtypeStruct((rows // count, width), BF),) * count,
        compiler_params=params(32),
        cost_estimate=cost(
            2 * rows * depth * len(bases) * width, width * (6 * rows + 2 * depth) * len(bases)
        ),
    )(*bases, *lows, marks, *expands)


def tied(first, *others):
    return lax.optimization_barrier((first, *others))


def per_device(
    tokens,
    gate_weight,
    up_weight,
    down_weight,
    shrink_gu,
    expand_gu,
    shrink_down,
    expand_down,
    variant_ids,
    variant_slot,
):
    ways = Ways()
    shards, order = ways.shards, ways.order
    me = lax.axis_index("ff").astype(I32)
    core = lax.axis_index("var").astype(I32)
    groups = lax.axis_size("groups")
    own_rows, width = tokens.shape
    rows = own_rows * shards
    slots = shrink_gu.shape[0]
    variants = variant_slot.shape[0]
    rank = shrink_down.shape[1]
    half_rank = expand_gu.shape[2]
    half = gate_weight.shape[1] // 2
    most = min(slots * MOST, rows)
    here = core.reshape(1)
    there = 1 - here
    at_here = 2 * order + core
    at_there = 2 * order + 1 - core
    split = ways.fast if ways.direct else 1
    swap = lambda a: lax.ppermute(a, "var", [(0, 1), (1, 0)])

    token_parts = ways.gather(tokens)
    if ways.direct:
        variant_ids, variant_slot, at_here, at_there, token_parts[ways.slow + 1] = tied(
            variant_ids, variant_slot, at_here, at_there, token_parts[ways.slow + 1]
        )
    named = jnp.concatenate([variant_ids[:, 0], variant_slot]).reshape(1, -1)
    all_named = [named]
    for turn in range(1, groups):
        pairs = [(g, (g + turn) % groups) for g in range(groups)]
        all_named.append(lax.ppermute(named, "groups", pairs))
    all_named = jnp.concatenate(all_named)
    kept, near, far, shrink_in = stage(
        at_here,
        at_there,
        tokens,
        expand_gu.reshape(slots * 2 * half_rank, -1),
        shrink_gu.reshape(slots * 2 * rank, width),
    )
    far = swap(far)
    if ways.direct:
        token_parts[0] = kept

    ids, id_slots = all_named[:, :rows], all_named[:, rows:]
    matches = ids[:, :, None] == jnp.arange(variants, dtype=I32)
    slot_row = jnp.sum(jnp.where(matches, id_slots[:, None, :], 0), axis=2)
    owner = slot_row // slots
    index = jnp.arange(rows, dtype=I32)
    earlier = (owner[:, :, None] == owner[:, None, :]) & (index[None, :] < index[:, None])
    place = jnp.sum(earlier.astype(I32), axis=2)
    highest = jnp.max(place).reshape(1)
    slot_row, place = slot_row[0], place[0]
    where_row = order[:, None] == jnp.arange(shards, dtype=I32)[None, :]
    turned = lambda a: jnp.sum(
        jnp.where(where_row[:, :, None], a.reshape(1, shards, own_rows), 0), axis=1
    ).reshape(rows)
    slot_row, place = turned(slot_row), turned(place)
    owner = slot_row // slots
    of_block = owner[:, None] == order[None, :]
    step = jnp.sum(jnp.where(of_block, jnp.arange(shards, dtype=I32)[None, :], 0), axis=1)
    arrival = jnp.sum(jnp.where(of_block, ways.arrival()[None, :], 0), axis=1)
    local = slot_row - me * slots
    next_owner = order[ways.slow % shards]
    marks = jnp.stack(
        [jnp.where(owner == me, place, -1), jnp.where(owner == next_owner, place, -1), step, place]
    )
    arrive = jnp.stack(
        [jnp.concatenate([2 * arrival, 2 * arrival + 1]), jnp.concatenate([place, place])]
    )
    kinds = jnp.arange(2, dtype=I32)
    in_cols = jnp.arange(slots * 2 * rank, dtype=I32)
    mask_in = (local[:, None] == (in_cols // (2 * rank))[None, :]).astype(F32)
    out_cols = jnp.arange(slots * rank, dtype=I32)
    slot_mask = (local[:, None] == (out_cols // rank)[None, :]).astype(BF)
    rank_at = in_cols % rank
    kind_at = in_cols // rank % 2
    row_at = in_cols // (2 * rank) * (2 * half_rank) + kind_at * half_rank + rank_at % half_rank
    depth = slots * 2 * half_rank
    both_cols = jnp.arange(2 * depth, dtype=I32)
    wanted = row_at + jnp.where(rank_at // half_rank == core, 0, depth)
    hit = wanted[:, None] == both_cols[None, :]
    cols = (hit[None] & (kind_at[None, :] == kinds[:, None])[:, :, None]).astype(BF)

    x, low_own = low_in_pairs(token_parts, shrink_in, mask_in)
    low_got = swap(low_own)

    def partial_sums(cap):
        made = expand_rows(low_own, low_got, marks, cols, near, far, shards, cap, split)
        held, *made = tied(x, *made)
        expand = expand_down.reshape(slots * rank, width)
        if split == 2:
            beside = lax.ppermute(made[1], "ff", ways.back(0, 1))
            base_there = base_half(there, held, gate_weight, up_weight, half, BF)
            base_there, beside, expand = tied(base_there, beside, expand)
            made = relay(made[0], beside, ways.slow)
            held, *made = tied(held, *made)
            delta = ways.slow_steps(made)
            expand_beside = lax.ppermute(expand, "ff", ways.back(0, 1))
        else:
            base_there = base_half(there, held, gate_weight, up_weight, half, BF)
            delta = ways.spread(made[0].reshape(shards, 2 * cap, half))
            delta = [delta.reshape(2 * shards * cap, half)]
        base_got = swap(base_there)
        base_own = base_half(here, held, gate_weight, up_weight, half, F32)
        if split == 2:
            base_own, expand_beside = tied(base_own, expand_beside)
        hidden, *sent = hidden_half(
            base_own, base_got, delta, marks, arrive, cap, shards, split
        )
        hidden_far = swap(hidden)
        shrink = shrink_down.reshape(slots * rank, -1)
        if split == 2:
            beside = lax.ppermute(sent[1], "ff", ways.back(0, 1))
            base, base_sent = down_base(here, hidden, hidden_far, down_weight, (F32, BF))
            base_sent, beside = tied(base_sent, beside)
            base_beside = lax.ppermute(base_sent, "ff", ways.back(0, 1))
            got = ways.slow_steps(relay(sent[0], beside, ways.slow))
        else:
            (base,) = down_base(here, hidden, hidden_far, down_weight, (F32,))
            got = [ways.spread(sent[0].reshape(shards, cap, half)).reshape(shards * cap, half)]
        if split == 2:
            base_beside, *got = tied(base_beside, *got)
        base, *got = tied(base, *got)
        out_own = low_out_pairs(at_here, marks, slot_mask, shrink, got, cap)
        out_got = swap(out_own)
        if split == 1:
            parts = add_delta([base], [out_own, out_got], marks, [expand], shards)
            return list(ways.spread(jnp.stack(parts)))
        out_beside = lax.ppermute(out_own, "ff", ways.back(0, 1))
        across = [
            (2 * f + v, 2 * g + 1 - v) for f, g in ways.back(0, 1) for v in range(2)
        ]
        out_across = lax.ppermute(out_own, ("ff", "var"), across)
        parts = add_delta(
            [base, base_beside],
            [out_own, out_got, out_beside, out_across],
            marks,
            [expand, expand_beside],
            ways.slow,
        )
        return ways.slow_steps(parts)

    if most <= USUAL:
        parts = partial_sums(most)
    else:
        parts = lax.cond(
            highest[0] < USUAL, lambda: partial_sums(USUAL), lambda: partial_sums(most)
        )
    return sum(part.astype(F32) for part in parts).astype(BF)


def solution(mesh):
    placed = (
        P(("groups", "ff"), "var"),
        P("var", "ff"),
        P("var", "ff"),
        P("ff", "var"),
        P(("groups", "ff"), None, "var"),
        P(("groups", "ff"), None, "var", None),
        P(("groups", "ff"), None, None),
        P(("groups", "ff"), None, "var"),
        P("groups", None),
        P("groups"),
    )
    return jax.shard_map(
        per_device,
        mesh=mesh,
        in_specs=placed,
        out_specs=P(("groups", "ff"), "var"),
        check_vma=False,
    )
```

profile of v0, /device:TPU:0, one launch (start us, length us, event | category | flops | bytes accessed | tf_op | source)
XLA Modules:
  0.0 87.1 jit_solution(17957776140041601116)
XLA Ops:
  0.0 4.0 %collective-permute-start.39 = (bf16[8,4096]{1,0:T(8,128)(2,1)}, bf16[8,4096]{1,0:T(8,128)(2,1)S(1)}, u32[]{:S(2)}, u32[]{:S(2)}) collective-permute-start(bf16[8,4096]{1,0:T(8,128)(2,1)} %x_ref.1), channel_id=1, source_target_pairs={{0,8},{2,10},{4,12},{6,14},{8,0},{10,2},{12,4},{14,6},{1,9},{3,11}... | collective-permute-start | bytes 196616 | tf_op jit(solution)/shard_map/ppermute | solution.py:84
  4.0 1.6 %collective-permute-start.36 = (bf16[8,4096]{1,0:T(8,128)(2,1)}, bf16[8,4096]{1,0:T(8,128)(2,1)S(1)}, u32[]{:S(2)}, u32[]{:S(2)}) collective-permute-start(bf16[8,4096]{1,0:T(8,128)(2,1)} %x_ref.1), channel_id=1, source_target_pairs={{0,4},{2,6},{4,8},{6,10},{8,12},{10,14},{12,0},{14,2},{1,5},{3,7},... | collective-permute-start | bytes 196616 | tf_op jit(solution)/shard_map/ppermute | solution.py:84
  5.6 1.5 %collective-permute-start.41 = (bf16[8,4096]{1,0:T(8,128)(2,1)}, bf16[8,4096]{1,0:T(8,128)(2,1)S(1)}, u32[]{:S(2)}, u32[]{:S(2)}) collective-permute-start(bf16[8,4096]{1,0:T(8,128)(2,1)} %x_ref.1), channel_id=1, source_target_pairs={{0,2},{2,0},{4,6},{6,4},{8,10},{10,8},{12,14},{14,12},{1,3},{3,1},... | collective-permute-start | bytes 196616 | tf_op jit(solution)/shard_map/ppermute | solution.py:87
  7.1 2.2 %collective-permute-start.40 = (bf16[8,4096]{1,0:T(8,128)(2,1)}, bf16[8,4096]{1,0:T(8,128)(2,1)S(1)}, u32[]{:S(2)}, u32[]{:S(2)}) collective-permute-start(bf16[8,4096]{1,0:T(8,128)(2,1)} %x_ref.1), channel_id=1, source_target_pairs={{0,12},{2,14},{4,0},{6,2},{8,4},{10,6},{12,8},{14,10},{1,13},{3,15... | collective-permute-start | bytes 196616 | tf_op jit(solution)/shard_map/ppermute | solution.py:84
  14.0 1.2 %collective-permute-done.37.refs_7_ = bf16[8,4096]{1,0:T(8,128)(2,1)S(1)} collective-permute-done((bf16[8,4096]{1,0:T(8,128)(2,1)S(1)}, bf16[8,4096]{1,0:T(8,128)(2,1)S(1)}, u32[]{:S(2)}, u32[]{:S(2)}) %collective-permute-start.37) | collective-permute-done | bytes 65568 | tf_op jit(solution)/shard_map/ppermute | solution.py:87
  16.0 1.5 %collective-permute-start.38 = (s32[1,96]{1,0:T(1,128)S(1)}, s32[1,96]{1,0:T(1,128)S(1)}, u32[]{:S(2)}, u32[]{:S(2)}) collective-permute-start(s32[1,96]{1,0:T(1,128)S(1)} %add_bitcast_fusion), channel_id=1, source_target_pairs={{0,16},{16,0},{1,17},{17,1},{2,18},{18,2},{3,19},{19,3},{4,20},{20... | collective-permute-start | bytes 1160 | tf_op jit(solution)/shard_map/ppermute | solution.py:438
  18.3 3.7 %shard_map.100 = (bf16[8,4096]{1,0:T(8,128)(2,1)S(1)}, bf16[64,8192]{1,0:T(8,128)(2,1)}, bf16[64,8192]{1,0:T(8,128)(2,1)S(1)}, bf16[128,4096]{1,0:T(8,128)(2,1)S(1)}) custom-call(s32[8]{0:T(128)S(1)} %multiply_add_fusion.1.here_ref, s32[8]{0:T(128)S(1)} %get-tuple-element.228.there_ref, bf16[8,4096]{1,0:T(8,128)(2,1)S(1)} %copy-done, ...), custom_call_target="tpu_custom_call" | custom-call | bytes 6291456 | tf_op jit(solution)/shard_map/pallas_call | solution.py:122
  27.2 59.3 %conditional.3 = (bf16[8,4096]{1,0:T(8,128)(2,1)S(1)}, f32[8,4096]{1,0:T(8,128)S(1)}, f32[8,4096]{1,0:T(8,128)S(1)}, f32[8,4096]{1,0:T(8,128)S(1)}) conditional(s32[]{:T(128)} %convert_element_type.52, (s32[]{:T(128)}, f32[64,128]{1,0:T(8,128)S(1)}, f32[64,128]{1,0:T(8,128)S(1)}, s32[4,64]{1,0:T(4,128)S(1)}, bf16[2,128,128]{2,1,0:T(8,128)(2,1)S(1)}, ...), branch_computations={%region_7.8_spmd, %region_8.9_spmd} | conditional | flops 3590422528 | bytes 89817896
  27.4 2.2 %branch_1_fun.9 = (bf16[128,1024]{1,0:T(8,128)(2,1)S(1)}, bf16[128,1024]{1,0:T(8,128)(2,1)S(1)}) custom-call(f32[64,128]{1,0:T(8,128)S(1)} %get-tuple-element.152.own_ref, f32[64,128]{1,0:T(8,128)S(1)} %get-tuple-element.153.got_ref, s32[4,64]{1,0:T(4,128)S(1)} %get-tuple-element.154.marks_ref.refs_6_, bf16[2,128,128]{2,1,0:T(8,128)(2,1)S(1)} %get-tuple-element.155.cols_ref, ...), custom_call_target="tpu_custom_call" | custom-call | flops 67108864 | bytes 2621440 | tf_op jit(solution)/shard_map/cond/branch_1_fun/pallas_call | solution.py:188
  30.6 6.3 %branch_1_fun.10 = bf16[2,64,1024]{2,1,0:T(8,128)(2,1)S(1)} custom-call(s32[1]{0:T(128)S(6)} %sub.78.side_ref, bf16[64,4096]{1,0:T(8,128)(2,1)S(1)} %get-tuple-element.171.x_ref, bf16[4096,2048]{1,0:T(8,128)(2,1)} %get-tuple-element.162.gate_ref, bf16[4096,2048]{1,0:T(8,128)(2,1)} %get-tuple-element.163.up_ref), custom_call_target="tpu_custom_call" | custom-call | flops 1073741824 | bytes 17301504 | tf_op jit(solution)/shard_map/cond/branch_1_fun/pallas_call | solution.py:220
  39.3 2.5 %collective-permute-start.22 = (bf16[64,1024]{1,0:T(8,128)(2,1)S(1)}, bf16[64,1024]{1,0:T(8,128)(2,1)S(1)}, u32[]{:S(2)}, u32[]{:S(2)}) collective-permute-start(bf16[64,1024]{1,0:T(8,128)(2,1)S(1)} %get-tuple-element.178), channel_id=1, source_target_pairs={{0,8},{2,10},{4,12},{6,14},{8,0},{10,2},{12,4},{14,6},{1,9},{3,11}... | collective-permute-start | bytes 393224 | tf_op jit(solution)/shard_map/cond/branch_1_fun/ppermute | solution.py:96
  41.8 2.8 %collective-permute-start.23 = (bf16[64,1024]{1,0:T(8,128)(2,1)S(1)}, bf16[64,1024]{1,0:T(8,128)(2,1)S(1)}, u32[]{:S(2)}, u32[]{:S(2)}) collective-permute-start(bf16[64,1024]{1,0:T(8,128)(2,1)S(1)} %get-tuple-element.179), channel_id=1, source_target_pairs={{0,12},{2,14},{4,0},{6,2},{8,4},{10,6},{12,8},{14,10},{1,13},{3,15... | collective-permute-start | bytes 393224 | tf_op jit(solution)/shard_map/cond/branch_1_fun/ppermute | solution.py:96
  44.6 6.2 %branch_1_fun.12.own_ref = f32[2,64,1024]{2,1,0:T(8,128)S(1)} custom-call(s32[1]{0:T(128)} %bitcast.3.side_ref.core_ref, bf16[64,4096]{1,0:T(8,128)(2,1)S(1)} %get-tuple-element.171.x_ref, bf16[4096,2048]{1,0:T(8,128)(2,1)} %get-tuple-element.162.gate_ref, bf16[4096,2048]{1,0:T(8,128)(2,1)} %get-tuple-element.163.up_ref), custom_call_target="tpu_custom_call" | custom-call | flops 1073741824 | bytes 17301504 | tf_op jit(solution)/shard_map/cond/branch_1_fun/pallas_call | solution.py:220
  50.9 1.2 %collective-permute-done.22.refs_2_ = bf16[64,1024]{1,0:T(8,128)(2,1)S(1)} collective-permute-done((bf16[64,1024]{1,0:T(8,128)(2,1)S(1)}, bf16[64,1024]{1,0:T(8,128)(2,1)S(1)}, u32[]{:S(2)}, u32[]{:S(2)}) %collective-permute-start.22) | collective-permute-done | bytes 131104 | tf_op jit(solution)/shard_map/cond/branch_1_fun/ppermute | solution.py:96
  54.2 6.5 %branch_1_fun.14 = (f32[32,4096]{1,0:T(8,128)S(1)}, bf16[32,4096]{1,0:T(8,128)(2,1)S(1)}) custom-call(s32[1]{0:T(128)} %bitcast.3.side_ref.core_ref, bf16[64,1024]{1,0:T(8,128)(2,1)S(1)} %get-tuple-element.180.near_ref, bf16[64,1024]{1,0:T(8,128)(2,1)S(1)} %collective-permute-done.24.far_ref, bf16[2048,4096]{1,0:T(8,128)(2,1)} %get-tuple-element.181.weight_ref), custom_call_target="tpu_custom_call" | custom-call | flops 1073741824 | bytes 17825792 | tf_op jit(solution)/shard_map/cond/branch_1_fun/pallas_call | solution.py:316
  61.6 3.0 %collective-permute-start.27 = (bf16[32,1024]{1,0:T(8,128)(2,1)S(1)}, bf16[32,1024]{1,0:T(8,128)(2,1)S(1)}, u32[]{:S(2)}, u32[]{:S(2)}) collective-permute-start(bf16[32,1024]{1,0:T(8,128)(2,1)S(1)} %get-tuple-element.189), channel_id=1, source_target_pairs={{0,4},{2,6},{4,8},{6,10},{8,12},{10,14},{12,0},{14,2},{1,5},{3,7},... | collective-permute-start | bytes 196616 | tf_op jit(solution)/shard_map/cond/branch_1_fun/ppermute | solution.py:96
  64.6 2.4 %collective-permute-start.28 = (bf16[32,1024]{1,0:T(8,128)(2,1)S(1)}, bf16[32,1024]{1,0:T(8,128)(2,1)S(1)}, u32[]{:S(2)}, u32[]{:S(2)}) collective-permute-start(bf16[32,1024]{1,0:T(8,128)(2,1)S(1)} %get-tuple-element.190), channel_id=1, source_target_pairs={{0,8},{2,10},{4,12},{6,14},{8,0},{10,2},{12,4},{14,6},{1,9},{3,11}... | collective-permute-start | bytes 196616 | tf_op jit(solution)/shard_map/cond/branch_1_fun/ppermute | solution.py:96
  67.0 2.4 %collective-permute-done.27.refs_1_ = bf16[32,1024]{1,0:T(8,128)(2,1)S(1)} collective-permute-done((bf16[32,1024]{1,0:T(8,128)(2,1)S(1)}, bf16[32,1024]{1,0:T(8,128)(2,1)S(1)}, u32[]{:S(2)}, u32[]{:S(2)}) %collective-permute-start.27) | collective-permute-done | bytes 65568 | tf_op jit(solution)/shard_map/cond/branch_1_fun/ppermute | solution.py:96
  69.4 2.0 %collective-permute-done.28.refs_2_ = bf16[32,1024]{1,0:T(8,128)(2,1)S(1)} collective-permute-done((bf16[32,1024]{1,0:T(8,128)(2,1)S(1)}, bf16[32,1024]{1,0:T(8,128)(2,1)S(1)}, u32[]{:S(2)}, u32[]{:S(2)}) %collective-permute-start.28) | collective-permute-done | bytes 65568 | tf_op jit(solution)/shard_map/cond/branch_1_fun/ppermute | solution.py:96
  74.8 1.2 %collective-permute-done.32.refs_5_ = f32[16,64]{1,0:T(8,128)S(1)} collective-permute-done((f32[16,64]{1,0:T(8,128)S(1)}, f32[16,64]{1,0:T(8,128)S(1)}, u32[]{:S(2)}, u32[]{:S(2)}) %collective-permute-start.32) | collective-permute-done | bytes 4128 | tf_op jit(solution)/shard_map/cond/branch_1_fun/ppermute | solution.py:540
  77.4 2.0 %collective-permute-start.33 = (bf16[8,4096]{1,0:T(8,128)(2,1)S(1)}, bf16[8,4096]{1,0:T(8,128)(2,1)S(1)}, u32[]{:S(2)}, u32[]{:S(2)}) collective-permute-start(bf16[8,4096]{1,0:T(8,128)(2,1)S(1)} %get-tuple-element.207), channel_id=1, source_target_pairs={{0,4},{2,6},{4,8},{6,10},{8,12},{10,14},{12,0},{14,2},{1,5},{3,7},... | collective-permute-start | bytes 196616 | tf_op jit(solution)/shard_map/cond/branch_1_fun/ppermute | solution.py:96
  80.3 1.5 %collective-permute-start.35 = (bf16[8,4096]{1,0:T(8,128)(2,1)S(1)}, bf16[8,4096]{1,0:T(8,128)(2,1)S(1)}, u32[]{:S(2)}, u32[]{:S(2)}) collective-permute-start(bf16[8,4096]{1,0:T(8,128)(2,1)S(1)} %get-tuple-element.209), channel_id=1, source_target_pairs={{0,12},{2,14},{4,0},{6,2},{8,4},{10,6},{12,8},{14,10},{1,13},{3,15... | collective-permute-start | bytes 196616 | tf_op jit(solution)/shard_map/cond/branch_1_fun/ppermute | solution.py:96
  81.8 2.4 %collective-permute-done.33 = bf16[8,4096]{1,0:T(8,128)(2,1)S(1)} collective-permute-done((bf16[8,4096]{1,0:T(8,128)(2,1)S(1)}, bf16[8,4096]{1,0:T(8,128)(2,1)S(1)}, u32[]{:S(2)}, u32[]{:S(2)}) %collective-permute-start.33) | collective-permute-done | bytes 65568 | tf_op jit(solution)/shard_map/cond/branch_1_fun/ppermute | solution.py:96
  84.2 2.0 %collective-permute-done.34 = bf16[8,4096]{1,0:T(8,128)(2,1)S(1)} collective-permute-done((bf16[8,4096]{1,0:T(8,128)(2,1)S(1)}, bf16[8,4096]{1,0:T(8,128)(2,1)S(1)}, u32[]{:S(2)}, u32[]{:S(2)}) %collective-permute-start.34) | collective-permute-done | bytes 65568 | tf_op jit(solution)/shard_map/cond/branch_1_fun/ppermute | solution.py:96
  (93 shorter events, 23.2 us)
Async XLA Ops:
  0.0 12.0 %collective-permute-start.39 = (bf16[8,4096]{1,0:T(8,128)(2,1)}, bf16[8,4096]{1,0:T(8,128)(2,1)S(1)}, u32[]{:S(2)}, u32[]{:S(2)}) collective-permute-start(bf16[8,4096]{1,0:T(8,128)(2,1)} %x_ref.1), channel_id=1, source_target_pairs={{0,8},{2,10},{4,12},{6,14},{8,0},{10,2},{12,4},{14,6},{1,9},{3,11}... | collective-permute-start | bytes 196616 | tf_op jit(solution)/shard_map/ppermute | solution.py:84
  4.0 6.9 %collective-permute-start.36 = (bf16[8,4096]{1,0:T(8,128)(2,1)}, bf16[8,4096]{1,0:T(8,128)(2,1)S(1)}, u32[]{:S(2)}, u32[]{:S(2)}) collective-permute-start(bf16[8,4096]{1,0:T(8,128)(2,1)} %x_ref.1), channel_id=1, source_target_pairs={{0,4},{2,6},{4,8},{6,10},{8,12},{10,14},{12,0},{14,2},{1,5},{3,7},... | collective-permute-start | bytes 196616 | tf_op jit(solution)/shard_map/ppermute | solution.py:84
  5.6 17.8 %collective-permute-start.41 = (bf16[8,4096]{1,0:T(8,128)(2,1)}, bf16[8,4096]{1,0:T(8,128)(2,1)S(1)}, u32[]{:S(2)}, u32[]{:S(2)}) collective-permute-start(bf16[8,4096]{1,0:T(8,128)(2,1)} %x_ref.1), channel_id=1, source_target_pairs={{0,2},{2,0},{4,6},{6,4},{8,10},{10,8},{12,14},{14,12},{1,3},{3,1},... | collective-permute-start | bytes 196616 | tf_op jit(solution)/shard_map/ppermute | solution.py:87
  7.1 5.9 %collective-permute-start.40 = (bf16[8,4096]{1,0:T(8,128)(2,1)}, bf16[8,4096]{1,0:T(8,128)(2,1)S(1)}, u32[]{:S(2)}, u32[]{:S(2)}) collective-permute-start(bf16[8,4096]{1,0:T(8,128)(2,1)} %x_ref.1), channel_id=1, source_target_pairs={{0,12},{2,14},{4,0},{6,2},{8,4},{10,6},{12,8},{14,10},{1,13},{3,15... | collective-permute-start | bytes 196616 | tf_op jit(solution)/shard_map/ppermute | solution.py:84
  11.0 4.3 %collective-permute-start.37 = (bf16[8,4096]{1,0:T(8,128)(2,1)S(1)}, bf16[8,4096]{1,0:T(8,128)(2,1)S(1)}, u32[]{:S(2)}, u32[]{:S(2)}) collective-permute-start(bf16[8,4096]{1,0:T(8,128)(2,1)S(1)} %collective-permute-done.36.refs_3_), channel_id=1, source_target_pairs={{0,2},{2,0},{4,6},{6,4},{8,10},{10,8},{12,14},{14,12},{1,3},{3,1},... | collective-permute-start | bytes 196616 | tf_op jit(solution)/shard_map/ppermute | solution.py:87
  12.0 11.4 %collective-permute-start.42 = (bf16[8,4096]{1,0:T(8,128)(2,1)S(1)}, bf16[8,4096]{1,0:T(8,128)(2,1)S(1)}, u32[]{:S(2)}, u32[]{:S(2)}) collective-permute-start(bf16[8,4096]{1,0:T(8,128)(2,1)S(1)} %collective-permute-done.39.refs_4_), channel_id=1, source_target_pairs={{0,2},{2,0},{4,6},{6,4},{8,10},{10,8},{12,14},{14,12},{1,3},{3,1},... | collective-permute-start | bytes 196616 | tf_op jit(solution)/shard_map/ppermute | solution.py:87
  13.0 10.4 %collective-permute-start.43 = (bf16[8,4096]{1,0:T(8,128)(2,1)S(1)}, bf16[8,4096]{1,0:T(8,128)(2,1)S(1)}, u32[]{:S(2)}, u32[]{:S(2)}) collective-permute-start(bf16[8,4096]{1,0:T(8,128)(2,1)S(1)} %collective-permute-done.40.refs_5_), channel_id=1, source_target_pairs={{0,2},{2,0},{4,6},{6,4},{8,10},{10,8},{12,14},{14,12},{1,3},{3,1},... | collective-permute-start | bytes 196616 | tf_op jit(solution)/shard_map/ppermute | solution.py:87
  16.0 6.1 %collective-permute-start.38 = (s32[1,96]{1,0:T(1,128)S(1)}, s32[1,96]{1,0:T(1,128)S(1)}, u32[]{:S(2)}, u32[]{:S(2)}) collective-permute-start(s32[1,96]{1,0:T(1,128)S(1)} %add_bitcast_fusion), channel_id=1, source_target_pairs={{0,16},{16,0},{1,17},{17,1},{2,18},{18,2},{3,19},{19,3},{4,20},{20... | collective-permute-start | bytes 1160 | tf_op jit(solution)/shard_map/ppermute | solution.py:438
  22.0 5.1 %collective-permute-start.45 = (bf16[64,8192]{1,0:T(8,128)(2,1)S(1)}, bf16[64,8192]{1,0:T(8,128)(2,1)}, u32[]{:S(2)}, u32[]{:S(2)}) collective-permute-start(bf16[64,8192]{1,0:T(8,128)(2,1)S(1)} %get-tuple-element.234), channel_id=1, source_target_pairs={{0,1},{1,0},{2,3},{3,2},{4,5},{5,4},{6,7},{7,6},{8,9},{9,8},{10,11... | collective-permute-start | bytes 3145736 | tf_op jit(solution)/shard_map/ppermute | solution.py:427
  29.5 8.3 %collective-permute-start.18 = (bf16[128,1024]{1,0:T(8,128)(2,1)S(1)}, bf16[128,1024]{1,0:T(8,128)(2,1)S(1)}, u32[]{:S(2)}, u32[]{:S(2)}) collective-permute-start(bf16[128,1024]{1,0:T(8,128)(2,1)S(1)} %get-tuple-element.164), channel_id=1, source_target_pairs={{0,2},{2,0},{4,6},{6,4},{8,10},{10,8},{12,14},{14,12},{1,3},{3,1},... | collective-permute-start | bytes 786440 | tf_op jit(solution)/shard_map/cond/branch_1_fun/ppermute | solution.py:499
  37.8 13.0 %collective-permute-start.19 = (bf16[64,4096]{1,0:T(8,128)(2,1)S(1)}, bf16[64,4096]{1,0:T(8,128)(2,1)S(1)}, u32[]{:S(2)}, u32[]{:S(2)}) collective-permute-start(bf16[64,4096]{1,0:T(8,128)(2,1)S(1)} %bitcast.22), channel_id=1, source_target_pairs={{0,2},{2,0},{4,6},{6,4},{8,10},{10,8},{12,14},{14,12},{1,3},{3,1},... | collective-permute-start | bytes 1572872 | tf_op jit(solution)/shard_map/cond/branch_1_fun/ppermute | solution.py:505
  38.8 13.3 %collective-permute-start.20 = (bf16[2,64,1024]{2,1,0:T(8,128)(2,1)S(1)}, bf16[2,64,1024]{2,1,0:T(8,128)(2,1)S(1)}, u32[]{:S(2)}, u32[]{:S(2)}) collective-permute-start(bf16[2,64,1024]{2,1,0:T(8,128)(2,1)S(1)} %branch_1_fun.10), channel_id=1, source_target_pairs={{0,1},{1,0},{2,3},{3,2},{4,5},{5,4},{6,7},{7,6},{8,9},{9,8},{10,11... | collective-permute-start | bytes 786440 | tf_op jit(solution)/shard_map/cond/branch_1_fun/ppermute | solution.py:427
  38.9 12.0 %collective-permute-start.21 = (bf16[64,1024]{1,0:T(8,128)(2,1)S(1)}, bf16[64,1024]{1,0:T(8,128)(2,1)S(1)}, u32[]{:S(2)}, u32[]{:S(2)}) collective-permute-start(bf16[64,1024]{1,0:T(8,128)(2,1)S(1)} %get-tuple-element.177), channel_id=1, source_target_pairs={{0,4},{2,6},{4,8},{6,10},{8,12},{10,14},{12,0},{14,2},{1,5},{3,7},... | collective-permute-start | bytes 393224 | tf_op jit(solution)/shard_map/cond/branch_1_fun/ppermute | solution.py:96
  39.3 12.9 %collective-permute-start.22 = (bf16[64,1024]{1,0:T(8,128)(2,1)S(1)}, bf16[64,1024]{1,0:T(8,128)(2,1)S(1)}, u32[]{:S(2)}, u32[]{:S(2)}) collective-permute-start(bf16[64,1024]{1,0:T(8,128)(2,1)S(1)} %get-tuple-element.178), channel_id=1, source_target_pairs={{0,8},{2,10},{4,12},{6,14},{8,0},{10,2},{12,4},{14,6},{1,9},{3,11}... | collective-permute-start | bytes 393224 | tf_op jit(solution)/shard_map/cond/branch_1_fun/ppermute | solution.py:96
  41.8 10.4 %collective-permute-start.23 = (bf16[64,1024]{1,0:T(8,128)(2,1)S(1)}, bf16[64,1024]{1,0:T(8,128)(2,1)S(1)}, u32[]{:S(2)}, u32[]{:S(2)}) collective-permute-start(bf16[64,1024]{1,0:T(8,128)(2,1)S(1)} %get-tuple-element.179), channel_id=1, source_target_pairs={{0,12},{2,14},{4,0},{6,2},{8,4},{10,6},{12,8},{14,10},{1,13},{3,15... | collective-permute-start | bytes 393224 | tf_op jit(solution)/shard_map/cond/branch_1_fun/ppermute | solution.py:96
  52.8 7.9 %collective-permute-start.25 = (bf16[64,1024]{1,0:T(8,128)(2,1)S(1)}, bf16[64,1024]{1,0:T(8,128)(2,1)S(1)}, u32[]{:S(2)}, u32[]{:S(2)}) collective-permute-start(bf16[64,1024]{1,0:T(8,128)(2,1)S(1)} %get-tuple-element.184), channel_id=1, source_target_pairs={{0,2},{2,0},{4,6},{6,4},{8,10},{10,8},{12,14},{14,12},{1,3},{3,1},... | collective-permute-start | bytes 393224 | tf_op jit(solution)/shard_map/cond/branch_1_fun/ppermute | solution.py:520
  60.7 11.3 %collective-permute-start.26 = (bf16[32,4096]{1,0:T(8,128)(2,1)S(1)}, bf16[32,4096]{1,0:T(8,128)(2,1)S(1)}, u32[]{:S(2)}, u32[]{:S(2)}) collective-permute-start(bf16[32,4096]{1,0:T(8,128)(2,1)S(1)} %get-tuple-element.185), channel_id=1, source_target_pairs={{0,2},{2,0},{4,6},{6,4},{8,10},{10,8},{12,14},{14,12},{1,3},{3,1},... | collective-permute-start | bytes 786440 | tf_op jit(solution)/shard_map/cond/branch_1_fun/ppermute | solution.py:523
  61.6 7.9 %collective-permute-start.27 = (bf16[32,1024]{1,0:T(8,128)(2,1)S(1)}, bf16[32,1024]{1,0:T(8,128)(2,1)S(1)}, u32[]{:S(2)}, u32[]{:S(2)}) collective-permute-start(bf16[32,1024]{1,0:T(8,128)(2,1)S(1)} %get-tuple-element.189), channel_id=1, source_target_pairs={{0,4},{2,6},{4,8},{6,10},{8,12},{10,14},{12,0},{14,2},{1,5},{3,7},... | collective-permute-start | bytes 196616 | tf_op jit(solution)/shard_map/cond/branch_1_fun/ppermute | solution.py:96
  64.6 6.8 %collective-permute-start.28 = (bf16[32,1024]{1,0:T(8,128)(2,1)S(1)}, bf16[32,1024]{1,0:T(8,128)(2,1)S(1)}, u32[]{:S(2)}, u32[]{:S(2)}) collective-permute-start(bf16[32,1024]{1,0:T(8,128)(2,1)S(1)} %get-tuple-element.190), channel_id=1, source_target_pairs={{0,8},{2,10},{4,12},{6,14},{8,0},{10,2},{12,4},{14,6},{1,9},{3,11}... | collective-permute-start | bytes 196616 | tf_op jit(solution)/shard_map/cond/branch_1_fun/ppermute | solution.py:96
  67.0 5.0 %collective-permute-start.29 = (bf16[32,1024]{1,0:T(8,128)(2,1)S(1)}, bf16[32,1024]{1,0:T(8,128)(2,1)S(1)}, u32[]{:S(2)}, u32[]{:S(2)}) collective-permute-start(bf16[32,1024]{1,0:T(8,128)(2,1)S(1)} %get-tuple-element.191), channel_id=1, source_target_pairs={{0,12},{2,14},{4,0},{6,2},{8,4},{10,6},{12,8},{14,10},{1,13},{3,15... | collective-permute-start | bytes 196616 | tf_op jit(solution)/shard_map/cond/branch_1_fun/ppermute | solution.py:96
  73.2 3.7 %collective-permute-start.31 = (f32[16,64]{1,0:T(8,128)S(1)}, f32[16,64]{1,0:T(8,128)S(1)}, u32[]{:S(2)}, u32[]{:S(2)}) collective-permute-start(f32[16,64]{1,0:T(8,128)S(1)} %branch_1_fun.16.refs_2_), channel_id=1, source_target_pairs={{0,2},{2,0},{4,6},{6,4},{8,10},{10,8},{12,14},{14,12},{1,3},{3,1},... | collective-permute-start | bytes 12296 | tf_op jit(solution)/shard_map/cond/branch_1_fun/ppermute | solution.py:536
  77.4 6.9 %collective-permute-start.33 = (bf16[8,4096]{1,0:T(8,128)(2,1)S(1)}, bf16[8,4096]{1,0:T(8,128)(2,1)S(1)}, u32[]{:S(2)}, u32[]{:S(2)}) collective-permute-start(bf16[8,4096]{1,0:T(8,128)(2,1)S(1)} %get-tuple-element.207), channel_id=1, source_target_pairs={{0,4},{2,6},{4,8},{6,10},{8,12},{10,14},{12,0},{14,2},{1,5},{3,7},... | collective-permute-start | bytes 196616 | tf_op jit(solution)/shard_map/cond/branch_1_fun/ppermute | solution.py:96
  79.4 6.9 %collective-permute-start.34 = (bf16[8,4096]{1,0:T(8,128)(2,1)S(1)}, bf16[8,4096]{1,0:T(8,128)(2,1)S(1)}, u32[]{:S(2)}, u32[]{:S(2)}) collective-permute-start(bf16[8,4096]{1,0:T(8,128)(2,1)S(1)} %get-tuple-element.208), channel_id=1, source_target_pairs={{0,8},{2,10},{4,12},{6,14},{8,0},{10,2},{12,4},{14,6},{1,9},{3,11}... | collective-permute-start | bytes 196616 | tf_op jit(solution)/shard_map/cond/branch_1_fun/ppermute | solution.py:96
  80.3 6.0 %collective-permute-start.35 = (bf16[8,4096]{1,0:T(8,128)(2,1)S(1)}, bf16[8,4096]{1,0:T(8,128)(2,1)S(1)}, u32[]{:S(2)}, u32[]{:S(2)}) collective-permute-start(bf16[8,4096]{1,0:T(8,128)(2,1)S(1)} %get-tuple-element.209), channel_id=1, source_target_pairs={{0,12},{2,14},{4,0},{6,2},{8,4},{10,6},{12,8},{14,10},{1,13},{3,15... | collective-permute-start | bytes 196616 | tf_op jit(solution)/shard_map/cond/branch_1_fun/ppermute | solution.py:96
  (7 other events, 39.0 us)
where the time goes:
time: 87.4 us; the launch traced here: 87.1 us
  starting transfers between devices  35.9 us (41%)
  Pallas kernels  28 us (32%)
  waiting for transfers between devices  16 us (18%)
  other arithmetic  3.88 us (4%)
  local copies, waits for them, and re-layouts  1.99 us (2%)
    ppermute x9, starting transfers between devices, slow_steps(): got[-a % self.slow] = lax.ppermute(blocks[a], 'ff', self.back(a, 0))  15.7 us
    pallas_call x2, Pallas kernels, base_half(): pl.pallas_call(base_kernel, out_shape=jax.ShapeDtypeStruct((2, rows, half...  12.5 us
    ppermute x9, waiting for transfers between devices, slow_steps(): got[-a % self.slow] = lax.ppermute(blocks[a], 'ff', self.back(a, 0))  10.5 us
    ppermute x3, starting transfers between devices, gather(): lax.ppermute(block, 'ff', self.back(-a, 0))  7.86 us
    pallas_call x1, Pallas kernels, down_base(): pl.pallas_call(down_kernel, out_shape=outs, in_specs=[SCALARS, WHOLE, WHO...  6.54 us
    ppermute x4, starting transfers between devices, gather(): lax.ppermute(part, 'ff', self.back(0, -c))  4.55 us
    pallas_call x1, Pallas kernels, stage(): pl.pallas_call(stage_kernel, out_shape=(jax.ShapeDtypeStruct(x.shape, BF)...  3.69 us
    pallas_call x1, Pallas kernels, expand_rows(): pl.pallas_call(functools.partial(expand_kernel, cap, fast), out_shape=(ou...  2.16 us
  transfers between devices with their start and end apart: 28, of which 12 were waited for; matrix products, arithmetic and copies ran while one was open for 5% of the time, Pallas kernels for 27%

commit v1 on v0

--- a/solution.py
+++ b/solution.py
@@ -77,15 +77,16 @@
         S, F = self.slow, self.fast
         return [(s * F + f, (s - a) % S * F + (f - c) % F) for s in range(S) for f in range(F)]
 
-    def gather(self, block):
+    def gather(self, block, other):
         if not self.direct:
-            return list(lax.all_gather(block, "ff"))
+            return list(lax.all_gather(block, "ff")), other
         got = [block] + [
             lax.ppermute(block, "ff", self.back(-a, 0)) for a in range(1, self.slow)
         ]
+        other, got[1] = tied(other, got[1])
         for c in range(1, self.fast):
             got += [lax.ppermute(part, "ff", self.back(0, -c)) for part in got[: self.slow]]
-        return got
+        return got, other
 
     def spread(self, blocks):
         return lax.all_to_all(blocks, "ff", 0, 0, tiled=True)
@@ -97,42 +98,26 @@
         return got
 
 
-def stage_kernel(
-    here_ref, there_ref, x_ref, expand_ref, shrink_ref, kept_ref, near_ref, far_ref, held_ref, sems
-):
-    half = near_ref.shape[1] // (sems.shape[0] - 1)
-    copies = []
-    for side, (at_ref, out) in enumerate(((there_ref, far_ref), (here_ref, near_ref))):
-        for b in range(sems.shape[0] - 1):
-            columns = pl.ds(pl.multiple_of(at_ref[b] * half, half), half)
-            put = out.at[:, pl.ds(b * half, half)]
-            copies.append(pltpu.make_async_copy(expand_ref.at[:, columns], put, sems.at[b, side]))
-    copies.append(pltpu.make_async_copy(shrink_ref, held_ref, sems.at[sems.shape[0] - 1, 0]))
-    copies.append(pltpu.make_async_copy(x_ref, kept_ref, sems.at[sems.shape[0] - 1, 1]))
+def stage_kernel(*refs):
+    count = len(refs) // 2
+    sems = refs[2 * count]
+    copies = [pltpu.make_async_copy(refs[n], refs[count + n], sems.at[n]) for n in range(count)]
     for copy in copies:
         copy.start()
     for copy in copies:
         copy.wait()
 
 
-def stage(at_here, at_there, x, expand, shrink):
-    depth, width = expand.shape
-    shards = at_here.shape[0]
-    out = jax.ShapeDtypeStruct((depth, width // 2), BF)
+def stage(*arrays):
     return pl.pallas_call(
         stage_kernel,
-        out_shape=(
-            jax.ShapeDtypeStruct(x.shape, BF),
-            out,
-            out,
-            jax.ShapeDtypeStruct(shrink.shape, BF),
-        ),
-        in_specs=[SCALARS, SCALARS, FAR, FAR, FAR],
-        out_specs=(WHOLE,) * 4,
-        scratch_shapes=[pltpu.SemaphoreType.DMA((shards + 1, 2))],
-        compiler_params=params(51),
-        cost_estimate=cost(0, 2 * (2 * expand.size + 2 * shrink.size)),
-    )(at_here, at_there, x, expand, shrink)
+        out_shape=tuple(jax.ShapeDtypeStruct(array.shape, array.dtype) for array in arrays),
+        in_specs=[FAR] * len(arrays),
+        out_specs=(WHOLE,) * len(arrays),
+        scratch_shapes=[pltpu.SemaphoreType.DMA((len(arrays),))],
+        compiler_params=params(52),
+        cost_estimate=cost(0, sum(4 * array.size for array in arrays)),
+    )(*arrays)
 
 
 def low_in_kernel(count, shrink_ref, mask_ref, *refs):
@@ -167,30 +152,33 @@
 
 
 def expand_kernel(
-    cap, fast, own_ref, got_ref, marks_ref, cols_ref, near_ref, far_ref, *out_refs
+    cap, fast, at_ref, own_ref, got_ref, marks_ref, cols_ref, near_ref, far_ref, *out_refs
 ):
     low = (own_ref[...] + got_ref[...]).astype(BF)
     picked = dot(one_hot(cap, marks_ref[MINE : MINE + 1]), low).astype(BF)
     lhs = jnp.concatenate([dot(picked, cols_ref[kind]) for kind in range(2)], axis=0).astype(BF)
     tall = lhs.shape[0]
     half = out_refs[0].shape[1]
-    count = near_ref.shape[1] // half
+    count = at_ref.shape[0]
     for b in range(count):
-        here = pl.ds(b * half, half)
+        here = pl.ds(pl.multiple_of(at_ref[b] * half, half), half)
         both = jnp.concatenate([near_ref[:, here], far_ref[:, here]], axis=0)
         at = b % (count // fast)
         out_refs[b * fast // count][pl.ds(at * tall, tall)] = dot(lhs, both).astype(BF)
 
 
-def expand_rows(own, got, marks, cols, near, far, shards, cap, fast):
+def expand_rows(at, own, got, marks, cols, near, far, cap, fast):
     depth, width = near.shape
-    out = jax.ShapeDtypeStruct((2 * cap * shards // fast, width // shards), BF)
+    shards = at.shape[0]
+    half = width // (2 * shards)
+    out = jax.ShapeDtypeStruct((2 * cap * shards // fast, half), BF)
     return pl.pallas_call(
         functools.partial(expand_kernel, cap, fast),
         out_shape=(out,) * fast,
+        in_specs=[SCALARS] + [WHOLE] * 6,
         compiler_params=params(16),
         cost_estimate=cost(8 * cap * depth * width, 4 * (depth + cap) * width),
-    )(own, got, marks, cols, near, far)
+    )(at, own, got, marks, cols, near, far)
 
 
 def base_kernel(side_ref, x_ref, gate_ref, up_ref, out_ref, held, sums, sems):
@@ -283,7 +271,7 @@
     )(own, got)
 
 
-def down_kernel(core_ref, near_ref, far_ref, weight_ref, *refs):
+def down_kernel(start, core_ref, near_ref, far_ref, weight_ref, *refs):
     out_refs, held, sems = refs[:-2], refs[-2], refs[-1]
     chunks = sems.shape[1]
     half, width = held.shape[1:]
@@ -295,7 +283,9 @@
         for side, at in enumerate((core_ref[0], 1 - core_ref[0])):
             lines = pl.ds(pl.multiple_of(at * half, half), half)
             copy = pltpu.make_async_copy(
-                weight_ref.at[lines, here], held.at[side, :, here], sems.at[side, c]
+                weight_ref.at[lines, pl.ds(start + c * block, block)],
+                held.at[side, :, here],
+                sems.at[side, c],
             )
             copy.start()
             copies.append(copy)
@@ -308,13 +298,12 @@
             out_ref[:, here] = total[n * tall : (n + 1) * tall].astype(out_ref.dtype)
 
 
-def down_base(core, near, far, weight, kinds):
+def down_base(core, near, far, weight, start, width, kinds):
     rows, half = near.shape
-    width = weight.shape[1]
     chunks = max(width // 512, 1)
     outs = tuple(jax.ShapeDtypeStruct((rows // len(kinds), width), kind) for kind in kinds)
     return pl.pallas_call(
-        down_kernel,
+        functools.partial(down_kernel, start),
         out_shape=outs,
         in_specs=[SCALARS, WHOLE, WHOLE, FAR],
         out_specs=(WHOLE,) * len(outs),
@@ -354,8 +343,8 @@
     )(at, marks, slot_mask, shrink, *parts)
 
 
-def add_kernel(owners, *refs):
-    base_refs, refs = refs[:owners], refs[owners:]
+def add_kernel(owners, sides, *refs):
+    base_refs, refs = refs[: owners * sides], refs[owners * sides :]
     low_refs, refs = refs[: 2 * owners], refs[2 * owners :]
     marks_ref, expand_refs, out_refs = refs[0], refs[1 : owners + 1], refs[owners + 1 :]
     rows = base_refs[0].shape[0]
@@ -366,26 +355,29 @@
         spreads.append(dot_first(pick, low).astype(BF))
     spread = jnp.concatenate(spreads, axis=1)
     own_rows, width = out_refs[0].shape
-    block = min(1024, width)
+    side = width // sides
+    block = min(1024, side)
     for first in range(0, width, block):
         here = pl.ds(first, block)
+        inside = pl.ds(first % side, block)
         expand = jnp.concatenate([ref[:, here] for ref in expand_refs], axis=0)
         total = dot(spread, expand)
-        for base_ref in base_refs:
-            total += base_ref[:, here].astype(F32)
+        for base_ref in base_refs[first // side :: sides]:
+            total += base_ref[:, inside].astype(F32)
         for b, out_ref in enumerate(out_refs):
             out_ref[:, here] = total[b * own_rows : (b + 1) * own_rows].astype(BF)
 
 
 def add_delta(bases, lows, marks, expands, count):
-    rows, width = bases[0].shape
-    depth = expands[0].shape[0]
-    return pl.pallas_call(
-        functools.partial(add_kernel, len(bases)),
+    owners = len(expands)
+    rows = bases[0].shape[0]
+    depth, width = expands[0].shape
+    return pl.pallas_call(
+        functools.partial(add_kernel, owners, len(bases) // owners),
         out_shape=(jax.ShapeDtypeStruct((rows // count, width), BF),) * count,
         compiler_params=params(32),
         cost_estimate=cost(
-            2 * rows * depth * len(bases) * width, width * (6 * rows + 2 * depth) * len(bases)
+            2 * rows * depth * owners * width, width * (6 * rows + 2 * depth) * owners
         ),
     )(*bases, *lows, marks, *expands)
 
@@ -422,35 +414,27 @@
     here = core.reshape(1)
     there = 1 - here
     at_here = 2 * order + core
-    at_there = 2 * order + 1 - core
     split = ways.fast if ways.direct else 1
     swap = lambda a: lax.ppermute(a, "var", [(0, 1), (1, 0)])
 
-    token_parts = ways.gather(tokens)
+    near = expand_gu.reshape(slots * 2 * half_rank, -1)
+    token_parts, far = ways.gather(tokens, swap(near))
+    shrink_in = shrink_gu.reshape(slots * 2 * rank, width)
     if ways.direct:
-        variant_ids, variant_slot, at_here, at_there, token_parts[ways.slow + 1] = tied(
-            variant_ids, variant_slot, at_here, at_there, token_parts[ways.slow + 1]
+        first_hop = ways.slow + 1
+        variant_ids, variant_slot, near, shrink_in, token_parts[first_hop] = tied(
+            variant_ids, variant_slot, near, shrink_in, token_parts[first_hop]
         )
-    named = jnp.concatenate([variant_ids[:, 0], variant_slot]).reshape(1, -1)
-    all_named = [named]
-    for turn in range(1, groups):
+    all_ids, all_slots = [variant_ids[:, 0]], [variant_slot]
+    for turn in range(1, 1 if ways.direct else groups):
         pairs = [(g, (g + turn) % groups) for g in range(groups)]
-        all_named.append(lax.ppermute(named, "groups", pairs))
-    all_named = jnp.concatenate(all_named)
-    kept, near, far, shrink_in = stage(
-        at_here,
-        at_there,
-        tokens,
-        expand_gu.reshape(slots * 2 * half_rank, -1),
-        shrink_gu.reshape(slots * 2 * rank, width),
-    )
-    far = swap(far)
-    if ways.direct:
-        token_parts[0] = kept
-
-    ids, id_slots = all_named[:, :rows], all_named[:, rows:]
-    matches = ids[:, :, None] == jnp.arange(variants, dtype=I32)
-    slot_row = jnp.sum(jnp.where(matches, id_slots[:, None, :], 0), axis=2)
+        all_ids.append(lax.ppermute(all_ids[0], "groups", pairs))
+        all_slots.append(lax.ppermute(all_slots[0], "groups", pairs))
+    all_ids, all_slots = jnp.stack(all_ids), jnp.stack(all_slots)
+    token_parts[0], near, shrink_in = stage(token_parts[0], near, shrink_in)
+
+    matches = all_ids[:, :, None] == jnp.arange(variants, dtype=I32)
+    slot_row = jnp.sum(jnp.where(matches, all_slots[:, None, :], 0), axis=2)
     owner = slot_row // slots
     index = jnp.arange(rows, dtype=I32)
     earlier = (owner[:, :, None] == owner[:, None, :]) & (index[None, :] < index[:, None])
@@ -492,7 +476,7 @@
     low_got = swap(low_own)
 
     def partial_sums(cap):
-        made = expand_rows(low_own, low_got, marks, cols, near, far, shards, cap, split)
+        made = expand_rows(at_here, low_own, low_got, marks, cols, near, far, cap, split)
         held, *made = tied(x, *made)
         expand = expand_down.reshape(slots * rank, width)
         if split == 2:
@@ -516,22 +500,23 @@
         )
         hidden_far = swap(hidden)
         shrink = shrink_down.reshape(slots * rank, -1)
+        down = functools.partial(down_base, here, hidden, hidden_far, down_weight, 0, width)
         if split == 2:
             beside = lax.ppermute(sent[1], "ff", ways.back(0, 1))
-            base, base_sent = down_base(here, hidden, hidden_far, down_weight, (F32, BF))
+            base, base_sent = down((F32, BF))
             base_sent, beside = tied(base_sent, beside)
             base_beside = lax.ppermute(base_sent, "ff", ways.back(0, 1))
             got = ways.slow_steps(relay(sent[0], beside, ways.slow))
+            base_beside, *got = tied(base_beside, *got)
+            bases = [base, base_beside]
         else:
-            (base,) = down_base(here, hidden, hidden_far, down_weight, (F32,))
+            bases = list(down((F32,)))
             got = [ways.spread(sent[0].reshape(shards, cap, half)).reshape(shards * cap, half)]
-        if split == 2:
-            base_beside, *got = tied(base_beside, *got)
-        base, *got = tied(base, *got)
+        bases[0], *got = tied(bases[0], *got)
         out_own = low_out_pairs(at_here, marks, slot_mask, shrink, got, cap)
         out_got = swap(out_own)
         if split == 1:
-            parts = add_delta([base], [out_own, out_got], marks, [expand], shards)
+            parts = add_delta(bases, [out_own, out_got], marks, [expand], shards)
             return list(ways.spread(jnp.stack(parts)))
         out_beside = lax.ppermute(out_own, "ff", ways.back(0, 1))
         across = [
@@ -539,7 +524,7 @@
         ]
         out_across = lax.ppermute(out_own, ("ff", "var"), across)
         parts = add_delta(
-            [base, base_beside],
+            bases,
             [out_own, out_got, out_beside, out_across],
             marks,
             [expand, expand_beside],

time: 87.4 us -> 87.2 us (level)
  waiting for transfers between devices: 16 us -> 15 us
    ppermute x1 -> x0, starting transfers between devices: 1.49 us -> none  [per_device(): all_named.append(lax.ppermute(named, 'groups', pairs))]
    ppermute x9, starting transfers between devices: 15.7 us -> 16.9 us  [slow_steps(): got[-a % self.slow] = lax.ppermute(blocks[a], 'ff', self.back(a, 0))]
    ppermute x4, starting transfers between devices: 4.55 us -> 5.5 us  [gather(): lax.ppermute(part, 'ff', self.back(0, -c))]
  transfers between devices with their start and end apart: 28 -> 27, of which waited for: 12 -> 12; matrix products, arithmetic and copies ran while one was open for 5% -> 5% of each run, Pallas kernels for 27% -> 26%
where the time goes in v1:
time: 87.2 us; the launch traced here: 87 us
  starting transfers between devices  36.5 us (42%)
  Pallas kernels  28.5 us (33%)
  waiting for transfers between devices  15 us (17%)
  other arithmetic  3.71 us (4%)
  local copies, waits for them, and re-layouts  1.91 us (2%)
    ppermute x9, starting transfers between devices, slow_steps(): got[-a % self.slow] = lax.ppermute(blocks[a], 'ff', self.back(a, 0))  16.9 us
    pallas_call x2, Pallas kernels, base_half(): pl.pallas_call(base_kernel, out_shape=jax.ShapeDtypeStruct((2, rows, half...  12.5 us
    ppermute x9, waiting for transfers between devices, slow_steps(): got[-a % self.slow] = lax.ppermute(blocks[a], 'ff', self.back(a, 0))  10.1 us
    ppermute x3, starting transfers between devices, gather(): lax.ppermute(block, 'ff', self.back(-a, 0))  7.41 us
    pallas_call x1, Pallas kernels, down_base(): pl.pallas_call(functools.partial(down_kernel, start), out_shape=outs, in_...  6.54 us
    ppermute x4, starting transfers between devices, gather(): lax.ppermute(part, 'ff', self.back(0, -c))  5.5 us
    pallas_call x1, Pallas kernels, stage(): pl.pallas_call(stage_kernel, out_shape=tuple((jax.ShapeDtypeStruct(array....  3.42 us
    pallas_call x1, Pallas kernels, expand_rows(): pl.pallas_call(functools.partial(expand_kernel, cap, fast), out_shape=(ou...  2.85 us
  transfers between devices with their start and end apart: 27, of which 12 were waited for; matrix products, arithmetic and copies ran while one was open for 5% of the time, Pallas kernels for 26%

profile of v1, /device:TPU:0, one launch (start us, length us, event | category | flops | bytes accessed | tf_op | source)
XLA Modules:
  0.0 87.0 jit_solution(237218272523729768)
XLA Ops:
  0.5 3.6 %collective-permute-start.39 = (bf16[8,4096]{1,0:T(8,128)(2,1)}, bf16[8,4096]{1,0:T(8,128)(2,1)S(1)}, u32[]{:S(2)}, u32[]{:S(2)}) collective-permute-start(bf16[8,4096]{1,0:T(8,128)(2,1)} %refs_0_.1), channel_id=1, source_target_pairs={{0,8},{2,10},{4,12},{6,14},{8,0},{10,2},{12,4},{14,6},{1,9},{3,11}... | collective-permute-start | bytes 196616 | tf_op jit(solution)/shard_map/ppermute | solution.py:84
  4.0 1.6 %collective-permute-start.37 = (bf16[8,4096]{1,0:T(8,128)(2,1)}, bf16[8,4096]{1,0:T(8,128)(2,1)S(1)}, u32[]{:S(2)}, u32[]{:S(2)}) collective-permute-start(bf16[8,4096]{1,0:T(8,128)(2,1)} %refs_0_.1), channel_id=1, source_target_pairs={{0,4},{2,6},{4,8},{6,10},{8,12},{10,14},{12,0},{14,2},{1,5},{3,7},... | collective-permute-start | bytes 196616 | tf_op jit(solution)/shard_map/ppermute | solution.py:84
  5.6 1.5 %collective-permute-start.41 = (bf16[8,4096]{1,0:T(8,128)(2,1)}, bf16[8,4096]{1,0:T(8,128)(2,1)S(1)}, u32[]{:S(2)}, u32[]{:S(2)}) collective-permute-start(bf16[8,4096]{1,0:T(8,128)(2,1)} %refs_0_.1), channel_id=1, source_target_pairs={{0,2},{2,0},{4,6},{6,4},{8,10},{10,8},{12,14},{14,12},{1,3},{3,1},... | collective-permute-start | bytes 196616 | tf_op jit(solution)/shard_map/ppermute | solution.py:88
  7.1 2.2 %collective-permute-start.40 = (bf16[8,4096]{1,0:T(8,128)(2,1)}, bf16[8,4096]{1,0:T(8,128)(2,1)S(1)}, u32[]{:S(2)}, u32[]{:S(2)}) collective-permute-start(bf16[8,4096]{1,0:T(8,128)(2,1)} %refs_0_.1), channel_id=1, source_target_pairs={{0,12},{2,14},{4,0},{6,2},{8,4},{10,6},{12,8},{14,10},{1,13},{3,15... | collective-permute-start | bytes 196616 | tf_op jit(solution)/shard_map/ppermute | solution.py:84
  10.6 2.0 %collective-permute-start.38 = (bf16[8,4096]{1,0:T(8,128)(2,1)S(1)}, bf16[8,4096]{1,0:T(8,128)(2,1)S(1)}, u32[]{:S(2)}, u32[]{:S(2)}) collective-permute-start(bf16[8,4096]{1,0:T(8,128)(2,1)S(1)} %collective-permute-done.37.refs_3_), channel_id=1, source_target_pairs={{0,2},{2,0},{4,6},{6,4},{8,10},{10,8},{12,14},{14,12},{1,3},{3,1},... | collective-permute-start | bytes 196616 | tf_op jit(solution)/shard_map/ppermute | solution.py:88
  12.6 1.9 %collective-permute-start.43 = (bf16[8,4096]{1,0:T(8,128)(2,1)S(1)}, bf16[8,4096]{1,0:T(8,128)(2,1)S(1)}, u32[]{:S(2)}, u32[]{:S(2)}) collective-permute-start(bf16[8,4096]{1,0:T(8,128)(2,1)S(1)} %collective-permute-done.40.refs_5_), channel_id=1, source_target_pairs={{0,2},{2,0},{4,6},{6,4},{8,10},{10,8},{12,14},{14,12},{1,3},{3,1},... | collective-permute-start | bytes 196616 | tf_op jit(solution)/shard_map/ppermute | solution.py:88
  18.1 3.4 %shard_map.100 = (bf16[8,4096]{1,0:T(8,128)(2,1)S(1)}, bf16[64,16384]{1,0:T(8,128)(2,1)}, bf16[128,4096]{1,0:T(8,128)(2,1)S(1)}) custom-call(bf16[8,4096]{1,0:T(8,128)(2,1)S(1)} %copy-done, bf16[64,16384]{1,0:T(8,128)(2,1)} %bitcast.22, bf16[128,4096]{1,0:T(8,128)(2,1)} %bitcast.23), custom_call_target="tpu_custom_call" | custom-call | bytes 6422528 | tf_op jit(solution)/shard_map/pallas_call | solution.py:112
  24.8 61.5 %conditional.3 = (bf16[8,4096]{1,0:T(8,128)(2,1)S(1)}, f32[8,4096]{1,0:T(8,128)S(1)}, f32[8,4096]{1,0:T(8,128)S(1)}, f32[8,4096]{1,0:T(8,128)S(1)}) conditional(s32[]{:T(128)} %convert_element_type.60, (s32[]{:T(128)}, s32[8]{0:T(128)S(1)}, s32[8]{0:T(128)S(1)}, f32[64,128]{1,0:T(8,128)S(1)}, f32[64,128]{1,0:T(8,128)S(1)}, ...), branch_computations={%region_7.8_spmd, %region_8.9_spmd} | conditional | flops 3724640256 | bytes 84575096
  25.0 2.9 %branch_1_fun.9 = (bf16[128,1024]{1,0:T(8,128)(2,1)S(1)}, bf16[128,1024]{1,0:T(8,128)(2,1)S(1)}) custom-call(s32[8]{0:T(128)S(1)} %multiply_add_fusion.1.at_ref, f32[64,128]{1,0:T(8,128)S(1)} %get-tuple-element.167.own_ref, f32[64,128]{1,0:T(8,128)S(1)} %get-tuple-element.168.got_ref, s32[4,64]{1,0:T(4,128)S(1)} %get-tuple-element.169.marks_ref.refs_6_, ...), custom_call_target="tpu_custom_call" | custom-call | flops 134217728 | bytes 5242880 | tf_op jit(solution)/shard_map/cond/branch_1_fun/pallas_call | solution.py:175
  27.9 1.4 %collective-permute-start.18 = (bf16[128,1024]{1,0:T(8,128)(2,1)S(1)}, bf16[128,1024]{1,0:T(8,128)(2,1)S(1)}, u32[]{:S(2)}, u32[]{:S(2)}) collective-permute-start(bf16[128,1024]{1,0:T(8,128)(2,1)S(1)} %get-tuple-element.179), channel_id=1, source_target_pairs={{0,2},{2,0},{4,6},{6,4},{8,10},{10,8},{12,14},{14,12},{1,3},{3,1},... | collective-permute-start | bytes 786440 | tf_op jit(solution)/shard_map/cond/branch_1_fun/ppermute | solution.py:483
  29.3 6.3 %branch_1_fun.10 = bf16[2,64,1024]{2,1,0:T(8,128)(2,1)S(1)} custom-call(s32[1]{0:T(128)S(6)} %sub.75.side_ref, bf16[64,4096]{1,0:T(8,128)(2,1)S(1)} %get-tuple-element.186.x_ref, bf16[4096,2048]{1,0:T(8,128)(2,1)} %get-tuple-element.177.gate_ref, bf16[4096,2048]{1,0:T(8,128)(2,1)} %get-tuple-element.178.up_ref), custom_call_target="tpu_custom_call" | custom-call | flops 1073741824 | bytes 17301504 | tf_op jit(solution)/shard_map/cond/branch_1_fun/pallas_call | solution.py:208
  36.7 1.3 %collective-permute-start.19 = (bf16[64,4096]{1,0:T(8,128)(2,1)S(1)}, bf16[64,4096]{1,0:T(8,128)(2,1)S(1)}, u32[]{:S(2)}, u32[]{:S(2)}) collective-permute-start(bf16[64,4096]{1,0:T(8,128)(2,1)S(1)} %bitcast.19), channel_id=1, source_target_pairs={{0,2},{2,0},{4,6},{6,4},{8,10},{10,8},{12,14},{14,12},{1,3},{3,1},... | collective-permute-start | bytes 1572872 | tf_op jit(solution)/shard_map/cond/branch_1_fun/ppermute | solution.py:489
  39.2 2.4 %collective-permute-start.22 = (bf16[64,1024]{1,0:T(8,128)(2,1)S(1)}, bf16[64,1024]{1,0:T(8,128)(2,1)S(1)}, u32[]{:S(2)}, u32[]{:S(2)}) collective-permute-start(bf16[64,1024]{1,0:T(8,128)(2,1)S(1)} %get-tuple-element.193), channel_id=1, source_target_pairs={{0,8},{2,10},{4,12},{6,14},{8,0},{10,2},{12,4},{14,6},{1,9},{3,11}... | collective-permute-start | bytes 393224 | tf_op jit(solution)/shard_map/cond/branch_1_fun/ppermute | solution.py:97
  41.6 2.8 %collective-permute-start.23 = (bf16[64,1024]{1,0:T(8,128)(2,1)S(1)}, bf16[64,1024]{1,0:T(8,128)(2,1)S(1)}, u32[]{:S(2)}, u32[]{:S(2)}) collective-permute-start(bf16[64,1024]{1,0:T(8,128)(2,1)S(1)} %get-tuple-element.194), channel_id=1, source_target_pairs={{0,12},{2,14},{4,0},{6,2},{8,4},{10,6},{12,8},{14,10},{1,13},{3,15... | collective-permute-start | bytes 393224 | tf_op jit(solution)/shard_map/cond/branch_1_fun/ppermute | solution.py:97
  44.5 6.2 %branch_1_fun.12.own_ref = f32[2,64,1024]{2,1,0:T(8,128)S(1)} custom-call(s32[1]{0:T(128)} %bitcast.3.side_ref.core_ref, bf16[64,4096]{1,0:T(8,128)(2,1)S(1)} %get-tuple-element.186.x_ref, bf16[4096,2048]{1,0:T(8,128)(2,1)} %get-tuple-element.177.gate_ref, bf16[4096,2048]{1,0:T(8,128)(2,1)} %get-tuple-element.178.up_ref), custom_call_target="tpu_custom_call" | custom-call | flops 1073741824 | bytes 17301504 | tf_op jit(solution)/shard_map/cond/branch_1_fun/pallas_call | solution.py:208
  53.5 6.5 %branch_1_fun.14 = (f32[32,4096]{1,0:T(8,128)S(1)}, bf16[32,4096]{1,0:T(8,128)(2,1)S(1)}) custom-call(s32[1]{0:T(128)} %bitcast.3.side_ref.core_ref, bf16[64,1024]{1,0:T(8,128)(2,1)S(1)} %get-tuple-element.195.near_ref, bf16[64,1024]{1,0:T(8,128)(2,1)S(1)} %collective-permute-done.24.far_ref, bf16[2048,4096]{1,0:T(8,128)(2,1)} %get-tuple-element.196.weight_ref), custom_call_target="tpu_custom_call" | custom-call | flops 1073741824 | bytes 17825792 | tf_op jit(solution)/shard_map/cond/branch_1_fun/pallas_call | solution.py:305
  60.9 3.4 %collective-permute-start.27 = (bf16[32,1024]{1,0:T(8,128)(2,1)S(1)}, bf16[32,1024]{1,0:T(8,128)(2,1)S(1)}, u32[]{:S(2)}, u32[]{:S(2)}) collective-permute-start(bf16[32,1024]{1,0:T(8,128)(2,1)S(1)} %get-tuple-element.204), channel_id=1, source_target_pairs={{0,4},{2,6},{4,8},{6,10},{8,12},{10,14},{12,0},{14,2},{1,5},{3,7},... | collective-permute-start | bytes 196616 | tf_op jit(solution)/shard_map/cond/branch_1_fun/ppermute | solution.py:97
  64.2 2.6 %collective-permute-start.28 = (bf16[32,1024]{1,0:T(8,128)(2,1)S(1)}, bf16[32,1024]{1,0:T(8,128)(2,1)S(1)}, u32[]{:S(2)}, u32[]{:S(2)}) collective-permute-start(bf16[32,1024]{1,0:T(8,128)(2,1)S(1)} %get-tuple-element.205), channel_id=1, source_target_pairs={{0,8},{2,10},{4,12},{6,14},{8,0},{10,2},{12,4},{14,6},{1,9},{3,11}... | collective-permute-start | bytes 196616 | tf_op jit(solution)/shard_map/cond/branch_1_fun/ppermute | solution.py:97
  66.8 2.5 %collective-permute-done.27.refs_1_ = bf16[32,1024]{1,0:T(8,128)(2,1)S(1)} collective-permute-done((bf16[32,1024]{1,0:T(8,128)(2,1)S(1)}, bf16[32,1024]{1,0:T(8,128)(2,1)S(1)}, u32[]{:S(2)}, u32[]{:S(2)}) %collective-permute-start.27) | collective-permute-done | bytes 65568 | tf_op jit(solution)/shard_map/cond/branch_1_fun/ppermute | solution.py:97
  69.3 2.0 %collective-permute-done.28.refs_2_ = bf16[32,1024]{1,0:T(8,128)(2,1)S(1)} collective-permute-done((bf16[32,1024]{1,0:T(8,128)(2,1)S(1)}, bf16[32,1024]{1,0:T(8,128)(2,1)S(1)}, u32[]{:S(2)}, u32[]{:S(2)}) %collective-permute-start.28) | collective-permute-done | bytes 65568 | tf_op jit(solution)/shard_map/cond/branch_1_fun/ppermute | solution.py:97
  77.2 2.0 %collective-permute-start.33 = (bf16[8,4096]{1,0:T(8,128)(2,1)S(1)}, bf16[8,4096]{1,0:T(8,128)(2,1)S(1)}, u32[]{:S(2)}, u32[]{:S(2)}) collective-permute-start(bf16[8,4096]{1,0:T(8,128)(2,1)S(1)} %get-tuple-element.221), channel_id=1, source_target_pairs={{0,4},{2,6},{4,8},{6,10},{8,12},{10,14},{12,0},{14,2},{1,5},{3,7},... | collective-permute-start | bytes 196616 | tf_op jit(solution)/shard_map/cond/branch_1_fun/ppermute | solution.py:97
  80.1 1.5 %collective-permute-start.35 = (bf16[8,4096]{1,0:T(8,128)(2,1)S(1)}, bf16[8,4096]{1,0:T(8,128)(2,1)S(1)}, u32[]{:S(2)}, u32[]{:S(2)}) collective-permute-start(bf16[8,4096]{1,0:T(8,128)(2,1)S(1)} %get-tuple-element.223), channel_id=1, source_target_pairs={{0,12},{2,14},{4,0},{6,2},{8,4},{10,6},{12,8},{14,10},{1,13},{3,15... | collective-permute-start | bytes 196616 | tf_op jit(solution)/shard_map/cond/branch_1_fun/ppermute | solution.py:97
  81.7 2.4 %collective-permute-done.33 = bf16[8,4096]{1,0:T(8,128)(2,1)S(1)} collective-permute-done((bf16[8,4096]{1,0:T(8,128)(2,1)S(1)}, bf16[8,4096]{1,0:T(8,128)(2,1)S(1)}, u32[]{:S(2)}, u32[]{:S(2)}) %collective-permute-start.33) | collective-permute-done | bytes 65568 | tf_op jit(solution)/shard_map/cond/branch_1_fun/ppermute | solution.py:97
  84.1 2.0 %collective-permute-done.34 = bf16[8,4096]{1,0:T(8,128)(2,1)S(1)} collective-permute-done((bf16[8,4096]{1,0:T(8,128)(2,1)S(1)}, bf16[8,4096]{1,0:T(8,128)(2,1)S(1)}, u32[]{:S(2)}, u32[]{:S(2)}) %collective-permute-start.34) | collective-permute-done | bytes 65568 | tf_op jit(solution)/shard_map/cond/branch_1_fun/ppermute | solution.py:97
  (86 shorter events, 21.1 us)
Async XLA Ops:
  0.0 10.6 %collective-permute-start.36 = (bf16[64,16384]{1,0:T(8,128)(2,1)}, bf16[64,16384]{1,0:T(8,128)(2,1)}, u32[]{:S(2)}, u32[]{:S(2)}) collective-permute-start(bf16[64,16384]{1,0:T(8,128)(2,1)} %bitcast.21), channel_id=1, source_target_pairs={{0,1},{1,0},{2,3},{3,2},{4,5},{5,4},{6,7},{7,6},{8,9},{9,8},{10,11... | collective-permute-start | bytes 6291464 | tf_op jit(solution)/shard_map/ppermute | solution.py:418
  0.5 12.1 %collective-permute-start.39 = (bf16[8,4096]{1,0:T(8,128)(2,1)}, bf16[8,4096]{1,0:T(8,128)(2,1)S(1)}, u32[]{:S(2)}, u32[]{:S(2)}) collective-permute-start(bf16[8,4096]{1,0:T(8,128)(2,1)} %refs_0_.1), channel_id=1, source_target_pairs={{0,8},{2,10},{4,12},{6,14},{8,0},{10,2},{12,4},{14,6},{1,9},{3,11}... | collective-permute-start | bytes 196616 | tf_op jit(solution)/shard_map/ppermute | solution.py:84
  4.0 6.5 %collective-permute-start.37 = (bf16[8,4096]{1,0:T(8,128)(2,1)}, bf16[8,4096]{1,0:T(8,128)(2,1)S(1)}, u32[]{:S(2)}, u32[]{:S(2)}) collective-permute-start(bf16[8,4096]{1,0:T(8,128)(2,1)} %refs_0_.1), channel_id=1, source_target_pairs={{0,4},{2,6},{4,8},{6,10},{8,12},{10,14},{12,0},{14,2},{1,5},{3,7},... | collective-permute-start | bytes 196616 | tf_op jit(solution)/shard_map/ppermute | solution.py:84
  5.6 16.0 %collective-permute-start.41 = (bf16[8,4096]{1,0:T(8,128)(2,1)}, bf16[8,4096]{1,0:T(8,128)(2,1)S(1)}, u32[]{:S(2)}, u32[]{:S(2)}) collective-permute-start(bf16[8,4096]{1,0:T(8,128)(2,1)} %refs_0_.1), channel_id=1, source_target_pairs={{0,2},{2,0},{4,6},{6,4},{8,10},{10,8},{12,14},{14,12},{1,3},{3,1},... | collective-permute-start | bytes 196616 | tf_op jit(solution)/shard_map/ppermute | solution.py:88
  7.1 5.5 %collective-permute-start.40 = (bf16[8,4096]{1,0:T(8,128)(2,1)}, bf16[8,4096]{1,0:T(8,128)(2,1)S(1)}, u32[]{:S(2)}, u32[]{:S(2)}) collective-permute-start(bf16[8,4096]{1,0:T(8,128)(2,1)} %refs_0_.1), channel_id=1, source_target_pairs={{0,12},{2,14},{4,0},{6,2},{8,4},{10,6},{12,8},{14,10},{1,13},{3,15... | collective-permute-start | bytes 196616 | tf_op jit(solution)/shard_map/ppermute | solution.py:84
  10.6 4.9 %collective-permute-start.38 = (bf16[8,4096]{1,0:T(8,128)(2,1)S(1)}, bf16[8,4096]{1,0:T(8,128)(2,1)S(1)}, u32[]{:S(2)}, u32[]{:S(2)}) collective-permute-start(bf16[8,4096]{1,0:T(8,128)(2,1)S(1)} %collective-permute-done.37.refs_3_), channel_id=1, source_target_pairs={{0,2},{2,0},{4,6},{6,4},{8,10},{10,8},{12,14},{14,12},{1,3},{3,1},... | collective-permute-start | bytes 196616 | tf_op jit(solution)/shard_map/ppermute | solution.py:88
  12.5 9.1 %collective-permute-start.42 = (bf16[8,4096]{1,0:T(8,128)(2,1)S(1)}, bf16[8,4096]{1,0:T(8,128)(2,1)S(1)}, u32[]{:S(2)}, u32[]{:S(2)}) collective-permute-start(bf16[8,4096]{1,0:T(8,128)(2,1)S(1)} %collective-permute-done.39.refs_4_), channel_id=1, source_target_pairs={{0,2},{2,0},{4,6},{6,4},{8,10},{10,8},{12,14},{14,12},{1,3},{3,1},... | collective-permute-start | bytes 196616 | tf_op jit(solution)/shard_map/ppermute | solution.py:88
  12.6 9.0 %collective-permute-start.43 = (bf16[8,4096]{1,0:T(8,128)(2,1)S(1)}, bf16[8,4096]{1,0:T(8,128)(2,1)S(1)}, u32[]{:S(2)}, u32[]{:S(2)}) collective-permute-start(bf16[8,4096]{1,0:T(8,128)(2,1)S(1)} %collective-permute-done.40.refs_5_), channel_id=1, source_target_pairs={{0,2},{2,0},{4,6},{6,4},{8,10},{10,8},{12,14},{14,12},{1,3},{3,1},... | collective-permute-start | bytes 196616 | tf_op jit(solution)/shard_map/ppermute | solution.py:88
  27.9 8.8 %collective-permute-start.18 = (bf16[128,1024]{1,0:T(8,128)(2,1)S(1)}, bf16[128,1024]{1,0:T(8,128)(2,1)S(1)}, u32[]{:S(2)}, u32[]{:S(2)}) collective-permute-start(bf16[128,1024]{1,0:T(8,128)(2,1)S(1)} %get-tuple-element.179), channel_id=1, source_target_pairs={{0,2},{2,0},{4,6},{6,4},{8,10},{10,8},{12,14},{14,12},{1,3},{3,1},... | collective-permute-start | bytes 786440 | tf_op jit(solution)/shard_map/cond/branch_1_fun/ppermute | solution.py:483
  36.7 14.0 %collective-permute-start.19 = (bf16[64,4096]{1,0:T(8,128)(2,1)S(1)}, bf16[64,4096]{1,0:T(8,128)(2,1)S(1)}, u32[]{:S(2)}, u32[]{:S(2)}) collective-permute-start(bf16[64,4096]{1,0:T(8,128)(2,1)S(1)} %bitcast.19), channel_id=1, source_target_pairs={{0,2},{2,0},{4,6},{6,4},{8,10},{10,8},{12,14},{14,12},{1,3},{3,1},... | collective-permute-start | bytes 1572872 | tf_op jit(solution)/shard_map/cond/branch_1_fun/ppermute | solution.py:489
  38.0 13.5 %collective-permute-start.20 = (bf16[2,64,1024]{2,1,0:T(8,128)(2,1)S(1)}, bf16[2,64,1024]{2,1,0:T(8,128)(2,1)S(1)}, u32[]{:S(2)}, u32[]{:S(2)}) collective-permute-start(bf16[2,64,1024]{2,1,0:T(8,128)(2,1)S(1)} %branch_1_fun.10), channel_id=1, source_target_pairs={{0,1},{1,0},{2,3},{3,2},{4,5},{5,4},{6,7},{7,6},{8,9},{9,8},{10,11... | collective-permute-start | bytes 786440 | tf_op jit(solution)/shard_map/cond/branch_1_fun/ppermute | solution.py:418
  38.0 12.7 %collective-permute-start.21 = (bf16[64,1024]{1,0:T(8,128)(2,1)S(1)}, bf16[64,1024]{1,0:T(8,128)(2,1)S(1)}, u32[]{:S(2)}, u32[]{:S(2)}) collective-permute-start(bf16[64,1024]{1,0:T(8,128)(2,1)S(1)} %get-tuple-element.192), channel_id=1, source_target_pairs={{0,4},{2,6},{4,8},{6,10},{8,12},{10,14},{12,0},{14,2},{1,5},{3,7},... | collective-permute-start | bytes 393224 | tf_op jit(solution)/shard_map/cond/branch_1_fun/ppermute | solution.py:97
  39.2 12.3 %collective-permute-start.22 = (bf16[64,1024]{1,0:T(8,128)(2,1)S(1)}, bf16[64,1024]{1,0:T(8,128)(2,1)S(1)}, u32[]{:S(2)}, u32[]{:S(2)}) collective-permute-start(bf16[64,1024]{1,0:T(8,128)(2,1)S(1)} %get-tuple-element.193), channel_id=1, source_target_pairs={{0,8},{2,10},{4,12},{6,14},{8,0},{10,2},{12,4},{14,6},{1,9},{3,11}... | collective-permute-start | bytes 393224 | tf_op jit(solution)/shard_map/cond/branch_1_fun/ppermute | solution.py:97
  41.6 9.8 %collective-permute-start.23 = (bf16[64,1024]{1,0:T(8,128)(2,1)S(1)}, bf16[64,1024]{1,0:T(8,128)(2,1)S(1)}, u32[]{:S(2)}, u32[]{:S(2)}) collective-permute-start(bf16[64,1024]{1,0:T(8,128)(2,1)S(1)} %get-tuple-element.194), channel_id=1, source_target_pairs={{0,12},{2,14},{4,0},{6,2},{8,4},{10,6},{12,8},{14,10},{1,13},{3,15... | collective-permute-start | bytes 393224 | tf_op jit(solution)/shard_map/cond/branch_1_fun/ppermute | solution.py:97
  52.1 7.9 %collective-permute-start.25 = (bf16[64,1024]{1,0:T(8,128)(2,1)S(1)}, bf16[64,1024]{1,0:T(8,128)(2,1)S(1)}, u32[]{:S(2)}, u32[]{:S(2)}) collective-permute-start(bf16[64,1024]{1,0:T(8,128)(2,1)S(1)} %get-tuple-element.199), channel_id=1, source_target_pairs={{0,2},{2,0},{4,6},{6,4},{8,10},{10,8},{12,14},{14,12},{1,3},{3,1},... | collective-permute-start | bytes 393224 | tf_op jit(solution)/shard_map/cond/branch_1_fun/ppermute | solution.py:505
  60.0 11.8 %collective-permute-start.26 = (bf16[32,4096]{1,0:T(8,128)(2,1)S(1)}, bf16[32,4096]{1,0:T(8,128)(2,1)S(1)}, u32[]{:S(2)}, u32[]{:S(2)}) collective-permute-start(bf16[32,4096]{1,0:T(8,128)(2,1)S(1)} %get-tuple-element.200), channel_id=1, source_target_pairs={{0,2},{2,0},{4,6},{6,4},{8,10},{10,8},{12,14},{14,12},{1,3},{3,1},... | collective-permute-start | bytes 786440 | tf_op jit(solution)/shard_map/cond/branch_1_fun/ppermute | solution.py:508
  60.9 8.4 %collective-permute-start.27 = (bf16[32,1024]{1,0:T(8,128)(2,1)S(1)}, bf16[32,1024]{1,0:T(8,128)(2,1)S(1)}, u32[]{:S(2)}, u32[]{:S(2)}) collective-permute-start(bf16[32,1024]{1,0:T(8,128)(2,1)S(1)} %get-tuple-element.204), channel_id=1, source_target_pairs={{0,4},{2,6},{4,8},{6,10},{8,12},{10,14},{12,0},{14,2},{1,5},{3,7},... | collective-permute-start | bytes 196616 | tf_op jit(solution)/shard_map/cond/branch_1_fun/ppermute | solution.py:97
  64.2 7.1 %collective-permute-start.28 = (bf16[32,1024]{1,0:T(8,128)(2,1)S(1)}, bf16[32,1024]{1,0:T(8,128)(2,1)S(1)}, u32[]{:S(2)}, u32[]{:S(2)}) collective-permute-start(bf16[32,1024]{1,0:T(8,128)(2,1)S(1)} %get-tuple-element.205), channel_id=1, source_target_pairs={{0,8},{2,10},{4,12},{6,14},{8,0},{10,2},{12,4},{14,6},{1,9},{3,11}... | collective-permute-start | bytes 196616 | tf_op jit(solution)/shard_map/cond/branch_1_fun/ppermute | solution.py:97
  66.8 5.0 %collective-permute-start.29 = (bf16[32,1024]{1,0:T(8,128)(2,1)S(1)}, bf16[32,1024]{1,0:T(8,128)(2,1)S(1)}, u32[]{:S(2)}, u32[]{:S(2)}) collective-permute-start(bf16[32,1024]{1,0:T(8,128)(2,1)S(1)} %get-tuple-element.206), channel_id=1, source_target_pairs={{0,12},{2,14},{4,0},{6,2},{8,4},{10,6},{12,8},{14,10},{1,13},{3,15... | collective-permute-start | bytes 196616 | tf_op jit(solution)/shard_map/cond/branch_1_fun/ppermute | solution.py:97
  72.7 3.1 %collective-permute-start.32 = (f32[16,64]{1,0:T(8,128)S(1)}, f32[16,64]{1,0:T(8,128)S(1)}, u32[]{:S(2)}, u32[]{:S(2)}) collective-permute-start(f32[16,64]{1,0:T(8,128)S(1)} %branch_1_fun.16.refs_2_), channel_id=1, source_target_pairs={{0,3},{1,2},{2,1},{3,0},{4,7},{5,6},{6,5},{7,4},{8,11},{9,10},{10,... | collective-permute-start | bytes 12296 | tf_op jit(solution)/shard_map/cond/branch_1_fun/ppermute | solution.py:525
  73.0 3.7 %collective-permute-start.31 = (f32[16,64]{1,0:T(8,128)S(1)}, f32[16,64]{1,0:T(8,128)S(1)}, u32[]{:S(2)}, u32[]{:S(2)}) collective-permute-start(f32[16,64]{1,0:T(8,128)S(1)} %branch_1_fun.16.refs_2_), channel_id=1, source_target_pairs={{0,2},{2,0},{4,6},{6,4},{8,10},{10,8},{12,14},{14,12},{1,3},{3,1},... | collective-permute-start | bytes 12296 | tf_op jit(solution)/shard_map/cond/branch_1_fun/ppermute | solution.py:521
  77.2 6.9 %collective-permute-start.33 = (bf16[8,4096]{1,0:T(8,128)(2,1)S(1)}, bf16[8,4096]{1,0:T(8,128)(2,1)S(1)}, u32[]{:S(2)}, u32[]{:S(2)}) collective-permute-start(bf16[8,4096]{1,0:T(8,128)(2,1)S(1)} %get-tuple-element.221), channel_id=1, source_target_pairs={{0,4},{2,6},{4,8},{6,10},{8,12},{10,14},{12,0},{14,2},{1,5},{3,7},... | collective-permute-start | bytes 196616 | tf_op jit(solution)/shard_map/cond/branch_1_fun/ppermute | solution.py:97
  79.2 6.8 %collective-permute-start.34 = (bf16[8,4096]{1,0:T(8,128)(2,1)S(1)}, bf16[8,4096]{1,0:T(8,128)(2,1)S(1)}, u32[]{:S(2)}, u32[]{:S(2)}) collective-permute-start(bf16[8,4096]{1,0:T(8,128)(2,1)S(1)} %get-tuple-element.222), channel_id=1, source_target_pairs={{0,8},{2,10},{4,12},{6,14},{8,0},{10,2},{12,4},{14,6},{1,9},{3,11}... | collective-permute-start | bytes 196616 | tf_op jit(solution)/shard_map/cond/branch_1_fun/ppermute | solution.py:97
  80.1 6.0 %collective-permute-start.35 = (bf16[8,4096]{1,0:T(8,128)(2,1)S(1)}, bf16[8,4096]{1,0:T(8,128)(2,1)S(1)}, u32[]{:S(2)}, u32[]{:S(2)}) collective-permute-start(bf16[8,4096]{1,0:T(8,128)(2,1)S(1)} %get-tuple-element.223), channel_id=1, source_target_pairs={{0,12},{2,14},{4,0},{6,2},{8,4},{10,6},{12,8},{14,10},{1,13},{3,15... | collective-permute-start | bytes 196616 | tf_op jit(solution)/shard_map/cond/branch_1_fun/ppermute | solution.py:97
  (6 other events, 21.1 us)

commit v2 on v1

--- a/solution.py
+++ b/solution.py
@@ -152,17 +152,33 @@
 
 
 def expand_kernel(
-    cap, fast, at_ref, own_ref, got_ref, marks_ref, cols_ref, near_ref, far_ref, *out_refs
+    cap,
+    fast,
+    at_ref,
+    own_ref,
+    got_ref,
+    marks_ref,
+    cols_ref,
+    far_ref,
+    near_ref,
+    *refs,
 ):
+    out_refs, held, sems = refs[:-2], refs[-2], refs[-1]
+    half = out_refs[0].shape[1]
+    count = at_ref.shape[0]
+    columns = [pl.ds(pl.multiple_of(at_ref[b] * half, half), half) for b in range(count)]
+    copies = []
+    for b in range(count):
+        put = held.at[:, pl.ds(b * half, half)]
+        copies.append(pltpu.make_async_copy(near_ref.at[:, columns[b]], put, sems.at[b]))
+        copies[b].start()
     low = (own_ref[...] + got_ref[...]).astype(BF)
     picked = dot(one_hot(cap, marks_ref[MINE : MINE + 1]), low).astype(BF)
     lhs = jnp.concatenate([dot(picked, cols_ref[kind]) for kind in range(2)], axis=0).astype(BF)
     tall = lhs.shape[0]
-    half = out_refs[0].shape[1]
-    count = at_ref.shape[0]
     for b in range(count):
-        here = pl.ds(pl.multiple_of(at_ref[b] * half, half), half)
-        both = jnp.concatenate([near_ref[:, here], far_ref[:, here]], axis=0)
+        copies[b].wait()
+        both = jnp.concatenate([held[:, pl.ds(b * half, half)], far_ref[:, columns[b]]], axis=0)
         at = b % (count // fast)
         out_refs[b * fast // count][pl.ds(at * tall, tall)] = dot(lhs, both).astype(BF)
 
@@ -175,10 +191,14 @@
     return pl.pallas_call(
         functools.partial(expand_kernel, cap, fast),
         out_shape=(out,) * fast,
-        in_specs=[SCALARS] + [WHOLE] * 6,
-        compiler_params=params(16),
+        in_specs=[SCALARS] + [WHOLE] * 5 + [FAR],
+        scratch_shapes=[
+            pltpu.VMEM((depth, width // 2), BF),
+            pltpu.SemaphoreType.DMA((shards,)),
+        ],
+        compiler_params=params(52),
         cost_estimate=cost(8 * cap * depth * width, 4 * (depth + cap) * width),
-    )(at, own, got, marks, cols, near, far)
+    )(at, own, got, marks, cols, far, near)
 
 
 def base_kernel(side_ref, x_ref, gate_ref, up_ref, out_ref, held, sums, sems):
@@ -422,8 +442,8 @@
     shrink_in = shrink_gu.reshape(slots * 2 * rank, width)
     if ways.direct:
         first_hop = ways.slow + 1
-        variant_ids, variant_slot, near, shrink_in, token_parts[first_hop] = tied(
-            variant_ids, variant_slot, near, shrink_in, token_parts[first_hop]
+        variant_ids, variant_slot, shrink_in, token_parts[first_hop] = tied(
+            variant_ids, variant_slot, shrink_in, token_parts[first_hop]
         )
     all_ids, all_slots = [variant_ids[:, 0]], [variant_slot]
     for turn in range(1, 1 if ways.direct else groups):
@@ -431,7 +451,7 @@
         all_ids.append(lax.ppermute(all_ids[0], "groups", pairs))
         all_slots.append(lax.ppermute(all_slots[0], "groups", pairs))
     all_ids, all_slots = jnp.stack(all_ids), jnp.stack(all_slots)
-    token_parts[0], near, shrink_in = stage(token_parts[0], near, shrink_in)
+    token_parts[0], shrink_in = stage(token_parts[0], shrink_in)
 
     matches = all_ids[:, :, None] == jnp.arange(variants, dtype=I32)
     slot_row = jnp.sum(jnp.where(matches, all_slots[:, None, :], 0), axis=2)
@@ -500,19 +520,25 @@
         )
         hidden_far = swap(hidden)
         shrink = shrink_down.reshape(slots * rank, -1)
-        down = functools.partial(down_base, here, hidden, hidden_far, down_weight, 0, width)
+        side = width // 2
+        down = functools.partial(down_base, here, hidden, hidden_far, down_weight)
         if split == 2:
             beside = lax.ppermute(sent[1], "ff", ways.back(0, 1))
-            base, base_sent = down((F32, BF))
-            base_sent, beside = tied(base_sent, beside)
-            base_beside = lax.ppermute(base_sent, "ff", ways.back(0, 1))
-            got = ways.slow_steps(relay(sent[0], beside, ways.slow))
-            base_beside, *got = tied(base_beside, *got)
-            bases = [base, base_beside]
+            left, left_sent = down(0, side, (F32, BF))
+            left_sent, beside = tied(left_sent, beside)
+            left_beside = lax.ppermute(left_sent, "ff", ways.back(0, 1))
+            sent = relay(sent[0], beside, ways.slow)
+            hidden, *sent = tied(hidden, *sent)
+            down = functools.partial(down_base, here, hidden, hidden_far, down_weight)
+            got = ways.slow_steps(sent)
+            right, right_sent = down(side, side, (F32, BF))
+            right_sent, left_beside, *got = tied(right_sent, left_beside, *got)
+            right_beside = lax.ppermute(right_sent, "ff", ways.back(0, 1))
+            bases = [left, right, left_beside, right_beside]
         else:
-            bases = list(down((F32,)))
+            bases = [down(0, side, (F32,))[0], down(side, side, (F32,))[0]]
             got = [ways.spread(sent[0].reshape(shards, cap, half)).reshape(shards * cap, half)]
-        bases[0], *got = tied(bases[0], *got)
+        bases[1], *got = tied(bases[1], *got)
         out_own = low_out_pairs(at_here, marks, slot_mask, shrink, got, cap)
         out_got = swap(out_own)
         if split == 1:

time: 87.2 us -> 83.5 us (0.958)
  waiting for transfers between devices: 15 us -> 11.2 us
    ppermute x9, waiting for transfers between devices: 10.1 us -> 6.04 us  [slow_steps(): got[-a % self.slow] = lax.ppermute(blocks[a], 'ff', self.back(a, 0))]
    pallas_call x1, Pallas kernels: 3.42 us -> 1.29 us  [stage(): pl.pallas_call(stage_kernel, out_shape=tuple((jax.ShapeDtypeStruct(array....]
    pallas_call x1 -> x2, Pallas kernels: 6.54 us -> 8.17 us  [down_base(): pl.pallas_call(functools.partial(down_kernel, start), out_shape=outs, in_...]
    ppermute x1 -> x2, starting transfers between devices: 0.83 us -> 2.08 us  [the longest x1 1.36 us: partial_sums(): right_beside = lax.ppermute(right_sent, 'ff', ways.back(0, 1))]
  transfers between devices with their start and end apart: 27 -> 28, of which waited for: 12 -> 12; matrix products, arithmetic and copies ran while one was open for 5% -> 5% of each run, Pallas kernels for 26% -> 28%
where the time goes in v2:
time: 83.5 us; the launch traced here: 83.2 us
  starting transfers between devices  37 us (44%)
  Pallas kernels  28 us (34%)
  waiting for transfers between devices  11.2 us (13%)
  other arithmetic  3.71 us (4%)
  local copies, waits for them, and re-layouts  1.91 us (2%)
    ppermute x9, starting transfers between devices, slow_steps(): got[-a % self.slow] = lax.ppermute(blocks[a], 'ff', self.back(a, 0))  16.2 us
    pallas_call x2, Pallas kernels, base_half(): pl.pallas_call(base_kernel, out_shape=jax.ShapeDtypeStruct((2, rows, half...  12.5 us
    pallas_call x2, Pallas kernels, down_base(): pl.pallas_call(functools.partial(down_kernel, start), out_shape=outs, in_...  8.17 us
    ppermute x3, starting transfers between devices, gather(): lax.ppermute(block, 'ff', self.back(-a, 0))  7.41 us
    ppermute x9, waiting for transfers between devices, slow_steps(): got[-a % self.slow] = lax.ppermute(blocks[a], 'ff', self.back(a, 0))  6.04 us
    ppermute x4, starting transfers between devices, gather(): lax.ppermute(part, 'ff', self.back(0, -c))  5.5 us
    pallas_call x1, Pallas kernels, expand_rows(): pl.pallas_call(functools.partial(expand_kernel, cap, fast), out_shape=(ou...  2.87 us
    ppermute x5, starting transfers between devices, per_device(): swap = lambda a: lax.ppermute(a, 'var', [(0, 1), (1, 0)])  1.73 us
  transfers between devices with their start and end apart: 28, of which 12 were waited for; matrix products, arithmetic and copies ran while one was open for 5% of the time, Pallas kernels for 28%

profile of v2, /device:TPU:0, one launch (start us, length us, event | category | flops | bytes accessed | tf_op | source)
XLA Modules:
  0.0 83.2 jit_solution(1688390837463318539)
XLA Ops:
  0.5 3.6 %collective-permute-start.41 = (bf16[8,4096]{1,0:T(8,128)(2,1)}, bf16[8,4096]{1,0:T(8,128)(2,1)S(1)}, u32[]{:S(2)}, u32[]{:S(2)}) collective-permute-start(bf16[8,4096]{1,0:T(8,128)(2,1)} %refs_0_.1), channel_id=1, source_target_pairs={{0,8},{2,10},{4,12},{6,14},{8,0},{10,2},{12,4},{14,6},{1,9},{3,11}... | collective-permute-start | bytes 196616 | tf_op jit(solution)/shard_map/ppermute | solution.py:84
  4.0 1.6 %collective-permute-start.39 = (bf16[8,4096]{1,0:T(8,128)(2,1)}, bf16[8,4096]{1,0:T(8,128)(2,1)S(1)}, u32[]{:S(2)}, u32[]{:S(2)}) collective-permute-start(bf16[8,4096]{1,0:T(8,128)(2,1)} %refs_0_.1), channel_id=1, source_target_pairs={{0,4},{2,6},{4,8},{6,10},{8,12},{10,14},{12,0},{14,2},{1,5},{3,7},... | collective-permute-start | bytes 196616 | tf_op jit(solution)/shard_map/ppermute | solution.py:84
  5.6 1.5 %collective-permute-start.43 = (bf16[8,4096]{1,0:T(8,128)(2,1)}, bf16[8,4096]{1,0:T(8,128)(2,1)S(1)}, u32[]{:S(2)}, u32[]{:S(2)}) collective-permute-start(bf16[8,4096]{1,0:T(8,128)(2,1)} %refs_0_.1), channel_id=1, source_target_pairs={{0,2},{2,0},{4,6},{6,4},{8,10},{10,8},{12,14},{14,12},{1,3},{3,1},... | collective-permute-start | bytes 196616 | tf_op jit(solution)/shard_map/ppermute | solution.py:88
  7.1 2.2 %collective-permute-start.42 = (bf16[8,4096]{1,0:T(8,128)(2,1)}, bf16[8,4096]{1,0:T(8,128)(2,1)S(1)}, u32[]{:S(2)}, u32[]{:S(2)}) collective-permute-start(bf16[8,4096]{1,0:T(8,128)(2,1)} %refs_0_.1), channel_id=1, source_target_pairs={{0,12},{2,14},{4,0},{6,2},{8,4},{10,6},{12,8},{14,10},{1,13},{3,15... | collective-permute-start | bytes 196616 | tf_op jit(solution)/shard_map/ppermute | solution.py:84
  10.6 2.0 %collective-permute-start.40 = (bf16[8,4096]{1,0:T(8,128)(2,1)S(1)}, bf16[8,4096]{1,0:T(8,128)(2,1)S(1)}, u32[]{:S(2)}, u32[]{:S(2)}) collective-permute-start(bf16[8,4096]{1,0:T(8,128)(2,1)S(1)} %collective-permute-done.39.refs_3_), channel_id=1, source_target_pairs={{0,2},{2,0},{4,6},{6,4},{8,10},{10,8},{12,14},{14,12},{1,3},{3,1},... | collective-permute-start | bytes 196616 | tf_op jit(solution)/shard_map/ppermute | solution.py:88
  12.6 1.9 %collective-permute-start.45 = (bf16[8,4096]{1,0:T(8,128)(2,1)S(1)}, bf16[8,4096]{1,0:T(8,128)(2,1)S(1)}, u32[]{:S(2)}, u32[]{:S(2)}) collective-permute-start(bf16[8,4096]{1,0:T(8,128)(2,1)S(1)} %collective-permute-done.42.refs_5_), channel_id=1, source_target_pairs={{0,2},{2,0},{4,6},{6,4},{8,10},{10,8},{12,14},{14,12},{1,3},{3,1},... | collective-permute-start | bytes 196616 | tf_op jit(solution)/shard_map/ppermute | solution.py:88
  18.1 1.3 %shard_map.100 = (bf16[8,4096]{1,0:T(8,128)(2,1)S(1)}, bf16[128,4096]{1,0:T(8,128)(2,1)S(1)}) custom-call(bf16[8,4096]{1,0:T(8,128)(2,1)S(1)} %copy-done, bf16[128,4096]{1,0:T(8,128)(2,1)} %bitcast.24), custom_call_target="tpu_custom_call" | custom-call | bytes 2228224 | tf_op jit(solution)/shard_map/pallas_call | solution.py:112
  22.7 59.9 %conditional.3 = (bf16[8,4096]{1,0:T(8,128)(2,1)S(1)}, f32[8,4096]{1,0:T(8,128)S(1)}, f32[8,4096]{1,0:T(8,128)S(1)}, f32[8,4096]{1,0:T(8,128)S(1)}) conditional(s32[]{:T(128)} %convert_element_type.60, (s32[]{:T(128)}, s32[8]{0:T(128)S(1)}, s32[8]{0:T(128)S(1)}, f32[64,128]{1,0:T(8,128)S(1)}, f32[64,128]{1,0:T(8,128)S(1)}, ...), branch_computations={%region_7.8_spmd, %region_8.9_spmd} | conditional | flops 3724640256 | bytes 92963768
  22.9 2.9 %branch_1_fun.10 = (bf16[128,1024]{1,0:T(8,128)(2,1)S(1)}, bf16[128,1024]{1,0:T(8,128)(2,1)S(1)}) custom-call(s32[8]{0:T(128)S(1)} %multiply_add_fusion.1.at_ref, f32[64,128]{1,0:T(8,128)S(1)} %get-tuple-element.175.own_ref, f32[64,128]{1,0:T(8,128)S(1)} %get-tuple-element.176.got_ref, s32[4,64]{1,0:T(4,128)S(1)} %get-tuple-element.177.marks_ref.refs_8_, ...), custom_call_target="tpu_custom_call" | custom-call | flops 134217728 | bytes 5242880 | tf_op jit(solution)/shard_map/cond/branch_1_fun/pallas_call | solution.py:191
  25.8 1.4 %collective-permute-start.19 = (bf16[128,1024]{1,0:T(8,128)(2,1)S(1)}, bf16[128,1024]{1,0:T(8,128)(2,1)S(1)}, u32[]{:S(2)}, u32[]{:S(2)}) collective-permute-start(bf16[128,1024]{1,0:T(8,128)(2,1)S(1)} %get-tuple-element.187), channel_id=1, source_target_pairs={{0,2},{2,0},{4,6},{6,4},{8,10},{10,8},{12,14},{14,12},{1,3},{3,1},... | collective-permute-start | bytes 786440 | tf_op jit(solution)/shard_map/cond/branch_1_fun/ppermute | solution.py:503
  27.1 6.3 %branch_1_fun.11 = bf16[2,64,1024]{2,1,0:T(8,128)(2,1)S(1)} custom-call(s32[1]{0:T(128)S(6)} %sub.75.side_ref, bf16[64,4096]{1,0:T(8,128)(2,1)S(1)} %get-tuple-element.194.x_ref, bf16[4096,2048]{1,0:T(8,128)(2,1)} %get-tuple-element.185.gate_ref, bf16[4096,2048]{1,0:T(8,128)(2,1)} %get-tuple-element.186.up_ref), custom_call_target="tpu_custom_call" | custom-call | flops 1073741824 | bytes 17301504 | tf_op jit(solution)/shard_map/cond/branch_1_fun/pallas_call | solution.py:228
  34.6 1.3 %collective-permute-start.20 = (bf16[64,4096]{1,0:T(8,128)(2,1)S(1)}, bf16[64,4096]{1,0:T(8,128)(2,1)S(1)}, u32[]{:S(2)}, u32[]{:S(2)}) collective-permute-start(bf16[64,4096]{1,0:T(8,128)(2,1)S(1)} %bitcast.22), channel_id=1, source_target_pairs={{0,2},{2,0},{4,6},{6,4},{8,10},{10,8},{12,14},{14,12},{1,3},{3,1},... | collective-permute-start | bytes 1572872 | tf_op jit(solution)/shard_map/cond/branch_1_fun/ppermute | solution.py:509
  37.1 2.4 %collective-permute-start.23 = (bf16[64,1024]{1,0:T(8,128)(2,1)S(1)}, bf16[64,1024]{1,0:T(8,128)(2,1)S(1)}, u32[]{:S(2)}, u32[]{:S(2)}) collective-permute-start(bf16[64,1024]{1,0:T(8,128)(2,1)S(1)} %get-tuple-element.201), channel_id=1, source_target_pairs={{0,8},{2,10},{4,12},{6,14},{8,0},{10,2},{12,4},{14,6},{1,9},{3,11}... | collective-permute-start | bytes 393224 | tf_op jit(solution)/shard_map/cond/branch_1_fun/ppermute | solution.py:97
  39.5 2.8 %collective-permute-start.24 = (bf16[64,1024]{1,0:T(8,128)(2,1)S(1)}, bf16[64,1024]{1,0:T(8,128)(2,1)S(1)}, u32[]{:S(2)}, u32[]{:S(2)}) collective-permute-start(bf16[64,1024]{1,0:T(8,128)(2,1)S(1)} %get-tuple-element.202), channel_id=1, source_target_pairs={{0,12},{2,14},{4,0},{6,2},{8,4},{10,6},{12,8},{14,10},{1,13},{3,15... | collective-permute-start | bytes 393224 | tf_op jit(solution)/shard_map/cond/branch_1_fun/ppermute | solution.py:97
  42.3 6.2 %branch_1_fun.13.own_ref = f32[2,64,1024]{2,1,0:T(8,128)S(1)} custom-call(s32[1]{0:T(128)} %bitcast.3.side_ref.core_ref, bf16[64,4096]{1,0:T(8,128)(2,1)S(1)} %get-tuple-element.194.x_ref, bf16[4096,2048]{1,0:T(8,128)(2,1)} %get-tuple-element.185.gate_ref, bf16[4096,2048]{1,0:T(8,128)(2,1)} %get-tuple-element.186.up_ref), custom_call_target="tpu_custom_call" | custom-call | flops 1073741824 | bytes 17301504 | tf_op jit(solution)/shard_map/cond/branch_1_fun/pallas_call | solution.py:228
  51.4 4.2 %branch_1_fun.15 = (f32[32,2048]{1,0:T(8,128)S(1)}, bf16[32,2048]{1,0:T(8,128)(2,1)S(1)}) custom-call(s32[1]{0:T(128)} %bitcast.3.side_ref.core_ref, bf16[64,1024]{1,0:T(8,128)(2,1)S(1)} %get-tuple-element.214.near_ref, bf16[64,1024]{1,0:T(8,128)(2,1)S(1)} %collective-permute-done.25.far_ref, bf16[2048,4096]{1,0:T(8,128)(2,1)} %get-tuple-element.204.weight_ref), custom_call_target="tpu_custom_call" | custom-call | flops 536870912 | bytes 8912896 | tf_op jit(solution)/shard_map/cond/branch_1_fun/pallas_call | solution.py:325
  56.7 3.1 %collective-permute-start.28 = (bf16[32,1024]{1,0:T(8,128)(2,1)S(1)}, bf16[32,1024]{1,0:T(8,128)(2,1)S(1)}, u32[]{:S(2)}, u32[]{:S(2)}) collective-permute-start(bf16[32,1024]{1,0:T(8,128)(2,1)S(1)} %get-tuple-element.219), channel_id=1, source_target_pairs={{0,4},{2,6},{4,8},{6,10},{8,12},{10,14},{12,0},{14,2},{1,5},{3,7},... | collective-permute-start | bytes 196616 | tf_op jit(solution)/shard_map/cond/branch_1_fun/ppermute | solution.py:97
  59.7 2.6 %collective-permute-start.29 = (bf16[32,1024]{1,0:T(8,128)(2,1)S(1)}, bf16[32,1024]{1,0:T(8,128)(2,1)S(1)}, u32[]{:S(2)}, u32[]{:S(2)}) collective-permute-start(bf16[32,1024]{1,0:T(8,128)(2,1)S(1)} %get-tuple-element.220), channel_id=1, source_target_pairs={{0,8},{2,10},{4,12},{6,14},{8,0},{10,2},{12,4},{14,6},{1,9},{3,11}... | collective-permute-start | bytes 196616 | tf_op jit(solution)/shard_map/cond/branch_1_fun/ppermute | solution.py:97
  62.5 4.0 %branch_1_fun.17 = (f32[32,2048]{1,0:T(8,128)S(1)}, bf16[32,2048]{1,0:T(8,128)(2,1)S(1)}) custom-call(s32[1]{0:T(128)} %bitcast.3.side_ref.core_ref, bf16[64,1024]{1,0:T(8,128)(2,1)S(1)} %get-tuple-element.214.near_ref, bf16[64,1024]{1,0:T(8,128)(2,1)S(1)} %collective-permute-done.25.far_ref, bf16[2048,4096]{1,0:T(8,128)(2,1)} %get-tuple-element.204.weight_ref), custom_call_target="tpu_custom_call" | custom-call | flops 536870912 | bytes 8912896 | tf_op jit(solution)/shard_map/cond/branch_1_fun/pallas_call | solution.py:325
  67.3 1.4 %collective-permute-start.31 = (bf16[32,2048]{1,0:T(8,128)(2,1)S(1)}, bf16[32,2048]{1,0:T(8,128)(2,1)S(1)}, u32[]{:S(2)}, u32[]{:S(2)}) collective-permute-start(bf16[32,2048]{1,0:T(8,128)(2,1)S(1)} %get-tuple-element.228), channel_id=1, source_target_pairs={{0,2},{2,0},{4,6},{6,4},{8,10},{10,8},{12,14},{14,12},{1,3},{3,1},... | collective-permute-start | bytes 393224 | tf_op jit(solution)/shard_map/cond/branch_1_fun/ppermute | solution.py:536
  73.8 1.5 %collective-permute-start.35 = (bf16[8,4096]{1,0:T(8,128)(2,1)S(1)}, bf16[8,4096]{1,0:T(8,128)(2,1)S(1)}, u32[]{:S(2)}, u32[]{:S(2)}) collective-permute-start(bf16[8,4096]{1,0:T(8,128)(2,1)S(1)} %get-tuple-element.237), channel_id=1, source_target_pairs={{0,4},{2,6},{4,8},{6,10},{8,12},{10,14},{12,0},{14,2},{1,5},{3,7},... | collective-permute-start | bytes 196616 | tf_op jit(solution)/shard_map/cond/branch_1_fun/ppermute | solution.py:97
  75.3 1.6 %collective-permute-start.36 = (bf16[8,4096]{1,0:T(8,128)(2,1)S(1)}, bf16[8,4096]{1,0:T(8,128)(2,1)S(1)}, u32[]{:S(2)}, u32[]{:S(2)}) collective-permute-start(bf16[8,4096]{1,0:T(8,128)(2,1)S(1)} %get-tuple-element.238), channel_id=1, source_target_pairs={{0,8},{2,10},{4,12},{6,14},{8,0},{10,2},{12,4},{14,6},{1,9},{3,11}... | collective-permute-start | bytes 196616 | tf_op jit(solution)/shard_map/cond/branch_1_fun/ppermute | solution.py:97
  77.7 2.9 %collective-permute-done.35 = bf16[8,4096]{1,0:T(8,128)(2,1)S(1)} collective-permute-done((bf16[8,4096]{1,0:T(8,128)(2,1)S(1)}, bf16[8,4096]{1,0:T(8,128)(2,1)S(1)}, u32[]{:S(2)}, u32[]{:S(2)}) %collective-permute-start.35) | collective-permute-done | bytes 65568 | tf_op jit(solution)/shard_map/cond/branch_1_fun/ppermute | solution.py:97
  80.6 1.7 %collective-permute-done.36 = bf16[8,4096]{1,0:T(8,128)(2,1)S(1)} collective-permute-done((bf16[8,4096]{1,0:T(8,128)(2,1)S(1)}, bf16[8,4096]{1,0:T(8,128)(2,1)S(1)}, u32[]{:S(2)}, u32[]{:S(2)}) %collective-permute-start.36) | collective-permute-done | bytes 65568 | tf_op jit(solution)/shard_map/cond/branch_1_fun/ppermute | solution.py:97
  (89 shorter events, 21.7 us)
Async XLA Ops:
  0.0 10.6 %collective-permute-start.38 = (bf16[64,16384]{1,0:T(8,128)(2,1)}, bf16[64,16384]{1,0:T(8,128)(2,1)S(1)}, u32[]{:S(2)}, u32[]{:S(2)}) collective-permute-start(bf16[64,16384]{1,0:T(8,128)(2,1)} %bitcast.15), channel_id=1, source_target_pairs={{0,1},{1,0},{2,3},{3,2},{4,5},{5,4},{6,7},{7,6},{8,9},{9,8},{10,11... | collective-permute-start | bytes 6291464 | tf_op jit(solution)/shard_map/ppermute | solution.py:438
  0.5 12.1 %collective-permute-start.41 = (bf16[8,4096]{1,0:T(8,128)(2,1)}, bf16[8,4096]{1,0:T(8,128)(2,1)S(1)}, u32[]{:S(2)}, u32[]{:S(2)}) collective-permute-start(bf16[8,4096]{1,0:T(8,128)(2,1)} %refs_0_.1), channel_id=1, source_target_pairs={{0,8},{2,10},{4,12},{6,14},{8,0},{10,2},{12,4},{14,6},{1,9},{3,11}... | collective-permute-start | bytes 196616 | tf_op jit(solution)/shard_map/ppermute | solution.py:84
  4.0 6.5 %collective-permute-start.39 = (bf16[8,4096]{1,0:T(8,128)(2,1)}, bf16[8,4096]{1,0:T(8,128)(2,1)S(1)}, u32[]{:S(2)}, u32[]{:S(2)}) collective-permute-start(bf16[8,4096]{1,0:T(8,128)(2,1)} %refs_0_.1), channel_id=1, source_target_pairs={{0,4},{2,6},{4,8},{6,10},{8,12},{10,14},{12,0},{14,2},{1,5},{3,7},... | collective-permute-start | bytes 196616 | tf_op jit(solution)/shard_map/ppermute | solution.py:84
  5.6 13.8 %collective-permute-start.43 = (bf16[8,4096]{1,0:T(8,128)(2,1)}, bf16[8,4096]{1,0:T(8,128)(2,1)S(1)}, u32[]{:S(2)}, u32[]{:S(2)}) collective-permute-start(bf16[8,4096]{1,0:T(8,128)(2,1)} %refs_0_.1), channel_id=1, source_target_pairs={{0,2},{2,0},{4,6},{6,4},{8,10},{10,8},{12,14},{14,12},{1,3},{3,1},... | collective-permute-start | bytes 196616 | tf_op jit(solution)/shard_map/ppermute | solution.py:88
  7.1 5.5 %collective-permute-start.42 = (bf16[8,4096]{1,0:T(8,128)(2,1)}, bf16[8,4096]{1,0:T(8,128)(2,1)S(1)}, u32[]{:S(2)}, u32[]{:S(2)}) collective-permute-start(bf16[8,4096]{1,0:T(8,128)(2,1)} %refs_0_.1), channel_id=1, source_target_pairs={{0,12},{2,14},{4,0},{6,2},{8,4},{10,6},{12,8},{14,10},{1,13},{3,15... | collective-permute-start | bytes 196616 | tf_op jit(solution)/shard_map/ppermute | solution.py:84
  10.6 4.9 %collective-permute-start.40 = (bf16[8,4096]{1,0:T(8,128)(2,1)S(1)}, bf16[8,4096]{1,0:T(8,128)(2,1)S(1)}, u32[]{:S(2)}, u32[]{:S(2)}) collective-permute-start(bf16[8,4096]{1,0:T(8,128)(2,1)S(1)} %collective-permute-done.39.refs_3_), channel_id=1, source_target_pairs={{0,2},{2,0},{4,6},{6,4},{8,10},{10,8},{12,14},{14,12},{1,3},{3,1},... | collective-permute-start | bytes 196616 | tf_op jit(solution)/shard_map/ppermute | solution.py:88
  12.5 6.9 %collective-permute-start.44 = (bf16[8,4096]{1,0:T(8,128)(2,1)S(1)}, bf16[8,4096]{1,0:T(8,128)(2,1)S(1)}, u32[]{:S(2)}, u32[]{:S(2)}) collective-permute-start(bf16[8,4096]{1,0:T(8,128)(2,1)S(1)} %collective-permute-done.41.refs_4_), channel_id=1, source_target_pairs={{0,2},{2,0},{4,6},{6,4},{8,10},{10,8},{12,14},{14,12},{1,3},{3,1},... | collective-permute-start | bytes 196616 | tf_op jit(solution)/shard_map/ppermute | solution.py:88
  12.6 6.9 %collective-permute-start.45 = (bf16[8,4096]{1,0:T(8,128)(2,1)S(1)}, bf16[8,4096]{1,0:T(8,128)(2,1)S(1)}, u32[]{:S(2)}, u32[]{:S(2)}) collective-permute-start(bf16[8,4096]{1,0:T(8,128)(2,1)S(1)} %collective-permute-done.42.refs_5_), channel_id=1, source_target_pairs={{0,2},{2,0},{4,6},{6,4},{8,10},{10,8},{12,14},{14,12},{1,3},{3,1},... | collective-permute-start | bytes 196616 | tf_op jit(solution)/shard_map/ppermute | solution.py:88
  25.8 8.8 %collective-permute-start.19 = (bf16[128,1024]{1,0:T(8,128)(2,1)S(1)}, bf16[128,1024]{1,0:T(8,128)(2,1)S(1)}, u32[]{:S(2)}, u32[]{:S(2)}) collective-permute-start(bf16[128,1024]{1,0:T(8,128)(2,1)S(1)} %get-tuple-element.187), channel_id=1, source_target_pairs={{0,2},{2,0},{4,6},{6,4},{8,10},{10,8},{12,14},{14,12},{1,3},{3,1},... | collective-permute-start | bytes 786440 | tf_op jit(solution)/shard_map/cond/branch_1_fun/ppermute | solution.py:503
  34.6 14.0 %collective-permute-start.20 = (bf16[64,4096]{1,0:T(8,128)(2,1)S(1)}, bf16[64,4096]{1,0:T(8,128)(2,1)S(1)}, u32[]{:S(2)}, u32[]{:S(2)}) collective-permute-start(bf16[64,4096]{1,0:T(8,128)(2,1)S(1)} %bitcast.22), channel_id=1, source_target_pairs={{0,2},{2,0},{4,6},{6,4},{8,10},{10,8},{12,14},{14,12},{1,3},{3,1},... | collective-permute-start | bytes 1572872 | tf_op jit(solution)/shard_map/cond/branch_1_fun/ppermute | solution.py:509
  35.8 13.5 %collective-permute-start.21 = (bf16[2,64,1024]{2,1,0:T(8,128)(2,1)S(1)}, bf16[2,64,1024]{2,1,0:T(8,128)(2,1)S(1)}, u32[]{:S(2)}, u32[]{:S(2)}) collective-permute-start(bf16[2,64,1024]{2,1,0:T(8,128)(2,1)S(1)} %branch_1_fun.11), channel_id=1, source_target_pairs={{0,1},{1,0},{2,3},{3,2},{4,5},{5,4},{6,7},{7,6},{8,9},{9,8},{10,11... | collective-permute-start | bytes 786440 | tf_op jit(solution)/shard_map/cond/branch_1_fun/ppermute | solution.py:438
  35.9 12.7 %collective-permute-start.22 = (bf16[64,1024]{1,0:T(8,128)(2,1)S(1)}, bf16[64,1024]{1,0:T(8,128)(2,1)S(1)}, u32[]{:S(2)}, u32[]{:S(2)}) collective-permute-start(bf16[64,1024]{1,0:T(8,128)(2,1)S(1)} %get-tuple-element.200), channel_id=1, source_target_pairs={{0,4},{2,6},{4,8},{6,10},{8,12},{10,14},{12,0},{14,2},{1,5},{3,7},... | collective-permute-start | bytes 393224 | tf_op jit(solution)/shard_map/cond/branch_1_fun/ppermute | solution.py:97
  37.1 12.3 %collective-permute-start.23 = (bf16[64,1024]{1,0:T(8,128)(2,1)S(1)}, bf16[64,1024]{1,0:T(8,128)(2,1)S(1)}, u32[]{:S(2)}, u32[]{:S(2)}) collective-permute-start(bf16[64,1024]{1,0:T(8,128)(2,1)S(1)} %get-tuple-element.201), channel_id=1, source_target_pairs={{0,8},{2,10},{4,12},{6,14},{8,0},{10,2},{12,4},{14,6},{1,9},{3,11}... | collective-permute-start | bytes 393224 | tf_op jit(solution)/shard_map/cond/branch_1_fun/ppermute | solution.py:97
  39.5 9.8 %collective-permute-start.24 = (bf16[64,1024]{1,0:T(8,128)(2,1)S(1)}, bf16[64,1024]{1,0:T(8,128)(2,1)S(1)}, u32[]{:S(2)}, u32[]{:S(2)}) collective-permute-start(bf16[64,1024]{1,0:T(8,128)(2,1)S(1)} %get-tuple-element.202), channel_id=1, source_target_pairs={{0,12},{2,14},{4,0},{6,2},{8,4},{10,6},{12,8},{14,10},{1,13},{3,15... | collective-permute-start | bytes 393224 | tf_op jit(solution)/shard_map/cond/branch_1_fun/ppermute | solution.py:97
  50.0 5.9 %collective-permute-start.26 = (bf16[64,1024]{1,0:T(8,128)(2,1)S(1)}, bf16[64,1024]{1,0:T(8,128)(2,1)S(1)}, u32[]{:S(2)}, u32[]{:S(2)}) collective-permute-start(bf16[64,1024]{1,0:T(8,128)(2,1)S(1)} %get-tuple-element.208), channel_id=1, source_target_pairs={{0,2},{2,0},{4,6},{6,4},{8,10},{10,8},{12,14},{14,12},{1,3},{3,1},... | collective-permute-start | bytes 393224 | tf_op jit(solution)/shard_map/cond/branch_1_fun/ppermute | solution.py:526
  55.9 11.4 %collective-permute-start.27 = (bf16[32,2048]{1,0:T(8,128)(2,1)S(1)}, bf16[32,2048]{1,0:T(8,128)(2,1)S(1)}, u32[]{:S(2)}, u32[]{:S(2)}) collective-permute-start(bf16[32,2048]{1,0:T(8,128)(2,1)S(1)} %get-tuple-element.217), channel_id=1, source_target_pairs={{0,2},{2,0},{4,6},{6,4},{8,10},{10,8},{12,14},{14,12},{1,3},{3,1},... | collective-permute-start | bytes 393224 | tf_op jit(solution)/shard_map/cond/branch_1_fun/ppermute | solution.py:529
  56.7 9.8 %collective-permute-start.28 = (bf16[32,1024]{1,0:T(8,128)(2,1)S(1)}, bf16[32,1024]{1,0:T(8,128)(2,1)S(1)}, u32[]{:S(2)}, u32[]{:S(2)}) collective-permute-start(bf16[32,1024]{1,0:T(8,128)(2,1)S(1)} %get-tuple-element.219), channel_id=1, source_target_pairs={{0,4},{2,6},{4,8},{6,10},{8,12},{10,14},{12,0},{14,2},{1,5},{3,7},... | collective-permute-start | bytes 196616 | tf_op jit(solution)/shard_map/cond/branch_1_fun/ppermute | solution.py:97
  59.7 7.1 %collective-permute-start.29 = (bf16[32,1024]{1,0:T(8,128)(2,1)S(1)}, bf16[32,1024]{1,0:T(8,128)(2,1)S(1)}, u32[]{:S(2)}, u32[]{:S(2)}) collective-permute-start(bf16[32,1024]{1,0:T(8,128)(2,1)S(1)} %get-tuple-element.220), channel_id=1, source_target_pairs={{0,8},{2,10},{4,12},{6,14},{8,0},{10,2},{12,4},{14,6},{1,9},{3,11}... | collective-permute-start | bytes 196616 | tf_op jit(solution)/shard_map/cond/branch_1_fun/ppermute | solution.py:97
  62.3 5.0 %collective-permute-start.30 = (bf16[32,1024]{1,0:T(8,128)(2,1)S(1)}, bf16[32,1024]{1,0:T(8,128)(2,1)S(1)}, u32[]{:S(2)}, u32[]{:S(2)}) collective-permute-start(bf16[32,1024]{1,0:T(8,128)(2,1)S(1)} %get-tuple-element.221), channel_id=1, source_target_pairs={{0,12},{2,14},{4,0},{6,2},{8,4},{10,6},{12,8},{14,10},{1,13},{3,15... | collective-permute-start | bytes 196616 | tf_op jit(solution)/shard_map/cond/branch_1_fun/ppermute | solution.py:97
  67.3 6.0 %collective-permute-start.31 = (bf16[32,2048]{1,0:T(8,128)(2,1)S(1)}, bf16[32,2048]{1,0:T(8,128)(2,1)S(1)}, u32[]{:S(2)}, u32[]{:S(2)}) collective-permute-start(bf16[32,2048]{1,0:T(8,128)(2,1)S(1)} %get-tuple-element.228), channel_id=1, source_target_pairs={{0,2},{2,0},{4,6},{6,4},{8,10},{10,8},{12,14},{14,12},{1,3},{3,1},... | collective-permute-start | bytes 393224 | tf_op jit(solution)/shard_map/cond/branch_1_fun/ppermute | solution.py:536
  69.6 3.7 %collective-permute-start.33 = (f32[16,64]{1,0:T(8,128)S(1)}, f32[16,64]{1,0:T(8,128)S(1)}, u32[]{:S(2)}, u32[]{:S(2)}) collective-permute-start(f32[16,64]{1,0:T(8,128)S(1)} %branch_1_fun.18.refs_4_), channel_id=1, source_target_pairs={{0,2},{2,0},{4,6},{6,4},{8,10},{10,8},{12,14},{14,12},{1,3},{3,1},... | collective-permute-start | bytes 12296 | tf_op jit(solution)/shard_map/cond/branch_1_fun/ppermute | solution.py:547
  73.8 6.8 %collective-permute-start.35 = (bf16[8,4096]{1,0:T(8,128)(2,1)S(1)}, bf16[8,4096]{1,0:T(8,128)(2,1)S(1)}, u32[]{:S(2)}, u32[]{:S(2)}) collective-permute-start(bf16[8,4096]{1,0:T(8,128)(2,1)S(1)} %get-tuple-element.237), channel_id=1, source_target_pairs={{0,4},{2,6},{4,8},{6,10},{8,12},{10,14},{12,0},{14,2},{1,5},{3,7},... | collective-permute-start | bytes 196616 | tf_op jit(solution)/shard_map/cond/branch_1_fun/ppermute | solution.py:97
  75.3 7.0 %collective-permute-start.36 = (bf16[8,4096]{1,0:T(8,128)(2,1)S(1)}, bf16[8,4096]{1,0:T(8,128)(2,1)S(1)}, u32[]{:S(2)}, u32[]{:S(2)}) collective-permute-start(bf16[8,4096]{1,0:T(8,128)(2,1)S(1)} %get-tuple-element.238), channel_id=1, source_target_pairs={{0,8},{2,10},{4,12},{6,14},{8,0},{10,2},{12,4},{14,6},{1,9},{3,11}... | collective-permute-start | bytes 196616 | tf_op jit(solution)/shard_map/cond/branch_1_fun/ppermute | solution.py:97
  76.9 5.4 %collective-permute-start.37 = (bf16[8,4096]{1,0:T(8,128)(2,1)S(1)}, bf16[8,4096]{1,0:T(8,128)(2,1)S(1)}, u32[]{:S(2)}, u32[]{:S(2)}) collective-permute-start(bf16[8,4096]{1,0:T(8,128)(2,1)S(1)} %get-tuple-element.239), channel_id=1, source_target_pairs={{0,12},{2,14},{4,0},{6,2},{8,4},{10,6},{12,8},{14,10},{1,13},{3,15... | collective-permute-start | bytes 196616 | tf_op jit(solution)/shard_map/cond/branch_1_fun/ppermute | solution.py:97
  (7 other events, 35.2 us)

commit v3 on v2

--- a/solution.py
+++ b/solution.py
@@ -9,8 +9,9 @@
 
 MOST = 8
 DIRECT = 8
-MINE, NEXT, STEP, PLACE = range(4)
+MINE, NEXT, STEP, PLACE, ARRIVE, PACKED = range(6)
 USUAL = 16
+USUAL_PAIR = 24
 BF = jnp.bfloat16
 F32 = jnp.float32
 I32 = jnp.int32
@@ -67,12 +68,6 @@
         else:
             self.order = steps
 
-    def arrival(self):
-        steps = jnp.arange(self.shards, dtype=I32)
-        if not self.direct:
-            return steps
-        return steps % self.slow * self.fast + steps // self.slow
-
     def back(self, a, c):
         S, F = self.slow, self.fast
         return [(s * F + f, (s - a) % S * F + (f - c) % F) for s in range(S) for f in range(F)]
@@ -98,26 +93,110 @@
         return got
 
 
-def stage_kernel(*refs):
-    count = len(refs) // 2
-    sems = refs[2 * count]
-    copies = [pltpu.make_async_copy(refs[n], refs[count + n], sems.at[n]) for n in range(count)]
+def tables_kernel(
+    ways,
+    slots,
+    order_ref,
+    me_ref,
+    ids_ref,
+    slot_ref,
+    x_ref,
+    shrink_ref,
+    marks_ref,
+    in_ref,
+    out_ref,
+    facts_ref,
+    kept_ref,
+    held_ref,
+    sems,
+):
+    copies = [
+        pltpu.make_async_copy(x_ref, kept_ref, sems.at[0]),
+        pltpu.make_async_copy(shrink_ref, held_ref, sems.at[1]),
+    ]
     for copy in copies:
         copy.start()
+    rows, variants = ids_ref.shape[0], slot_ref.shape[1]
+    shards = order_ref.shape[0]
+    own_rows = rows // shards
+    me = me_ref[0].astype(F32)
+    order = [order_ref[b].astype(F32) for b in range(shards)]
+    count = lambda shape, axis: lax.broadcasted_iota(I32, shape, axis).astype(F32)
+    across = lambda a: jnp.sum(a, axis=1, keepdims=True)
+    along = lambda a: jnp.sum(a, axis=0, keepdims=True)
+    line, lane = count((rows, rows), 0), count((rows, rows), 1)
+    matches = ids_ref[...].astype(F32) == count((rows, variants), 1)
+    slot = across(jnp.where(matches, slot_ref[...].astype(F32), 0.0))
+    owner = across((slot >= (count((rows, shards), 1) + 1.0) * slots).astype(F32))
+    owner_along = along(jnp.where(line == lane, owner, 0.0))
+    same = owner == owner_along
+    place = across((same & (lane < line)).astype(F32))
+    paired = ways.direct and ways.fast == 2
+    beside = jnp.zeros_like(place)
+    if paired:
+        odd = across((owner == 2.0 * count((rows, shards), 1) + 1.0).astype(F32))
+        beside = across((owner + 1.0 - 2.0 * odd == owner_along).astype(F32))
+    facts_ref[0] = jnp.max(place).astype(I32)
+    facts_ref[1] = jnp.max(across(same.astype(F32)) + beside).astype(I32)
+    facts_ref[2] = jnp.sum((owner == me).astype(F32)).astype(I32)
+    facts_ref[3] = jnp.sum((owner == order[ways.slow % shards]).astype(F32)).astype(I32)
+    row_along, row_down = count((1, rows), 1), count((rows, 1), 0)
+    at_along, at_down = row_along, row_down
+    for b in range(shards):
+        shift = (order[b] - b) * own_rows
+        low, high = b * own_rows, (b + 1) * own_rows
+        at_along = jnp.where((row_along >= low) & (row_along < high), row_along + shift, at_along)
+        at_down = jnp.where((row_down >= low) & (row_down < high), row_down + shift, at_down)
+    turned = lambda a: along(jnp.where(line == at_along, a, 0.0))
+    slot_along = along(jnp.where(line == lane, slot, 0.0))
+    slot = across(jnp.where(lane == at_down, slot_along, 0.0))
+    owner, place, beside = turned(owner), turned(place), turned(beside)
+    step = jnp.zeros_like(owner)
+    arrive, packed = step, place
+    for b in range(shards):
+        hit = owner == order[b]
+        step = jnp.where(hit, float(b), step)
+        arrive = jnp.where(hit, float(b % ways.slow if paired else b), arrive)
+        if paired and b >= ways.slow:
+            packed = jnp.where(hit, place + beside, packed)
+    lines = {
+        MINE: jnp.where(owner == me, place, -1.0),
+        NEXT: jnp.where(owner == order[ways.slow % shards], place, -1.0),
+        STEP: step,
+        PLACE: place,
+        ARRIVE: arrive,
+        PACKED: packed,
+    }
+    for n, values in lines.items():
+        marks_ref[n : n + 1] = values.astype(I32)
+    local = slot - me * slots
+    for ref in (in_ref, out_ref):
+        wide = ref.shape[1] // slots
+        column = count(ref.shape, 1)
+        inside = (column >= local * wide) & (column < (local + 1.0) * wide)
+        ref[...] = inside.astype(F32).astype(ref.dtype)
     for copy in copies:
         copy.wait()
 
 
-def stage(*arrays):
-    return pl.pallas_call(
-        stage_kernel,
-        out_shape=tuple(jax.ShapeDtypeStruct(array.shape, array.dtype) for array in arrays),
-        in_specs=[FAR] * len(arrays),
-        out_specs=(WHOLE,) * len(arrays),
-        scratch_shapes=[pltpu.SemaphoreType.DMA((len(arrays),))],
+def tables(ways, me, ids, variant_slot, x, shrink, slots, rank):
+    rows = ids.shape[0]
+    return pl.pallas_call(
+        functools.partial(tables_kernel, ways, slots),
+        out_shape=(
+            jax.ShapeDtypeStruct((8, rows), I32),
+            jax.ShapeDtypeStruct((rows, slots * 2 * rank), F32),
+            jax.ShapeDtypeStruct((rows, slots * rank), BF),
+            jax.ShapeDtypeStruct((4,), I32),
+            jax.ShapeDtypeStruct(x.shape, BF),
+            jax.ShapeDtypeStruct(shrink.shape, BF),
+        ),
+        in_specs=[SCALARS, SCALARS, WHOLE, WHOLE, FAR, FAR],
+        out_specs=(WHOLE, WHOLE, WHOLE, SCALARS, WHOLE, WHOLE),
+        scratch_shapes=[pltpu.SemaphoreType.DMA((2,))],
         compiler_params=params(52),
-        cost_estimate=cost(0, sum(4 * array.size for array in arrays)),
-    )(*arrays)
+        cost_estimate=cost(0, 4 * x.size + 4 * shrink.size),
+    )(ways.order, me, ids, variant_slot, x, shrink)
 
 
 def low_in_kernel(count, shrink_ref, mask_ref, *refs):
@@ -240,20 +319,25 @@
     )(side, x, gate_weight, up_weight)
 
 
-def hidden_kernel(cap, count, own_ref, got_ref, marks_ref, arrive_ref, *refs):
+def hidden_kernel(cap, room, count, own_ref, got_ref, marks_ref, *refs):
     parts, hid_ref, out_refs = refs[:count], refs[count], refs[count + 1 :]
-    rows, half = hid_ref.shape
+    half = hid_ref.shape[1]
     cells = sum(part.shape[0] for part in parts)
-    place = one_hot(cells, arrive_ref[0:1] * cap + arrive_ref[1:2])
+    first_cell = marks_ref[ARRIVE : ARRIVE + 1] * (2 * room) + marks_ref[PACKED : PACKED + 1]
+    places = [one_hot(cells, first_cell + kind * room) for kind in range(2)]
     tall = out_refs[0].shape[0]
     leave = marks_ref[STEP : STEP + 1] * cap + marks_ref[PLACE : PLACE + 1]
     send = one_hot(tall * len(out_refs), leave)
     block = min(256, half)
     for first in range(0, half, block):
         here = pl.ds(first, block)
-        delta = dot_first(place, jnp.concatenate([part[:, here] for part in parts], axis=0))
-        gate = own_ref[0, :, here] + got_ref[0, :, here].astype(F32) + delta[:rows]
-        up = own_ref[1, :, here] + got_ref[1, :, here].astype(F32) + delta[rows:]
+        delta = jnp.concatenate([part[:, here] for part in parts], axis=0)
+        gate, up = [
+            own_ref[kind, :, here]
+            + got_ref[kind, :, here].astype(F32)
+            + dot_first(places[kind], delta)
+            for kind in range(2)
+        ]
         hidden = (gate / (1.0 + jnp.exp(-gate)) * up).astype(BF)
         hid_ref[:, here] = hidden
         sent = dot(send, hidden).astype(BF)
@@ -261,16 +345,43 @@
             out_ref[:, here] = sent[n * tall : (n + 1) * tall]
 
 
-def hidden_half(own, got, parts, marks, arrive, cap, shards, count):
+def hidden_half(own, got, parts, marks, cap, room, shards, count):
     rows, half = own.shape[1:]
     cells = shards * cap
     return pl.pallas_call(
-        functools.partial(hidden_kernel, cap, len(parts)),
+        functools.partial(hidden_kernel, cap, room, len(parts)),
         out_shape=(jax.ShapeDtypeStruct((rows, half), BF),)
         + (jax.ShapeDtypeStruct((cells // count, half), BF),) * count,
         compiler_params=params(40),
         cost_estimate=cost(10 * half * cells * rows, 2 * half * (6 * rows + 3 * cells)),
-    )(own, got, marks, arrive, *parts)
+    )(own, got, marks, *parts)
+
+
+def pack_kernel(cap, facts_ref, own_ref, got_ref, *out_refs):
+    column = lax.broadcasted_iota(I32, (1, 4 * cap), 1)
+    from_got = column >= 2 * cap
+    column = column - jnp.where(from_got, 2 * cap, 0)
+    kind = jnp.where(column >= cap, 1, 0)
+    row = column - kind * cap
+    live = row < jnp.where(from_got, facts_ref[3], facts_ref[2])
+    row = row + jnp.where(from_got, facts_ref[2], 0)
+    room = out_refs[0].shape[0] // 2
+    packing = one_hot(2 * room, jnp.where(live, row + kind * room, -1))
+    for a, out_ref in enumerate(out_refs):
+        here = pl.ds(a * 2 * cap, 2 * cap)
+        both = jnp.concatenate([own_ref[here], got_ref[here]], axis=0)
+        out_ref[...] = dot(packing, both).astype(BF)
+
+
+def pack(facts, own, got, cap, room, count):
+    half = own.shape[1]
+    return pl.pallas_call(
+        functools.partial(pack_kernel, cap),
+        out_shape=(jax.ShapeDtypeStruct((2 * room, half), BF),) * count,
+        in_specs=[SCALARS, WHOLE, WHOLE],
+        compiler_params=params(16),
+        cost_estimate=cost(0, 8 * own.size),
+    )(facts, own, got)
 
 
 def relay_kernel(own_ref, got_ref, *out_refs):
@@ -445,44 +556,22 @@
         variant_ids, variant_slot, shrink_in, token_parts[first_hop] = tied(
             variant_ids, variant_slot, shrink_in, token_parts[first_hop]
         )
-    all_ids, all_slots = [variant_ids[:, 0]], [variant_slot]
+    marks, mask_in, slot_mask, facts, token_parts[0], shrink_in = tables(
+        ways,
+        me.reshape(1),
+        variant_ids,
+        variant_slot.reshape(1, variants),
+        token_parts[0],
+        shrink_in,
+        slots,
+        rank,
+    )
+    most_facts = facts
     for turn in range(1, 1 if ways.direct else groups):
         pairs = [(g, (g + turn) % groups) for g in range(groups)]
-        all_ids.append(lax.ppermute(all_ids[0], "groups", pairs))
-        all_slots.append(lax.ppermute(all_slots[0], "groups", pairs))
-    all_ids, all_slots = jnp.stack(all_ids), jnp.stack(all_slots)
-    token_parts[0], shrink_in = stage(token_parts[0], shrink_in)
-
-    matches = all_ids[:, :, None] == jnp.arange(variants, dtype=I32)
-    slot_row = jnp.sum(jnp.where(matches, all_slots[:, None, :], 0), axis=2)
-    owner = slot_row // slots
-    index = jnp.arange(rows, dtype=I32)
-    earlier = (owner[:, :, None] == owner[:, None, :]) & (index[None, :] < index[:, None])
-    place = jnp.sum(earlier.astype(I32), axis=2)
-    highest = jnp.max(place).reshape(1)
-    slot_row, place = slot_row[0], place[0]
-    where_row = order[:, None] == jnp.arange(shards, dtype=I32)[None, :]
-    turned = lambda a: jnp.sum(
-        jnp.where(where_row[:, :, None], a.reshape(1, shards, own_rows), 0), axis=1
-    ).reshape(rows)
-    slot_row, place = turned(slot_row), turned(place)
-    owner = slot_row // slots
-    of_block = owner[:, None] == order[None, :]
-    step = jnp.sum(jnp.where(of_block, jnp.arange(shards, dtype=I32)[None, :], 0), axis=1)
-    arrival = jnp.sum(jnp.where(of_block, ways.arrival()[None, :], 0), axis=1)
-    local = slot_row - me * slots
-    next_owner = order[ways.slow % shards]
-    marks = jnp.stack(
-        [jnp.where(owner == me, place, -1), jnp.where(owner == next_owner, place, -1), step, place]
-    )
-    arrive = jnp.stack(
-        [jnp.concatenate([2 * arrival, 2 * arrival + 1]), jnp.concatenate([place, place])]
-    )
+        most_facts = jnp.maximum(most_facts, lax.ppermute(facts, "groups", pairs))
     kinds = jnp.arange(2, dtype=I32)
     in_cols = jnp.arange(slots * 2 * rank, dtype=I32)
-    mask_in = (local[:, None] == (in_cols // (2 * rank))[None, :]).astype(F32)
-    out_cols = jnp.arange(slots * rank, dtype=I32)
-    slot_mask = (local[:, None] == (out_cols // rank)[None, :]).astype(BF)
     rank_at = in_cols % rank
     kind_at = in_cols // rank % 2
     row_at = in_cols // (2 * rank) * (2 * half_rank) + kind_at * half_rank + rank_at % half_rank
@@ -495,7 +584,7 @@
     x, low_own = low_in_pairs(token_parts, shrink_in, mask_in)
     low_got = swap(low_own)
 
-    def partial_sums(cap):
+    def partial_sums(cap, room):
         made = expand_rows(at_here, low_own, low_got, marks, cols, near, far, cap, split)
         held, *made = tied(x, *made)
         expand = expand_down.reshape(slots * rank, width)
@@ -503,7 +592,7 @@
             beside = lax.ppermute(made[1], "ff", ways.back(0, 1))
             base_there = base_half(there, held, gate_weight, up_weight, half, BF)
             base_there, beside, expand = tied(base_there, beside, expand)
-            made = relay(made[0], beside, ways.slow)
+            made = pack(facts, made[0], beside, cap, room, ways.slow)
             held, *made = tied(held, *made)
             delta = ways.slow_steps(made)
             expand_beside = lax.ppermute(expand, "ff", ways.back(0, 1))
@@ -516,7 +605,7 @@
         if split == 2:
             base_own, expand_beside = tied(base_own, expand_beside)
         hidden, *sent = hidden_half(
-            base_own, base_got, delta, marks, arrive, cap, shards, split
+            base_own, base_got, delta, marks, cap, room, shards, split
         )
         hidden_far = swap(hidden)
         shrink = shrink_down.reshape(slots * rank, -1)
@@ -558,11 +647,17 @@
         )
         return ways.slow_steps(parts)
 
+    most_room = 2 * most if split == 2 else most
     if most <= USUAL:
-        parts = partial_sums(most)
+        parts = partial_sums(most, most_room)
     else:
+        usual = most_facts[0] < USUAL
+        if split == 2:
+            usual = usual & (most_facts[1] <= USUAL_PAIR)
         parts = lax.cond(
-            highest[0] < USUAL, lambda: partial_sums(USUAL), lambda: partial_sums(most)
+            usual,
+            lambda: partial_sums(USUAL, USUAL_PAIR if split == 2 else USUAL),
+            lambda: partial_sums(most, most_room),
         )
     return sum(part.astype(F32) for part in parts).astype(BF)
 

time: 83.5 us -> 83.8 us (level)
  starting transfers between devices: 37 us -> 31.8 us
  waiting for transfers between devices: 11.2 us -> 15.7 us
  other arithmetic: 3.71 us -> 0.91 us
  Pallas kernels: 28 us -> 30.4 us
  local copies, waits for them, and re-layouts: 1.91 us -> 2.83 us
    ppermute x9, starting transfers between devices: 16.2 us -> 13.4 us  [slow_steps(): got[-a % self.slow] = lax.ppermute(blocks[a], 'ff', self.back(a, 0))]
    ppermute x4, waiting for transfers between devices: 0.95 us -> 3.44 us  [gather(): lax.ppermute(part, 'ff', self.back(0, -c))]
    pallas_call x2 -> x3, Pallas kernels: 1.89 us -> 4.35 us  [the longest x1 2.7 us: tables(): pl.pallas_call(functools.partial(tables_kernel, ways, slots), out_shape=(...]
    ppermute x4, starting transfers between devices: 5.5 us -> 4.12 us  [gather(): lax.ppermute(part, 'ff', self.back(0, -c))]
    ppermute x3, waiting for transfers between devices: 0.26 us -> 1.51 us  [gather(): lax.ppermute(block, 'ff', self.back(-a, 0))]
    reduce_sum x4 -> x0, other arithmetic: 1.13 us -> none  [the longest x1 0.76 us: per_device(): slot_row = jnp.sum(jnp.where(matches, all_slots[:, None, :], 0), axis=2)]
    ppermute x1, waiting for transfers between devices: 0.01 us -> 1.07 us  [partial_sums(): expand_beside = lax.ppermute(expand, 'ff', ways.back(0, 1))]
  transfers between devices with their start and end apart: 28 -> 28, of which waited for: 12 -> 11; matrix products, arithmetic and copies ran while one was open for 5% -> 2% of each run, Pallas kernels for 28% -> 30%
where the time goes in v3:
time: 83.8 us; the launch traced here: 83.6 us
  starting transfers between devices  31.8 us (38%)
  Pallas kernels  30.4 us (36%)
  waiting for transfers between devices  15.7 us (19%)
  local copies, waits for them, and re-layouts  2.83 us (3%)
  between operations  1.39 us (2%)
  other arithmetic  0.91 us (1%)
    ppermute x9, starting transfers between devices, slow_steps(): got[-a % self.slow] = lax.ppermute(blocks[a], 'ff', self.back(a, 0))  13.4 us
    pallas_call x2, Pallas kernels, base_half(): pl.pallas_call(base_kernel, out_shape=jax.ShapeDtypeStruct((2, rows, half...  12.5 us
    pallas_call x2, Pallas kernels, down_base(): pl.pallas_call(functools.partial(down_kernel, start), out_shape=outs, in_...  8.17 us
    ppermute x3, starting transfers between devices, gather(): lax.ppermute(block, 'ff', self.back(-a, 0))  7.41 us
    ppermute x9, waiting for transfers between devices, slow_steps(): got[-a % self.slow] = lax.ppermute(blocks[a], 'ff', self.back(a, 0))  5.33 us
    ppermute x4, starting transfers between devices, gather(): lax.ppermute(part, 'ff', self.back(0, -c))  4.12 us
    ppermute x4, waiting for transfers between devices, gather(): lax.ppermute(part, 'ff', self.back(0, -c))  3.44 us
    pallas_call x1, Pallas kernels, expand_rows(): pl.pallas_call(functools.partial(expand_kernel, cap, fast), out_shape=(ou...  2.87 us
  transfers between devices with their start and end apart: 28, of which 11 were waited for; matrix products, arithmetic and copies ran while one was open for 2% of the time, Pallas kernels for 30%

profile of v3, /device:TPU:0, one launch (start us, length us, event | category | flops | bytes accessed | tf_op | source)
XLA Modules:
  0.0 83.6 jit_solution(14061946536509217302)
XLA Ops:
  0.5 3.6 %collective-permute-start.41 = (bf16[8,4096]{1,0:T(8,128)(2,1)}, bf16[8,4096]{1,0:T(8,128)(2,1)S(1)}, u32[]{:S(2)}, u32[]{:S(2)}) collective-permute-start(bf16[8,4096]{1,0:T(8,128)(2,1)} %x_ref.1), channel_id=1, source_target_pairs={{0,8},{2,10},{4,12},{6,14},{8,0},{10,2},{12,4},{14,6},{1,9},{3,11}... | collective-permute-start | bytes 196616 | tf_op jit(solution)/shard_map/ppermute | solution.py:79
  4.0 1.6 %collective-permute-start.39 = (bf16[8,4096]{1,0:T(8,128)(2,1)}, bf16[8,4096]{1,0:T(8,128)(2,1)S(1)}, u32[]{:S(2)}, u32[]{:S(2)}) collective-permute-start(bf16[8,4096]{1,0:T(8,128)(2,1)} %x_ref.1), channel_id=1, source_target_pairs={{0,4},{2,6},{4,8},{6,10},{8,12},{10,14},{12,0},{14,2},{1,5},{3,7},... | collective-permute-start | bytes 196616 | tf_op jit(solution)/shard_map/ppermute | solution.py:79
  5.6 1.5 %collective-permute-start.43 = (bf16[8,4096]{1,0:T(8,128)(2,1)}, bf16[8,4096]{1,0:T(8,128)(2,1)S(1)}, u32[]{:S(2)}, u32[]{:S(2)}) collective-permute-start(bf16[8,4096]{1,0:T(8,128)(2,1)} %x_ref.1), channel_id=1, source_target_pairs={{0,2},{2,0},{4,6},{6,4},{8,10},{10,8},{12,14},{14,12},{1,3},{3,1},... | collective-permute-start | bytes 196616 | tf_op jit(solution)/shard_map/ppermute | solution.py:83
  7.1 2.2 %collective-permute-start.42 = (bf16[8,4096]{1,0:T(8,128)(2,1)}, bf16[8,4096]{1,0:T(8,128)(2,1)S(1)}, u32[]{:S(2)}, u32[]{:S(2)}) collective-permute-start(bf16[8,4096]{1,0:T(8,128)(2,1)} %x_ref.1), channel_id=1, source_target_pairs={{0,12},{2,14},{4,0},{6,2},{8,4},{10,6},{12,8},{14,10},{1,13},{3,15... | collective-permute-start | bytes 196616 | tf_op jit(solution)/shard_map/ppermute | solution.py:79
  10.2 1.5 %collective-permute-done.42.refs_5_ = bf16[8,4096]{1,0:T(8,128)(2,1)S(1)} collective-permute-done((bf16[8,4096]{1,0:T(8,128)(2,1)}, bf16[8,4096]{1,0:T(8,128)(2,1)S(1)}, u32[]{:S(2)}, u32[]{:S(2)}) %collective-permute-start.42) | collective-permute-done | bytes 65568 | tf_op jit(solution)/shard_map/ppermute | solution.py:79
  11.7 1.2 %collective-permute-start.45 = (bf16[8,4096]{1,0:T(8,128)(2,1)S(1)}, bf16[8,4096]{1,0:T(8,128)(2,1)S(1)}, u32[]{:S(2)}, u32[]{:S(2)}) collective-permute-start(bf16[8,4096]{1,0:T(8,128)(2,1)S(1)} %collective-permute-done.42.refs_5_), channel_id=1, source_target_pairs={{0,2},{2,0},{4,6},{6,4},{8,10},{10,8},{12,14},{14,12},{1,3},{3,1},... | collective-permute-start | bytes 196616 | tf_op jit(solution)/shard_map/ppermute | solution.py:83
  13.8 3.4 %collective-permute-done.40.refs_7_ = bf16[8,4096]{1,0:T(8,128)(2,1)S(1)} collective-permute-done((bf16[8,4096]{1,0:T(8,128)(2,1)S(1)}, bf16[8,4096]{1,0:T(8,128)(2,1)S(1)}, u32[]{:S(2)}, u32[]{:S(2)}) %collective-permute-start.40) | collective-permute-done | bytes 65568 | tf_op jit(solution)/shard_map/ppermute | solution.py:83
  19.4 2.7 %shard_map.100 = (s32[8,64]{1,0:T(8,128)S(1)}, f32[64,128]{1,0:T(8,128)S(1)}, bf16[64,64]{1,0:T(8,128)(2,1)S(1)}, s32[4]{0:T(128)S(1)}, bf16[8,4096]{1,0:T(8,128)(2,1)S(1)}, /*index=5*/bf16[128,4096]{1,0:T(8,128)(2,1)S(1)}) custom-call(s32[8]{0:T(128)S(1)} %fusion.order_ref, s32[1]{0:T(128)} %bitcast.6.me_ref, s32[64,1]{1,0:T(8,128)S(1)} %copy.11.ids_ref, ...), custom_call_target="tpu_custom_call" | custom-call | bytes 2228224 | tf_op jit(solution)/shard_map/pallas_call | solution.py:184
  25.2 57.7 %conditional.3 = (bf16[8,4096]{1,0:T(8,128)(2,1)S(1)}, f32[8,4096]{1,0:T(8,128)S(1)}, f32[8,4096]{1,0:T(8,128)S(1)}, f32[8,4096]{1,0:T(8,128)S(1)}) conditional(s32[]{:T(128)} %bitcast.10, (s32[]{:T(128)}, s32[8]{0:T(128)S(1)}, s32[8]{0:T(128)S(1)}, f32[64,128]{1,0:T(8,128)S(1)}, f32[64,128]{1,0:T(8,128)S(1)}, /*index=5*/s32[8,64]{1,0:T(8,128)S(1)}, ...), branch_computations={%region_0.1_spmd, %region_1.2_spmd} | conditional | flops 3724640256 | bytes 92963768
  25.4 2.9 %branch_1_fun.10 = (bf16[128,1024]{1,0:T(8,128)(2,1)S(1)}, bf16[128,1024]{1,0:T(8,128)(2,1)S(1)}) custom-call(s32[8]{0:T(128)S(1)} %multiply_add_fusion.1.at_ref, f32[64,128]{1,0:T(8,128)S(1)} %get-tuple-element.175.own_ref, f32[64,128]{1,0:T(8,128)S(1)} %get-tuple-element.176.got_ref, s32[8,64]{1,0:T(8,128)S(1)} %get-tuple-element.177.marks_ref.refs_8_, ...), custom_call_target="tpu_custom_call" | custom-call | flops 134217728 | bytes 5242880 | tf_op jit(solution)/shard_map/cond/branch_1_fun/pallas_call | solution.py:270
  29.2 6.3 %branch_1_fun.11 = bf16[2,64,1024]{2,1,0:T(8,128)(2,1)S(1)} custom-call(s32[1]{0:T(128)S(6)} %sub.32.side_ref, bf16[64,4096]{1,0:T(8,128)(2,1)S(1)} %get-tuple-element.195.x_ref, bf16[4096,2048]{1,0:T(8,128)(2,1)} %get-tuple-element.186.gate_ref, bf16[4096,2048]{1,0:T(8,128)(2,1)} %get-tuple-element.187.up_ref), custom_call_target="tpu_custom_call" | custom-call | flops 1073741824 | bytes 17301504 | tf_op jit(solution)/shard_map/cond/branch_1_fun/pallas_call | solution.py:307
  35.5 1.6 %collective-permute-done.19.got_ref = bf16[128,1024]{1,0:T(8,128)(2,1)S(1)} collective-permute-done((bf16[128,1024]{1,0:T(8,128)(2,1)S(1)}, bf16[128,1024]{1,0:T(8,128)(2,1)S(1)}, u32[]{:S(2)}, u32[]{:S(2)}) %collective-permute-start.19) | collective-permute-done | bytes 262176 | tf_op jit(solution)/shard_map/cond/branch_1_fun/ppermute | solution.py:592
  39.3 3.9 %collective-permute-start.23 = (bf16[48,1024]{1,0:T(8,128)(2,1)S(1)}, bf16[48,1024]{1,0:T(8,128)(2,1)S(1)}, u32[]{:S(2)}, u32[]{:S(2)}) collective-permute-start(bf16[48,1024]{1,0:T(8,128)(2,1)S(1)} %get-tuple-element.201), channel_id=1, source_target_pairs={{0,8},{2,10},{4,12},{6,14},{8,0},{10,2},{12,4},{14,6},{1,9},{3,11}... | collective-permute-start | bytes 294920 | tf_op jit(solution)/shard_map/cond/branch_1_fun/ppermute | solution.py:92
  43.3 6.2 %branch_1_fun.13.own_ref = f32[2,64,1024]{2,1,0:T(8,128)S(1)} custom-call(s32[1]{0:T(128)} %bitcast.3.side_ref.core_ref, bf16[64,4096]{1,0:T(8,128)(2,1)S(1)} %get-tuple-element.195.x_ref, bf16[4096,2048]{1,0:T(8,128)(2,1)} %get-tuple-element.186.gate_ref, bf16[4096,2048]{1,0:T(8,128)(2,1)} %get-tuple-element.187.up_ref), custom_call_target="tpu_custom_call" | custom-call | flops 1073741824 | bytes 17301504 | tf_op jit(solution)/shard_map/cond/branch_1_fun/pallas_call | solution.py:307
  52.9 4.2 %branch_1_fun.15 = (f32[32,2048]{1,0:T(8,128)S(1)}, bf16[32,2048]{1,0:T(8,128)(2,1)S(1)}) custom-call(s32[1]{0:T(128)} %bitcast.3.side_ref.core_ref, bf16[64,1024]{1,0:T(8,128)(2,1)S(1)} %get-tuple-element.214.near_ref, bf16[64,1024]{1,0:T(8,128)(2,1)S(1)} %collective-permute-done.25.far_ref, bf16[2048,4096]{1,0:T(8,128)(2,1)} %get-tuple-element.204.weight_ref), custom_call_target="tpu_custom_call" | custom-call | flops 536870912 | bytes 8912896 | tf_op jit(solution)/shard_map/cond/branch_1_fun/pallas_call | solution.py:436
  58.3 2.4 %collective-permute-start.28 = (bf16[32,1024]{1,0:T(8,128)(2,1)S(1)}, bf16[32,1024]{1,0:T(8,128)(2,1)S(1)}, u32[]{:S(2)}, u32[]{:S(2)}) collective-permute-start(bf16[32,1024]{1,0:T(8,128)(2,1)S(1)} %get-tuple-element.219), channel_id=1, source_target_pairs={{0,4},{2,6},{4,8},{6,10},{8,12},{10,14},{12,0},{14,2},{1,5},{3,7},... | collective-permute-start | bytes 196616 | tf_op jit(solution)/shard_map/cond/branch_1_fun/ppermute | solution.py:92
  60.8 2.1 %collective-permute-start.29 = (bf16[32,1024]{1,0:T(8,128)(2,1)S(1)}, bf16[32,1024]{1,0:T(8,128)(2,1)S(1)}, u32[]{:S(2)}, u32[]{:S(2)}) collective-permute-start(bf16[32,1024]{1,0:T(8,128)(2,1)S(1)} %get-tuple-element.220), channel_id=1, source_target_pairs={{0,8},{2,10},{4,12},{6,14},{8,0},{10,2},{12,4},{14,6},{1,9},{3,11}... | collective-permute-start | bytes 196616 | tf_op jit(solution)/shard_map/cond/branch_1_fun/ppermute | solution.py:92
  63.2 4.0 %branch_1_fun.17 = (f32[32,2048]{1,0:T(8,128)S(1)}, bf16[32,2048]{1,0:T(8,128)(2,1)S(1)}) custom-call(s32[1]{0:T(128)} %bitcast.3.side_ref.core_ref, bf16[64,1024]{1,0:T(8,128)(2,1)S(1)} %get-tuple-element.214.near_ref, bf16[64,1024]{1,0:T(8,128)(2,1)S(1)} %collective-permute-done.25.far_ref, bf16[2048,4096]{1,0:T(8,128)(2,1)} %get-tuple-element.204.weight_ref), custom_call_target="tpu_custom_call" | custom-call | flops 536870912 | bytes 8912896 | tf_op jit(solution)/shard_map/cond/branch_1_fun/pallas_call | solution.py:436
  69.6 1.1 %collective-permute-start.33 = (f32[16,64]{1,0:T(8,128)S(1)}, f32[16,64]{1,0:T(8,128)S(1)}, u32[]{:S(2)}, u32[]{:S(2)}) collective-permute-start(f32[16,64]{1,0:T(8,128)S(1)} %branch_1_fun.18.refs_4_), channel_id=1, source_target_pairs={{0,2},{2,0},{4,6},{6,4},{8,10},{10,8},{12,14},{14,12},{1,3},{3,1},... | collective-permute-start | bytes 12296 | tf_op jit(solution)/shard_map/cond/branch_1_fun/ppermute | solution.py:636
  71.4 1.3 %collective-permute-done.34.refs_7_ = f32[16,64]{1,0:T(8,128)S(1)} collective-permute-done((f32[16,64]{1,0:T(8,128)S(1)}, f32[16,64]{1,0:T(8,128)S(1)}, u32[]{:S(2)}, u32[]{:S(2)}) %collective-permute-start.34) | collective-permute-done | bytes 4128 | tf_op jit(solution)/shard_map/cond/branch_1_fun/ppermute | solution.py:640
  73.8 1.4 %collective-permute-start.35 = (bf16[8,4096]{1,0:T(8,128)(2,1)S(1)}, bf16[8,4096]{1,0:T(8,128)(2,1)S(1)}, u32[]{:S(2)}, u32[]{:S(2)}) collective-permute-start(bf16[8,4096]{1,0:T(8,128)(2,1)S(1)} %get-tuple-element.237), channel_id=1, source_target_pairs={{0,4},{2,6},{4,8},{6,10},{8,12},{10,14},{12,0},{14,2},{1,5},{3,7},... | collective-permute-start | bytes 196616 | tf_op jit(solution)/shard_map/cond/branch_1_fun/ppermute | solution.py:92
  75.2 1.6 %collective-permute-start.36 = (bf16[8,4096]{1,0:T(8,128)(2,1)S(1)}, bf16[8,4096]{1,0:T(8,128)(2,1)S(1)}, u32[]{:S(2)}, u32[]{:S(2)}) collective-permute-start(bf16[8,4096]{1,0:T(8,128)(2,1)S(1)} %get-tuple-element.238), channel_id=1, source_target_pairs={{0,8},{2,10},{4,12},{6,14},{8,0},{10,2},{12,4},{14,6},{1,9},{3,11}... | collective-permute-start | bytes 196616 | tf_op jit(solution)/shard_map/cond/branch_1_fun/ppermute | solution.py:92
  77.7 2.9 %collective-permute-done.35 = bf16[8,4096]{1,0:T(8,128)(2,1)S(1)} collective-permute-done((bf16[8,4096]{1,0:T(8,128)(2,1)S(1)}, bf16[8,4096]{1,0:T(8,128)(2,1)S(1)}, u32[]{:S(2)}, u32[]{:S(2)}) %collective-permute-start.35) | collective-permute-done | bytes 65568 | tf_op jit(solution)/shard_map/cond/branch_1_fun/ppermute | solution.py:92
  80.7 2.0 %collective-permute-done.36 = bf16[8,4096]{1,0:T(8,128)(2,1)S(1)} collective-permute-done((bf16[8,4096]{1,0:T(8,128)(2,1)S(1)}, bf16[8,4096]{1,0:T(8,128)(2,1)S(1)}, u32[]{:S(2)}, u32[]{:S(2)}) %collective-permute-start.36) | collective-permute-done | bytes 65568 | tf_op jit(solution)/shard_map/cond/branch_1_fun/ppermute | solution.py:92
  (67 shorter events, 19.8 us)
Async XLA Ops:
  0.0 12.9 %collective-permute-start.38 = (bf16[64,16384]{1,0:T(8,128)(2,1)}, bf16[64,16384]{1,0:T(8,128)(2,1)S(1)}, u32[]{:S(2)}, u32[]{:S(2)}) collective-permute-start(bf16[64,16384]{1,0:T(8,128)(2,1)} %bitcast.14), channel_id=1, source_target_pairs={{0,1},{1,0},{2,3},{3,2},{4,5},{5,4},{6,7},{7,6},{8,9},{9,8},{10,11... | collective-permute-start | bytes 6291464 | tf_op jit(solution)/shard_map/ppermute | solution.py:549
  0.5 9.2 %collective-permute-start.41 = (bf16[8,4096]{1,0:T(8,128)(2,1)}, bf16[8,4096]{1,0:T(8,128)(2,1)S(1)}, u32[]{:S(2)}, u32[]{:S(2)}) collective-permute-start(bf16[8,4096]{1,0:T(8,128)(2,1)} %x_ref.1), channel_id=1, source_target_pairs={{0,8},{2,10},{4,12},{6,14},{8,0},{10,2},{12,4},{14,6},{1,9},{3,11}... | collective-permute-start | bytes 196616 | tf_op jit(solution)/shard_map/ppermute | solution.py:79
  4.0 8.9 %collective-permute-start.39 = (bf16[8,4096]{1,0:T(8,128)(2,1)}, bf16[8,4096]{1,0:T(8,128)(2,1)S(1)}, u32[]{:S(2)}, u32[]{:S(2)}) collective-permute-start(bf16[8,4096]{1,0:T(8,128)(2,1)} %x_ref.1), channel_id=1, source_target_pairs={{0,4},{2,6},{4,8},{6,10},{8,12},{10,14},{12,0},{14,2},{1,5},{3,7},... | collective-permute-start | bytes 196616 | tf_op jit(solution)/shard_map/ppermute | solution.py:79
  5.6 16.5 %collective-permute-start.43 = (bf16[8,4096]{1,0:T(8,128)(2,1)}, bf16[8,4096]{1,0:T(8,128)(2,1)S(1)}, u32[]{:S(2)}, u32[]{:S(2)}) collective-permute-start(bf16[8,4096]{1,0:T(8,128)(2,1)} %x_ref.1), channel_id=1, source_target_pairs={{0,2},{2,0},{4,6},{6,4},{8,10},{10,8},{12,14},{14,12},{1,3},{3,1},... | collective-permute-start | bytes 196616 | tf_op jit(solution)/shard_map/ppermute | solution.py:83
  7.1 4.6 %collective-permute-start.42 = (bf16[8,4096]{1,0:T(8,128)(2,1)}, bf16[8,4096]{1,0:T(8,128)(2,1)S(1)}, u32[]{:S(2)}, u32[]{:S(2)}) collective-permute-start(bf16[8,4096]{1,0:T(8,128)(2,1)} %x_ref.1), channel_id=1, source_target_pairs={{0,12},{2,14},{4,0},{6,2},{8,4},{10,6},{12,8},{14,10},{1,13},{3,15... | collective-permute-start | bytes 196616 | tf_op jit(solution)/shard_map/ppermute | solution.py:79
  9.6 12.5 %collective-permute-start.44 = (bf16[8,4096]{1,0:T(8,128)(2,1)S(1)}, bf16[8,4096]{1,0:T(8,128)(2,1)S(1)}, u32[]{:S(2)}, u32[]{:S(2)}) collective-permute-start(bf16[8,4096]{1,0:T(8,128)(2,1)S(1)} %collective-permute-done.41.refs_4_), channel_id=1, source_target_pairs={{0,2},{2,0},{4,6},{6,4},{8,10},{10,8},{12,14},{14,12},{1,3},{3,1},... | collective-permute-start | bytes 196616 | tf_op jit(solution)/shard_map/ppermute | solution.py:83
  11.7 10.5 %collective-permute-start.45 = (bf16[8,4096]{1,0:T(8,128)(2,1)S(1)}, bf16[8,4096]{1,0:T(8,128)(2,1)S(1)}, u32[]{:S(2)}, u32[]{:S(2)}) collective-permute-start(bf16[8,4096]{1,0:T(8,128)(2,1)S(1)} %collective-permute-done.42.refs_5_), channel_id=1, source_target_pairs={{0,2},{2,0},{4,6},{6,4},{8,10},{10,8},{12,14},{14,12},{1,3},{3,1},... | collective-permute-start | bytes 196616 | tf_op jit(solution)/shard_map/ppermute | solution.py:83
  12.9 4.3 %collective-permute-start.40 = (bf16[8,4096]{1,0:T(8,128)(2,1)S(1)}, bf16[8,4096]{1,0:T(8,128)(2,1)S(1)}, u32[]{:S(2)}, u32[]{:S(2)}) collective-permute-start(bf16[8,4096]{1,0:T(8,128)(2,1)S(1)} %collective-permute-done.39.refs_3_), channel_id=1, source_target_pairs={{0,2},{2,0},{4,6},{6,4},{8,10},{10,8},{12,14},{14,12},{1,3},{3,1},... | collective-permute-start | bytes 196616 | tf_op jit(solution)/shard_map/ppermute | solution.py:83
  28.3 8.8 %collective-permute-start.19 = (bf16[128,1024]{1,0:T(8,128)(2,1)S(1)}, bf16[128,1024]{1,0:T(8,128)(2,1)S(1)}, u32[]{:S(2)}, u32[]{:S(2)}) collective-permute-start(bf16[128,1024]{1,0:T(8,128)(2,1)S(1)} %get-tuple-element.188), channel_id=1, source_target_pairs={{0,2},{2,0},{4,6},{6,4},{8,10},{10,8},{12,14},{14,12},{1,3},{3,1},... | collective-permute-start | bytes 786440 | tf_op jit(solution)/shard_map/cond/branch_1_fun/ppermute | solution.py:592
  37.0 13.6 %collective-permute-start.20 = (bf16[64,4096]{1,0:T(8,128)(2,1)S(1)}, bf16[64,4096]{1,0:T(8,128)(2,1)S(1)}, u32[]{:S(2)}, u32[]{:S(2)}) collective-permute-start(bf16[64,4096]{1,0:T(8,128)(2,1)S(1)} %bitcast.19), channel_id=1, source_target_pairs={{0,2},{2,0},{4,6},{6,4},{8,10},{10,8},{12,14},{14,12},{1,3},{3,1},... | collective-permute-start | bytes 1572872 | tf_op jit(solution)/shard_map/cond/branch_1_fun/ppermute | solution.py:598
  37.9 12.8 %collective-permute-start.21 = (bf16[2,64,1024]{2,1,0:T(8,128)(2,1)S(1)}, bf16[2,64,1024]{2,1,0:T(8,128)(2,1)S(1)}, u32[]{:S(2)}, u32[]{:S(2)}) collective-permute-start(bf16[2,64,1024]{2,1,0:T(8,128)(2,1)S(1)} %branch_1_fun.11), channel_id=1, source_target_pairs={{0,1},{1,0},{2,3},{3,2},{4,5},{5,4},{6,7},{7,6},{8,9},{9,8},{10,11... | collective-permute-start | bytes 786440 | tf_op jit(solution)/shard_map/cond/branch_1_fun/ppermute | solution.py:549
  38.7 11.9 %collective-permute-start.22 = (bf16[48,1024]{1,0:T(8,128)(2,1)S(1)}, bf16[48,1024]{1,0:T(8,128)(2,1)S(1)}, u32[]{:S(2)}, u32[]{:S(2)}) collective-permute-start(bf16[48,1024]{1,0:T(8,128)(2,1)S(1)} %get-tuple-element.200), channel_id=1, source_target_pairs={{0,4},{2,6},{4,8},{6,10},{8,12},{10,14},{12,0},{14,2},{1,5},{3,7},... | collective-permute-start | bytes 294920 | tf_op jit(solution)/shard_map/cond/branch_1_fun/ppermute | solution.py:92
  39.3 11.3 %collective-permute-start.23 = (bf16[48,1024]{1,0:T(8,128)(2,1)S(1)}, bf16[48,1024]{1,0:T(8,128)(2,1)S(1)}, u32[]{:S(2)}, u32[]{:S(2)}) collective-permute-start(bf16[48,1024]{1,0:T(8,128)(2,1)S(1)} %get-tuple-element.201), channel_id=1, source_target_pairs={{0,8},{2,10},{4,12},{6,14},{8,0},{10,2},{12,4},{14,6},{1,9},{3,11}... | collective-permute-start | bytes 294920 | tf_op jit(solution)/shard_map/cond/branch_1_fun/ppermute | solution.py:92
  43.2 7.4 %collective-permute-start.24 = (bf16[48,1024]{1,0:T(8,128)(2,1)S(1)}, bf16[48,1024]{1,0:T(8,128)(2,1)S(1)}, u32[]{:S(2)}, u32[]{:S(2)}) collective-permute-start(bf16[48,1024]{1,0:T(8,128)(2,1)S(1)} %get-tuple-element.202), channel_id=1, source_target_pairs={{0,12},{2,14},{4,0},{6,2},{8,4},{10,6},{12,8},{14,10},{1,13},{3,15... | collective-permute-start | bytes 294920 | tf_op jit(solution)/shard_map/cond/branch_1_fun/ppermute | solution.py:92
  51.6 5.9 %collective-permute-start.26 = (bf16[64,1024]{1,0:T(8,128)(2,1)S(1)}, bf16[64,1024]{1,0:T(8,128)(2,1)S(1)}, u32[]{:S(2)}, u32[]{:S(2)}) collective-permute-start(bf16[64,1024]{1,0:T(8,128)(2,1)S(1)} %get-tuple-element.208), channel_id=1, source_target_pairs={{0,2},{2,0},{4,6},{6,4},{8,10},{10,8},{12,14},{14,12},{1,3},{3,1},... | collective-permute-start | bytes 393224 | tf_op jit(solution)/shard_map/cond/branch_1_fun/ppermute | solution.py:615
  57.5 10.1 %collective-permute-start.27 = (bf16[32,2048]{1,0:T(8,128)(2,1)S(1)}, bf16[32,2048]{1,0:T(8,128)(2,1)S(1)}, u32[]{:S(2)}, u32[]{:S(2)}) collective-permute-start(bf16[32,2048]{1,0:T(8,128)(2,1)S(1)} %get-tuple-element.217), channel_id=1, source_target_pairs={{0,2},{2,0},{4,6},{6,4},{8,10},{10,8},{12,14},{14,12},{1,3},{3,1},... | collective-permute-start | bytes 393224 | tf_op jit(solution)/shard_map/cond/branch_1_fun/ppermute | solution.py:618
  58.3 8.9 %collective-permute-start.28 = (bf16[32,1024]{1,0:T(8,128)(2,1)S(1)}, bf16[32,1024]{1,0:T(8,128)(2,1)S(1)}, u32[]{:S(2)}, u32[]{:S(2)}) collective-permute-start(bf16[32,1024]{1,0:T(8,128)(2,1)S(1)} %get-tuple-element.219), channel_id=1, source_target_pairs={{0,4},{2,6},{4,8},{6,10},{8,12},{10,14},{12,0},{14,2},{1,5},{3,7},... | collective-permute-start | bytes 196616 | tf_op jit(solution)/shard_map/cond/branch_1_fun/ppermute | solution.py:92
  60.8 6.5 %collective-permute-start.29 = (bf16[32,1024]{1,0:T(8,128)(2,1)S(1)}, bf16[32,1024]{1,0:T(8,128)(2,1)S(1)}, u32[]{:S(2)}, u32[]{:S(2)}) collective-permute-start(bf16[32,1024]{1,0:T(8,128)(2,1)S(1)} %get-tuple-element.220), channel_id=1, source_target_pairs={{0,8},{2,10},{4,12},{6,14},{8,0},{10,2},{12,4},{14,6},{1,9},{3,11}... | collective-permute-start | bytes 196616 | tf_op jit(solution)/shard_map/cond/branch_1_fun/ppermute | solution.py:92
  62.9 4.7 %collective-permute-start.30 = (bf16[32,1024]{1,0:T(8,128)(2,1)S(1)}, bf16[32,1024]{1,0:T(8,128)(2,1)S(1)}, u32[]{:S(2)}, u32[]{:S(2)}) collective-permute-start(bf16[32,1024]{1,0:T(8,128)(2,1)S(1)} %get-tuple-element.221), channel_id=1, source_target_pairs={{0,12},{2,14},{4,0},{6,2},{8,4},{10,6},{12,8},{14,10},{1,13},{3,15... | collective-permute-start | bytes 196616 | tf_op jit(solution)/shard_map/cond/branch_1_fun/ppermute | solution.py:92
  67.6 5.7 %collective-permute-start.31 = (bf16[32,2048]{1,0:T(8,128)(2,1)S(1)}, bf16[32,2048]{1,0:T(8,128)(2,1)S(1)}, u32[]{:S(2)}, u32[]{:S(2)}) collective-permute-start(bf16[32,2048]{1,0:T(8,128)(2,1)S(1)} %get-tuple-element.228), channel_id=1, source_target_pairs={{0,2},{2,0},{4,6},{6,4},{8,10},{10,8},{12,14},{14,12},{1,3},{3,1},... | collective-permute-start | bytes 393224 | tf_op jit(solution)/shard_map/cond/branch_1_fun/ppermute | solution.py:625
  69.6 3.7 %collective-permute-start.33 = (f32[16,64]{1,0:T(8,128)S(1)}, f32[16,64]{1,0:T(8,128)S(1)}, u32[]{:S(2)}, u32[]{:S(2)}) collective-permute-start(f32[16,64]{1,0:T(8,128)S(1)} %branch_1_fun.18.refs_4_), channel_id=1, source_target_pairs={{0,2},{2,0},{4,6},{6,4},{8,10},{10,8},{12,14},{14,12},{1,3},{3,1},... | collective-permute-start | bytes 12296 | tf_op jit(solution)/shard_map/cond/branch_1_fun/ppermute | solution.py:636
  73.8 6.8 %collective-permute-start.35 = (bf16[8,4096]{1,0:T(8,128)(2,1)S(1)}, bf16[8,4096]{1,0:T(8,128)(2,1)S(1)}, u32[]{:S(2)}, u32[]{:S(2)}) collective-permute-start(bf16[8,4096]{1,0:T(8,128)(2,1)S(1)} %get-tuple-element.237), channel_id=1, source_target_pairs={{0,4},{2,6},{4,8},{6,10},{8,12},{10,14},{12,0},{14,2},{1,5},{3,7},... | collective-permute-start | bytes 196616 | tf_op jit(solution)/shard_map/cond/branch_1_fun/ppermute | solution.py:92
  75.2 7.4 %collective-permute-start.36 = (bf16[8,4096]{1,0:T(8,128)(2,1)S(1)}, bf16[8,4096]{1,0:T(8,128)(2,1)S(1)}, u32[]{:S(2)}, u32[]{:S(2)}) collective-permute-start(bf16[8,4096]{1,0:T(8,128)(2,1)S(1)} %get-tuple-element.238), channel_id=1, source_target_pairs={{0,8},{2,10},{4,12},{6,14},{8,0},{10,2},{12,4},{14,6},{1,9},{3,11}... | collective-permute-start | bytes 196616 | tf_op jit(solution)/shard_map/cond/branch_1_fun/ppermute | solution.py:92
  76.9 5.8 %collective-permute-start.37 = (bf16[8,4096]{1,0:T(8,128)(2,1)S(1)}, bf16[8,4096]{1,0:T(8,128)(2,1)S(1)}, u32[]{:S(2)}, u32[]{:S(2)}) collective-permute-start(bf16[8,4096]{1,0:T(8,128)(2,1)S(1)} %get-tuple-element.239), channel_id=1, source_target_pairs={{0,12},{2,14},{4,0},{6,2},{8,4},{10,6},{12,8},{14,10},{1,13},{3,15... | collective-permute-start | bytes 196616 | tf_op jit(solution)/shard_map/cond/branch_1_fun/ppermute | solution.py:92
  (8 other events, 34.3 us)

commit v4 on v3

--- a/solution.py
+++ b/solution.py
@@ -132,14 +132,16 @@
     same = owner == owner_along
     place = across((same & (lane < line)).astype(F32))
     paired = ways.direct and ways.fast == 2
-    beside = jnp.zeros_like(place)
+    beside = pair = jnp.zeros_like(place)
     if paired:
         odd = across((owner == 2.0 * count((rows, shards), 1) + 1.0).astype(F32))
         beside = across((owner + 1.0 - 2.0 * odd == owner_along).astype(F32))
-    facts_ref[0] = jnp.max(place).astype(I32)
-    facts_ref[1] = jnp.max(across(same.astype(F32)) + beside).astype(I32)
-    facts_ref[2] = jnp.sum((owner == me).astype(F32)).astype(I32)
-    facts_ref[3] = jnp.sum((owner == order[ways.slow % shards]).astype(F32)).astype(I32)
+        pair = across(same.astype(F32)) + beside
+    facts_ref[0] = jnp.where(
+        (jnp.max(place) < USUAL) & (jnp.max(pair) <= USUAL_PAIR), 0, 1
+    )
+    facts_ref[1] = jnp.sum((owner == me).astype(F32)).astype(I32)
+    facts_ref[2] = jnp.sum((owner == order[ways.slow % shards]).astype(F32)).astype(I32)
     row_along, row_down = count((1, rows), 1), count((rows, 1), 0)
     at_along, at_down = row_along, row_down
     for b in range(shards):
@@ -187,7 +189,7 @@
             jax.ShapeDtypeStruct((8, rows), I32),
             jax.ShapeDtypeStruct((rows, slots * 2 * rank), F32),
             jax.ShapeDtypeStruct((rows, slots * rank), BF),
-            jax.ShapeDtypeStruct((4,), I32),
+            jax.ShapeDtypeStruct((3,), I32),
             jax.ShapeDtypeStruct(x.shape, BF),
             jax.ShapeDtypeStruct(shrink.shape, BF),
         ),
@@ -363,8 +365,8 @@
     column = column - jnp.where(from_got, 2 * cap, 0)
     kind = jnp.where(column >= cap, 1, 0)
     row = column - kind * cap
-    live = row < jnp.where(from_got, facts_ref[3], facts_ref[2])
-    row = row + jnp.where(from_got, facts_ref[2], 0)
+    live = row < jnp.where(from_got, facts_ref[2], facts_ref[1])
+    row = row + jnp.where(from_got, facts_ref[1], 0)
     room = out_refs[0].shape[0] // 2
     packing = one_hot(2 * room, jnp.where(live, row + kind * room, -1))
     for a, out_ref in enumerate(out_refs):
@@ -551,11 +553,6 @@
     near = expand_gu.reshape(slots * 2 * half_rank, -1)
     token_parts, far = ways.gather(tokens, swap(near))
     shrink_in = shrink_gu.reshape(slots * 2 * rank, width)
-    if ways.direct:
-        first_hop = ways.slow + 1
-        variant_ids, variant_slot, shrink_in, token_parts[first_hop] = tied(
-            variant_ids, variant_slot, shrink_in, token_parts[first_hop]
-        )
     marks, mask_in, slot_mask, facts, token_parts[0], shrink_in = tables(
         ways,
         me.reshape(1),
@@ -602,8 +599,6 @@
             delta = [delta.reshape(2 * shards * cap, half)]
         base_got = swap(base_there)
         base_own = base_half(here, held, gate_weight, up_weight, half, F32)
-        if split == 2:
-            base_own, expand_beside = tied(base_own, expand_beside)
         hidden, *sent = hidden_half(
             base_own, base_got, delta, marks, cap, room, shards, split
         )
@@ -614,7 +609,7 @@
         if split == 2:
             beside = lax.ppermute(sent[1], "ff", ways.back(0, 1))
             left, left_sent = down(0, side, (F32, BF))
-            left_sent, beside = tied(left_sent, beside)
+            left_sent, beside, expand_beside = tied(left_sent, beside, expand_beside)
             left_beside = lax.ppermute(left_sent, "ff", ways.back(0, 1))
             sent = relay(sent[0], beside, ways.slow)
             hidden, *sent = tied(hidden, *sent)
@@ -651,11 +646,8 @@
     if most <= USUAL:
         parts = partial_sums(most, most_room)
     else:
-        usual = most_facts[0] < USUAL
-        if split == 2:
-            usual = usual & (most_facts[1] <= USUAL_PAIR)
         parts = lax.cond(
-            usual,
+            most_facts[0] == 0,
             lambda: partial_sums(USUAL, USUAL_PAIR if split == 2 else USUAL),
             lambda: partial_sums(most, most_room),
         )

time: 83.8 us -> 78.4 us (0.936)
  waiting for transfers between devices: 15.7 us -> 10.7 us
  starting transfers between devices: 31.8 us -> 33.3 us
  between operations: 1.39 us -> 0.16 us
    ppermute x4, waiting for transfers between devices: 3.44 us -> 0.01 us  [gather(): lax.ppermute(part, 'ff', self.back(0, -c))]
    ppermute x1, waiting for transfers between devices: 1.07 us -> 0.01 us  [partial_sums(): expand_beside = lax.ppermute(expand, 'ff', ways.back(0, 1))]
    unnamed x8 -> x9, local copies, waits for them, and re-layouts: 1.5 us -> 2.24 us
  transfers between devices with their start and end apart: 28 -> 28, of which waited for: 11 -> 9; matrix products, arithmetic and copies ran while one was open for 2% -> 1% of each run, Pallas kernels for 30% -> 33%
where the time goes in v4:
time: 78.4 us; the launch traced here: 78.1 us
  starting transfers between devices  33.3 us (42%)
  Pallas kernels  30.4 us (39%)
  waiting for transfers between devices  10.7 us (14%)
  local copies, waits for them, and re-layouts  2.24 us (3%)
  other arithmetic  0.92 us (1%)
    ppermute x9, starting transfers between devices, slow_steps(): got[-a % self.slow] = lax.ppermute(blocks[a], 'ff', self.back(a, 0))  13.4 us
    pallas_call x2, Pallas kernels, base_half(): pl.pallas_call(base_kernel, out_shape=jax.ShapeDtypeStruct((2, rows, half...  12.5 us
    pallas_call x2, Pallas kernels, down_base(): pl.pallas_call(functools.partial(down_kernel, start), out_shape=outs, in_...  8.17 us
    ppermute x3, starting transfers between devices, gather(): lax.ppermute(block, 'ff', self.back(-a, 0))  7.41 us
    ppermute x9, waiting for transfers between devices, slow_steps(): got[-a % self.slow] = lax.ppermute(blocks[a], 'ff', self.back(a, 0))  5.62 us
    ppermute x4, starting transfers between devices, gather(): lax.ppermute(part, 'ff', self.back(0, -c))  4.12 us
    pallas_call x1, Pallas kernels, expand_rows(): pl.pallas_call(functools.partial(expand_kernel, cap, fast), out_shape=(ou...  2.87 us
    pallas_call x1, Pallas kernels, tables(): pl.pallas_call(functools.partial(tables_kernel, ways, slots), out_shape=(...  2.7 us
  transfers between devices with their start and end apart: 28, of which 9 were waited for; matrix products, arithmetic and copies ran while one was open for 1% of the time, Pallas kernels for 33%

profile of v4, /device:TPU:0, one launch (start us, length us, event | category | flops | bytes accessed | tf_op | source)
XLA Modules:
  0.0 78.1 jit_solution(7985009502828630316)
XLA Ops:
  0.5 3.6 %collective-permute-start.40 = (bf16[8,4096]{1,0:T(8,128)(2,1)}, bf16[8,4096]{1,0:T(8,128)(2,1)S(1)}, u32[]{:S(2)}, u32[]{:S(2)}) collective-permute-start(bf16[8,4096]{1,0:T(8,128)(2,1)} %x_ref.1), channel_id=1, source_target_pairs={{0,8},{2,10},{4,12},{6,14},{8,0},{10,2},{12,4},{14,6},{1,9},{3,11}... | collective-permute-start | bytes 196616 | tf_op jit(solution)/shard_map/ppermute | solution.py:79
  4.0 1.6 %collective-permute-start.39 = (bf16[8,4096]{1,0:T(8,128)(2,1)}, bf16[8,4096]{1,0:T(8,128)(2,1)S(1)}, u32[]{:S(2)}, u32[]{:S(2)}) collective-permute-start(bf16[8,4096]{1,0:T(8,128)(2,1)} %x_ref.1), channel_id=1, source_target_pairs={{0,4},{2,6},{4,8},{6,10},{8,12},{10,14},{12,0},{14,2},{1,5},{3,7},... | collective-permute-start | bytes 196616 | tf_op jit(solution)/shard_map/ppermute | solution.py:79
  5.6 1.5 %collective-permute-start.42 = (bf16[8,4096]{1,0:T(8,128)(2,1)}, bf16[8,4096]{1,0:T(8,128)(2,1)S(1)}, u32[]{:S(2)}, u32[]{:S(2)}) collective-permute-start(bf16[8,4096]{1,0:T(8,128)(2,1)} %x_ref.1), channel_id=1, source_target_pairs={{0,2},{2,0},{4,6},{6,4},{8,10},{10,8},{12,14},{14,12},{1,3},{3,1},... | collective-permute-start | bytes 196616 | tf_op jit(solution)/shard_map/ppermute | solution.py:83
  7.1 2.2 %collective-permute-start.41 = (bf16[8,4096]{1,0:T(8,128)(2,1)}, bf16[8,4096]{1,0:T(8,128)(2,1)S(1)}, u32[]{:S(2)}, u32[]{:S(2)}) collective-permute-start(bf16[8,4096]{1,0:T(8,128)(2,1)} %x_ref.1), channel_id=1, source_target_pairs={{0,12},{2,14},{4,0},{6,2},{8,4},{10,6},{12,8},{14,10},{1,13},{3,15... | collective-permute-start | bytes 196616 | tf_op jit(solution)/shard_map/ppermute | solution.py:79
  15.3 2.7 %shard_map.100 = (s32[8,64]{1,0:T(8,128)S(1)}, f32[64,128]{1,0:T(8,128)S(1)}, bf16[64,64]{1,0:T(8,128)(2,1)S(1)}, s32[3]{0:T(128)S(1)}, bf16[8,4096]{1,0:T(8,128)(2,1)S(1)}, /*index=5*/bf16[128,4096]{1,0:T(8,128)(2,1)S(1)}) custom-call(s32[8]{0:T(128)S(1)} %fusion.order_ref, s32[1]{0:T(128)} %bitcast.6.me_ref, s32[64,1]{1,0:T(8,128)S(1)} %copy.11.ids_ref, ...), custom_call_target="tpu_custom_call" | custom-call | bytes 2228224 | tf_op jit(solution)/shard_map/pallas_call | solution.py:186
  20.3 57.1 %conditional.3 = (bf16[8,4096]{1,0:T(8,128)(2,1)S(1)}, f32[8,4096]{1,0:T(8,128)S(1)}, f32[8,4096]{1,0:T(8,128)S(1)}, f32[8,4096]{1,0:T(8,128)S(1)}) conditional(s32[]{:T(128)} %bitcast.9, (s32[]{:T(128)}, s32[8]{0:T(128)S(1)}, s32[8]{0:T(128)S(1)}, f32[64,128]{1,0:T(8,128)S(1)}, f32[64,128]{1,0:T(8,128)S(1)}, /*index=5*/s32[8,64]{1,0:T(8,128)S(1)}, ...), branch_computations={%region_0.1_spmd, %region_1.2_spmd} | conditional | flops 3724640256 | bytes 92963768
  20.3 2.9 %branch_1_fun.10 = (bf16[128,1024]{1,0:T(8,128)(2,1)S(1)}, bf16[128,1024]{1,0:T(8,128)(2,1)S(1)}) custom-call(s32[8]{0:T(128)S(1)} %multiply_add_fusion.1.at_ref, f32[64,128]{1,0:T(8,128)S(1)} %get-tuple-element.174.own_ref, f32[64,128]{1,0:T(8,128)S(1)} %get-tuple-element.175.got_ref, s32[8,64]{1,0:T(8,128)S(1)} %get-tuple-element.176.marks_ref.refs_8_, ...), custom_call_target="tpu_custom_call" | custom-call | flops 134217728 | bytes 5242880 | tf_op jit(solution)/shard_map/cond/branch_1_fun/pallas_call | solution.py:272
  23.2 1.3 %collective-permute-start.19 = (bf16[128,1024]{1,0:T(8,128)(2,1)S(1)}, bf16[128,1024]{1,0:T(8,128)(2,1)S(1)}, u32[]{:S(2)}, u32[]{:S(2)}) collective-permute-start(bf16[128,1024]{1,0:T(8,128)(2,1)S(1)} %get-tuple-element.187), channel_id=1, source_target_pairs={{0,2},{2,0},{4,6},{6,4},{8,10},{10,8},{12,14},{14,12},{1,3},{3,1},... | collective-permute-start | bytes 786440 | tf_op jit(solution)/shard_map/cond/branch_1_fun/ppermute | solution.py:589
  24.5 6.3 %branch_1_fun.11 = bf16[2,64,1024]{2,1,0:T(8,128)(2,1)S(1)} custom-call(s32[1]{0:T(128)S(6)} %sub.32.side_ref, bf16[64,4096]{1,0:T(8,128)(2,1)S(1)} %get-tuple-element.194.x_ref, bf16[4096,2048]{1,0:T(8,128)(2,1)} %get-tuple-element.185.gate_ref, bf16[4096,2048]{1,0:T(8,128)(2,1)} %get-tuple-element.186.up_ref), custom_call_target="tpu_custom_call" | custom-call | flops 1073741824 | bytes 17301504 | tf_op jit(solution)/shard_map/cond/branch_1_fun/pallas_call | solution.py:309
  31.7 1.2 %collective-permute-start.26 = (bf16[64,4096]{1,0:T(8,128)(2,1)S(1)}, bf16[64,4096]{1,0:T(8,128)(2,1)S(1)}, u32[]{:S(2)}, u32[]{:S(2)}) collective-permute-start(bf16[64,4096]{1,0:T(8,128)(2,1)S(1)} %bitcast.20), channel_id=1, source_target_pairs={{0,2},{2,0},{4,6},{6,4},{8,10},{10,8},{12,14},{14,12},{1,3},{3,1},... | collective-permute-start | bytes 1572872 | tf_op jit(solution)/shard_map/cond/branch_1_fun/ppermute | solution.py:595
  34.2 3.5 %collective-permute-start.22 = (bf16[48,1024]{1,0:T(8,128)(2,1)S(1)}, bf16[48,1024]{1,0:T(8,128)(2,1)S(1)}, u32[]{:S(2)}, u32[]{:S(2)}) collective-permute-start(bf16[48,1024]{1,0:T(8,128)(2,1)S(1)} %get-tuple-element.198), channel_id=1, source_target_pairs={{0,8},{2,10},{4,12},{6,14},{8,0},{10,2},{12,4},{14,6},{1,9},{3,11}... | collective-permute-start | bytes 294920 | tf_op jit(solution)/shard_map/cond/branch_1_fun/ppermute | solution.py:92
  37.6 6.2 %branch_1_fun.13.own_ref = f32[2,64,1024]{2,1,0:T(8,128)S(1)} custom-call(s32[1]{0:T(128)} %bitcast.3.side_ref.core_ref, bf16[64,4096]{1,0:T(8,128)(2,1)S(1)} %get-tuple-element.194.x_ref, bf16[4096,2048]{1,0:T(8,128)(2,1)} %get-tuple-element.185.gate_ref, bf16[4096,2048]{1,0:T(8,128)(2,1)} %get-tuple-element.186.up_ref), custom_call_target="tpu_custom_call" | custom-call | flops 1073741824 | bytes 17301504 | tf_op jit(solution)/shard_map/cond/branch_1_fun/pallas_call | solution.py:309
  46.0 1.3 %collective-permute-start.25 = (bf16[64,1024]{1,0:T(8,128)(2,1)S(1)}, bf16[64,1024]{1,0:T(8,128)(2,1)S(1)}, u32[]{:S(2)}, u32[]{:S(2)}) collective-permute-start(bf16[64,1024]{1,0:T(8,128)(2,1)S(1)} %get-tuple-element.205), channel_id=1, source_target_pairs={{0,2},{2,0},{4,6},{6,4},{8,10},{10,8},{12,14},{14,12},{1,3},{3,1},... | collective-permute-start | bytes 393224 | tf_op jit(solution)/shard_map/cond/branch_1_fun/ppermute | solution.py:610
  47.3 4.2 %branch_1_fun.15 = (f32[32,2048]{1,0:T(8,128)S(1)}, bf16[32,2048]{1,0:T(8,128)(2,1)S(1)}) custom-call(s32[1]{0:T(128)} %bitcast.3.side_ref.core_ref, bf16[64,1024]{1,0:T(8,128)(2,1)S(1)} %get-tuple-element.212.near_ref, bf16[64,1024]{1,0:T(8,128)(2,1)S(1)} %collective-permute-done.24.far_ref, bf16[2048,4096]{1,0:T(8,128)(2,1)} %get-tuple-element.201.weight_ref), custom_call_target="tpu_custom_call" | custom-call | flops 536870912 | bytes 8912896 | tf_op jit(solution)/shard_map/cond/branch_1_fun/pallas_call | solution.py:438
  51.9 1.2 %collective-permute-start.27 = (bf16[32,2048]{1,0:T(8,128)(2,1)S(1)}, bf16[32,2048]{1,0:T(8,128)(2,1)S(1)}, u32[]{:S(2)}, u32[]{:S(2)}) collective-permute-start(bf16[32,2048]{1,0:T(8,128)(2,1)S(1)} %get-tuple-element.215), channel_id=1, source_target_pairs={{0,2},{2,0},{4,6},{6,4},{8,10},{10,8},{12,14},{14,12},{1,3},{3,1},... | collective-permute-start | bytes 393224 | tf_op jit(solution)/shard_map/cond/branch_1_fun/ppermute | solution.py:613
  53.1 2.7 %collective-permute-start.28 = (bf16[32,1024]{1,0:T(8,128)(2,1)S(1)}, bf16[32,1024]{1,0:T(8,128)(2,1)S(1)}, u32[]{:S(2)}, u32[]{:S(2)}) collective-permute-start(bf16[32,1024]{1,0:T(8,128)(2,1)S(1)} %get-tuple-element.217), channel_id=1, source_target_pairs={{0,4},{2,6},{4,8},{6,10},{8,12},{10,14},{12,0},{14,2},{1,5},{3,7},... | collective-permute-start | bytes 196616 | tf_op jit(solution)/shard_map/cond/branch_1_fun/ppermute | solution.py:92
  56.4 1.8 %collective-permute-start.30 = (bf16[32,1024]{1,0:T(8,128)(2,1)S(1)}, bf16[32,1024]{1,0:T(8,128)(2,1)S(1)}, u32[]{:S(2)}, u32[]{:S(2)}) collective-permute-start(bf16[32,1024]{1,0:T(8,128)(2,1)S(1)} %get-tuple-element.219), channel_id=1, source_target_pairs={{0,12},{2,14},{4,0},{6,2},{8,4},{10,6},{12,8},{14,10},{1,13},{3,15... | collective-permute-start | bytes 196616 | tf_op jit(solution)/shard_map/cond/branch_1_fun/ppermute | solution.py:92
  58.2 4.0 %branch_1_fun.17 = (f32[32,2048]{1,0:T(8,128)S(1)}, bf16[32,2048]{1,0:T(8,128)(2,1)S(1)}) custom-call(s32[1]{0:T(128)} %bitcast.3.side_ref.core_ref, bf16[64,1024]{1,0:T(8,128)(2,1)S(1)} %get-tuple-element.212.near_ref, bf16[64,1024]{1,0:T(8,128)(2,1)S(1)} %collective-permute-done.24.far_ref, bf16[2048,4096]{1,0:T(8,128)(2,1)} %get-tuple-element.201.weight_ref), custom_call_target="tpu_custom_call" | custom-call | flops 536870912 | bytes 8912896 | tf_op jit(solution)/shard_map/cond/branch_1_fun/pallas_call | solution.py:438
  64.1 1.3 %collective-permute-start.33 = (f32[16,64]{1,0:T(8,128)S(1)}, f32[16,64]{1,0:T(8,128)S(1)}, u32[]{:S(2)}, u32[]{:S(2)}) collective-permute-start(f32[16,64]{1,0:T(8,128)S(1)} %branch_1_fun.18.refs_4_), channel_id=1, source_target_pairs={{0,2},{2,0},{4,6},{6,4},{8,10},{10,8},{12,14},{14,12},{1,3},{3,1},... | collective-permute-start | bytes 12296 | tf_op jit(solution)/shard_map/cond/branch_1_fun/ppermute | solution.py:631
  66.0 1.3 %collective-permute-done.34.refs_7_ = f32[16,64]{1,0:T(8,128)S(1)} collective-permute-done((f32[16,64]{1,0:T(8,128)S(1)}, f32[16,64]{1,0:T(8,128)S(1)}, u32[]{:S(2)}, u32[]{:S(2)}) %collective-permute-start.34) | collective-permute-done | bytes 4128 | tf_op jit(solution)/shard_map/cond/branch_1_fun/ppermute | solution.py:635
  68.3 1.9 %collective-permute-start.35 = (bf16[8,4096]{1,0:T(8,128)(2,1)S(1)}, bf16[8,4096]{1,0:T(8,128)(2,1)S(1)}, u32[]{:S(2)}, u32[]{:S(2)}) collective-permute-start(bf16[8,4096]{1,0:T(8,128)(2,1)S(1)} %get-tuple-element.235), channel_id=1, source_target_pairs={{0,4},{2,6},{4,8},{6,10},{8,12},{10,14},{12,0},{14,2},{1,5},{3,7},... | collective-permute-start | bytes 196616 | tf_op jit(solution)/shard_map/cond/branch_1_fun/ppermute | solution.py:92
  71.2 1.5 %collective-permute-start.37 = (bf16[8,4096]{1,0:T(8,128)(2,1)S(1)}, bf16[8,4096]{1,0:T(8,128)(2,1)S(1)}, u32[]{:S(2)}, u32[]{:S(2)}) collective-permute-start(bf16[8,4096]{1,0:T(8,128)(2,1)S(1)} %get-tuple-element.237), channel_id=1, source_target_pairs={{0,12},{2,14},{4,0},{6,2},{8,4},{10,6},{12,8},{14,10},{1,13},{3,15... | collective-permute-start | bytes 196616 | tf_op jit(solution)/shard_map/cond/branch_1_fun/ppermute | solution.py:92
  72.7 2.5 %collective-permute-done.35 = bf16[8,4096]{1,0:T(8,128)(2,1)S(1)} collective-permute-done((bf16[8,4096]{1,0:T(8,128)(2,1)S(1)}, bf16[8,4096]{1,0:T(8,128)(2,1)S(1)}, u32[]{:S(2)}, u32[]{:S(2)}) %collective-permute-start.35) | collective-permute-done | bytes 65568 | tf_op jit(solution)/shard_map/cond/branch_1_fun/ppermute | solution.py:92
  75.2 2.1 %collective-permute-done.36 = bf16[8,4096]{1,0:T(8,128)(2,1)S(1)} collective-permute-done((bf16[8,4096]{1,0:T(8,128)(2,1)S(1)}, bf16[8,4096]{1,0:T(8,128)(2,1)S(1)}, u32[]{:S(2)}, u32[]{:S(2)}) %collective-permute-start.36) | collective-permute-done | bytes 65568 | tf_op jit(solution)/shard_map/cond/branch_1_fun/ppermute | solution.py:92
  (66 shorter events, 19.0 us)
Async XLA Ops:
  0.0 12.9 %collective-permute-start.38 = (bf16[64,16384]{1,0:T(8,128)(2,1)}, bf16[64,16384]{1,0:T(8,128)(2,1)S(1)}, u32[]{:S(2)}, u32[]{:S(2)}) collective-permute-start(bf16[64,16384]{1,0:T(8,128)(2,1)} %bitcast.15), channel_id=1, source_target_pairs={{0,1},{1,0},{2,3},{3,2},{4,5},{5,4},{6,7},{7,6},{8,9},{9,8},{10,11... | collective-permute-start | bytes 6291464 | tf_op jit(solution)/shard_map/ppermute | solution.py:551
  0.5 9.8 %collective-permute-start.40 = (bf16[8,4096]{1,0:T(8,128)(2,1)}, bf16[8,4096]{1,0:T(8,128)(2,1)S(1)}, u32[]{:S(2)}, u32[]{:S(2)}) collective-permute-start(bf16[8,4096]{1,0:T(8,128)(2,1)} %x_ref.1), channel_id=1, source_target_pairs={{0,8},{2,10},{4,12},{6,14},{8,0},{10,2},{12,4},{14,6},{1,9},{3,11}... | collective-permute-start | bytes 196616 | tf_op jit(solution)/shard_map/ppermute | solution.py:79
  4.0 8.9 %collective-permute-start.39 = (bf16[8,4096]{1,0:T(8,128)(2,1)}, bf16[8,4096]{1,0:T(8,128)(2,1)S(1)}, u32[]{:S(2)}, u32[]{:S(2)}) collective-permute-start(bf16[8,4096]{1,0:T(8,128)(2,1)} %x_ref.1), channel_id=1, source_target_pairs={{0,4},{2,6},{4,8},{6,10},{8,12},{10,14},{12,0},{14,2},{1,5},{3,7},... | collective-permute-start | bytes 196616 | tf_op jit(solution)/shard_map/ppermute | solution.py:79
  5.6 12.4 %collective-permute-start.42 = (bf16[8,4096]{1,0:T(8,128)(2,1)}, bf16[8,4096]{1,0:T(8,128)(2,1)S(1)}, u32[]{:S(2)}, u32[]{:S(2)}) collective-permute-start(bf16[8,4096]{1,0:T(8,128)(2,1)} %x_ref.1), channel_id=1, source_target_pairs={{0,2},{2,0},{4,6},{6,4},{8,10},{10,8},{12,14},{14,12},{1,3},{3,1},... | collective-permute-start | bytes 196616 | tf_op jit(solution)/shard_map/ppermute | solution.py:83
  7.1 4.6 %collective-permute-start.41 = (bf16[8,4096]{1,0:T(8,128)(2,1)}, bf16[8,4096]{1,0:T(8,128)(2,1)S(1)}, u32[]{:S(2)}, u32[]{:S(2)}) collective-permute-start(bf16[8,4096]{1,0:T(8,128)(2,1)} %x_ref.1), channel_id=1, source_target_pairs={{0,12},{2,14},{4,0},{6,2},{8,4},{10,6},{12,8},{14,10},{1,13},{3,15... | collective-permute-start | bytes 196616 | tf_op jit(solution)/shard_map/ppermute | solution.py:79
  10.3 7.7 %collective-permute-start.44 = (bf16[8,4096]{1,0:T(8,128)(2,1)S(1)}, bf16[8,4096]{1,0:T(8,128)(2,1)S(1)}, u32[]{:S(2)}, u32[]{:S(2)}) collective-permute-start(bf16[8,4096]{1,0:T(8,128)(2,1)S(1)} %collective-permute-done.40.refs_4_), channel_id=1, source_target_pairs={{0,2},{2,0},{4,6},{6,4},{8,10},{10,8},{12,14},{14,12},{1,3},{3,1},... | collective-permute-start | bytes 196616 | tf_op jit(solution)/shard_map/ppermute | solution.py:83
  11.7 6.3 %collective-permute-start.45 = (bf16[8,4096]{1,0:T(8,128)(2,1)S(1)}, bf16[8,4096]{1,0:T(8,128)(2,1)S(1)}, u32[]{:S(2)}, u32[]{:S(2)}) collective-permute-start(bf16[8,4096]{1,0:T(8,128)(2,1)S(1)} %collective-permute-done.41.refs_5_), channel_id=1, source_target_pairs={{0,2},{2,0},{4,6},{6,4},{8,10},{10,8},{12,14},{14,12},{1,3},{3,1},... | collective-permute-start | bytes 196616 | tf_op jit(solution)/shard_map/ppermute | solution.py:83
  12.9 5.1 %collective-permute-start.43 = (bf16[8,4096]{1,0:T(8,128)(2,1)S(1)}, bf16[8,4096]{1,0:T(8,128)(2,1)S(1)}, u32[]{:S(2)}, u32[]{:S(2)}) collective-permute-start(bf16[8,4096]{1,0:T(8,128)(2,1)S(1)} %collective-permute-done.39.refs_3_), channel_id=1, source_target_pairs={{0,2},{2,0},{4,6},{6,4},{8,10},{10,8},{12,14},{14,12},{1,3},{3,1},... | collective-permute-start | bytes 196616 | tf_op jit(solution)/shard_map/ppermute | solution.py:83
  23.2 8.4 %collective-permute-start.19 = (bf16[128,1024]{1,0:T(8,128)(2,1)S(1)}, bf16[128,1024]{1,0:T(8,128)(2,1)S(1)}, u32[]{:S(2)}, u32[]{:S(2)}) collective-permute-start(bf16[128,1024]{1,0:T(8,128)(2,1)S(1)} %get-tuple-element.187), channel_id=1, source_target_pairs={{0,2},{2,0},{4,6},{6,4},{8,10},{10,8},{12,14},{14,12},{1,3},{3,1},... | collective-permute-start | bytes 786440 | tf_op jit(solution)/shard_map/cond/branch_1_fun/ppermute | solution.py:589
  31.7 20.2 %collective-permute-start.26 = (bf16[64,4096]{1,0:T(8,128)(2,1)S(1)}, bf16[64,4096]{1,0:T(8,128)(2,1)S(1)}, u32[]{:S(2)}, u32[]{:S(2)}) collective-permute-start(bf16[64,4096]{1,0:T(8,128)(2,1)S(1)} %bitcast.20), channel_id=1, source_target_pairs={{0,2},{2,0},{4,6},{6,4},{8,10},{10,8},{12,14},{14,12},{1,3},{3,1},... | collective-permute-start | bytes 1572872 | tf_op jit(solution)/shard_map/cond/branch_1_fun/ppermute | solution.py:595
  32.9 12.1 %collective-permute-start.20 = (bf16[2,64,1024]{2,1,0:T(8,128)(2,1)S(1)}, bf16[2,64,1024]{2,1,0:T(8,128)(2,1)S(1)}, u32[]{:S(2)}, u32[]{:S(2)}) collective-permute-start(bf16[2,64,1024]{2,1,0:T(8,128)(2,1)S(1)} %branch_1_fun.11), channel_id=1, source_target_pairs={{0,1},{1,0},{2,3},{3,2},{4,5},{5,4},{6,7},{7,6},{8,9},{9,8},{10,11... | collective-permute-start | bytes 786440 | tf_op jit(solution)/shard_map/cond/branch_1_fun/ppermute | solution.py:551
  33.7 10.2 %collective-permute-start.21 = (bf16[48,1024]{1,0:T(8,128)(2,1)S(1)}, bf16[48,1024]{1,0:T(8,128)(2,1)S(1)}, u32[]{:S(2)}, u32[]{:S(2)}) collective-permute-start(bf16[48,1024]{1,0:T(8,128)(2,1)S(1)} %get-tuple-element.197), channel_id=1, source_target_pairs={{0,4},{2,6},{4,8},{6,10},{8,12},{10,14},{12,0},{14,2},{1,5},{3,7},... | collective-permute-start | bytes 294920 | tf_op jit(solution)/shard_map/cond/branch_1_fun/ppermute | solution.py:92
  34.2 10.8 %collective-permute-start.22 = (bf16[48,1024]{1,0:T(8,128)(2,1)S(1)}, bf16[48,1024]{1,0:T(8,128)(2,1)S(1)}, u32[]{:S(2)}, u32[]{:S(2)}) collective-permute-start(bf16[48,1024]{1,0:T(8,128)(2,1)S(1)} %get-tuple-element.198), channel_id=1, source_target_pairs={{0,8},{2,10},{4,12},{6,14},{8,0},{10,2},{12,4},{14,6},{1,9},{3,11}... | collective-permute-start | bytes 294920 | tf_op jit(solution)/shard_map/cond/branch_1_fun/ppermute | solution.py:92
  37.6 7.4 %collective-permute-start.23 = (bf16[48,1024]{1,0:T(8,128)(2,1)S(1)}, bf16[48,1024]{1,0:T(8,128)(2,1)S(1)}, u32[]{:S(2)}, u32[]{:S(2)}) collective-permute-start(bf16[48,1024]{1,0:T(8,128)(2,1)S(1)} %get-tuple-element.199), channel_id=1, source_target_pairs={{0,12},{2,14},{4,0},{6,2},{8,4},{10,6},{12,8},{14,10},{1,13},{3,15... | collective-permute-start | bytes 294920 | tf_op jit(solution)/shard_map/cond/branch_1_fun/ppermute | solution.py:92
  46.0 5.9 %collective-permute-start.25 = (bf16[64,1024]{1,0:T(8,128)(2,1)S(1)}, bf16[64,1024]{1,0:T(8,128)(2,1)S(1)}, u32[]{:S(2)}, u32[]{:S(2)}) collective-permute-start(bf16[64,1024]{1,0:T(8,128)(2,1)S(1)} %get-tuple-element.205), channel_id=1, source_target_pairs={{0,2},{2,0},{4,6},{6,4},{8,10},{10,8},{12,14},{14,12},{1,3},{3,1},... | collective-permute-start | bytes 393224 | tf_op jit(solution)/shard_map/cond/branch_1_fun/ppermute | solution.py:610
  51.9 10.4 %collective-permute-start.27 = (bf16[32,2048]{1,0:T(8,128)(2,1)S(1)}, bf16[32,2048]{1,0:T(8,128)(2,1)S(1)}, u32[]{:S(2)}, u32[]{:S(2)}) collective-permute-start(bf16[32,2048]{1,0:T(8,128)(2,1)S(1)} %get-tuple-element.215), channel_id=1, source_target_pairs={{0,2},{2,0},{4,6},{6,4},{8,10},{10,8},{12,14},{14,12},{1,3},{3,1},... | collective-permute-start | bytes 393224 | tf_op jit(solution)/shard_map/cond/branch_1_fun/ppermute | solution.py:613
  53.1 9.1 %collective-permute-start.28 = (bf16[32,1024]{1,0:T(8,128)(2,1)S(1)}, bf16[32,1024]{1,0:T(8,128)(2,1)S(1)}, u32[]{:S(2)}, u32[]{:S(2)}) collective-permute-start(bf16[32,1024]{1,0:T(8,128)(2,1)S(1)} %get-tuple-element.217), channel_id=1, source_target_pairs={{0,4},{2,6},{4,8},{6,10},{8,12},{10,14},{12,0},{14,2},{1,5},{3,7},... | collective-permute-start | bytes 196616 | tf_op jit(solution)/shard_map/cond/branch_1_fun/ppermute | solution.py:92
  55.8 6.5 %collective-permute-start.29 = (bf16[32,1024]{1,0:T(8,128)(2,1)S(1)}, bf16[32,1024]{1,0:T(8,128)(2,1)S(1)}, u32[]{:S(2)}, u32[]{:S(2)}) collective-permute-start(bf16[32,1024]{1,0:T(8,128)(2,1)S(1)} %get-tuple-element.218), channel_id=1, source_target_pairs={{0,8},{2,10},{4,12},{6,14},{8,0},{10,2},{12,4},{14,6},{1,9},{3,11}... | collective-permute-start | bytes 196616 | tf_op jit(solution)/shard_map/cond/branch_1_fun/ppermute | solution.py:92
  56.4 5.8 %collective-permute-start.30 = (bf16[32,1024]{1,0:T(8,128)(2,1)S(1)}, bf16[32,1024]{1,0:T(8,128)(2,1)S(1)}, u32[]{:S(2)}, u32[]{:S(2)}) collective-permute-start(bf16[32,1024]{1,0:T(8,128)(2,1)S(1)} %get-tuple-element.219), channel_id=1, source_target_pairs={{0,12},{2,14},{4,0},{6,2},{8,4},{10,6},{12,8},{14,10},{1,13},{3,15... | collective-permute-start | bytes 196616 | tf_op jit(solution)/shard_map/cond/branch_1_fun/ppermute | solution.py:92
  62.3 5.5 %collective-permute-start.31 = (bf16[32,2048]{1,0:T(8,128)(2,1)S(1)}, bf16[32,2048]{1,0:T(8,128)(2,1)S(1)}, u32[]{:S(2)}, u32[]{:S(2)}) collective-permute-start(bf16[32,2048]{1,0:T(8,128)(2,1)S(1)} %get-tuple-element.226), channel_id=1, source_target_pairs={{0,2},{2,0},{4,6},{6,4},{8,10},{10,8},{12,14},{14,12},{1,3},{3,1},... | collective-permute-start | bytes 393224 | tf_op jit(solution)/shard_map/cond/branch_1_fun/ppermute | solution.py:620
  64.1 3.7 %collective-permute-start.33 = (f32[16,64]{1,0:T(8,128)S(1)}, f32[16,64]{1,0:T(8,128)S(1)}, u32[]{:S(2)}, u32[]{:S(2)}) collective-permute-start(f32[16,64]{1,0:T(8,128)S(1)} %branch_1_fun.18.refs_4_), channel_id=1, source_target_pairs={{0,2},{2,0},{4,6},{6,4},{8,10},{10,8},{12,14},{14,12},{1,3},{3,1},... | collective-permute-start | bytes 12296 | tf_op jit(solution)/shard_map/cond/branch_1_fun/ppermute | solution.py:631
  68.3 6.8 %collective-permute-start.35 = (bf16[8,4096]{1,0:T(8,128)(2,1)S(1)}, bf16[8,4096]{1,0:T(8,128)(2,1)S(1)}, u32[]{:S(2)}, u32[]{:S(2)}) collective-permute-start(bf16[8,4096]{1,0:T(8,128)(2,1)S(1)} %get-tuple-element.235), channel_id=1, source_target_pairs={{0,4},{2,6},{4,8},{6,10},{8,12},{10,14},{12,0},{14,2},{1,5},{3,7},... | collective-permute-start | bytes 196616 | tf_op jit(solution)/shard_map/cond/branch_1_fun/ppermute | solution.py:92
  70.2 7.0 %collective-permute-start.36 = (bf16[8,4096]{1,0:T(8,128)(2,1)S(1)}, bf16[8,4096]{1,0:T(8,128)(2,1)S(1)}, u32[]{:S(2)}, u32[]{:S(2)}) collective-permute-start(bf16[8,4096]{1,0:T(8,128)(2,1)S(1)} %get-tuple-element.236), channel_id=1, source_target_pairs={{0,8},{2,10},{4,12},{6,14},{8,0},{10,2},{12,4},{14,6},{1,9},{3,11}... | collective-permute-start | bytes 196616 | tf_op jit(solution)/shard_map/cond/branch_1_fun/ppermute | solution.py:92
  71.2 6.0 %collective-permute-start.37 = (bf16[8,4096]{1,0:T(8,128)(2,1)S(1)}, bf16[8,4096]{1,0:T(8,128)(2,1)S(1)}, u32[]{:S(2)}, u32[]{:S(2)}) collective-permute-start(bf16[8,4096]{1,0:T(8,128)(2,1)S(1)} %get-tuple-element.237), channel_id=1, source_target_pairs={{0,12},{2,14},{4,0},{6,2},{8,4},{10,6},{12,8},{14,10},{1,13},{3,15... | collective-permute-start | bytes 196616 | tf_op jit(solution)/shard_map/cond/branch_1_fun/ppermute | solution.py:92
  (8 other events, 32.9 us)

commit v5 on v4

--- a/solution.py
+++ b/solution.py
@@ -98,72 +98,83 @@
     slots,
     order_ref,
     me_ref,
+    at_ref,
+    slot_ref,
     ids_ref,
-    slot_ref,
     x_ref,
     shrink_ref,
+    expand_ref,
     marks_ref,
     in_ref,
     out_ref,
     facts_ref,
     kept_ref,
     held_ref,
+    near_ref,
     sems,
 ):
+    shards = order_ref.shape[0]
+    half = near_ref.shape[1] // shards
     copies = [
         pltpu.make_async_copy(x_ref, kept_ref, sems.at[0]),
         pltpu.make_async_copy(shrink_ref, held_ref, sems.at[1]),
     ]
+    for b in range(shards):
+        columns = pl.ds(pl.multiple_of(at_ref[b] * half, half), half)
+        put = near_ref.at[:, pl.ds(b * half, half)]
+        copies.append(pltpu.make_async_copy(expand_ref.at[:, columns], put, sems.at[2 + b]))
     for copy in copies:
         copy.start()
-    rows, variants = ids_ref.shape[0], slot_ref.shape[1]
-    shards = order_ref.shape[0]
+    rows, variants = ids_ref.shape[1], slot_ref.shape[0]
     own_rows = rows // shards
     me = me_ref[0].astype(F32)
     order = [order_ref[b].astype(F32) for b in range(shards)]
+    beside_me = order[ways.slow % shards]
     count = lambda shape, axis: lax.broadcasted_iota(I32, shape, axis).astype(F32)
     across = lambda a: jnp.sum(a, axis=1, keepdims=True)
     along = lambda a: jnp.sum(a, axis=0, keepdims=True)
     line, lane = count((rows, rows), 0), count((rows, rows), 1)
-    matches = ids_ref[...].astype(F32) == count((rows, variants), 1)
-    slot = across(jnp.where(matches, slot_ref[...].astype(F32), 0.0))
-    owner = across((slot >= (count((rows, shards), 1) + 1.0) * slots).astype(F32))
-    owner_along = along(jnp.where(line == lane, owner, 0.0))
-    same = owner == owner_along
-    place = across((same & (lane < line)).astype(F32))
-    paired = ways.direct and ways.fast == 2
-    beside = pair = jnp.zeros_like(place)
-    if paired:
-        odd = across((owner == 2.0 * count((rows, shards), 1) + 1.0).astype(F32))
-        beside = across((owner + 1.0 - 2.0 * odd == owner_along).astype(F32))
-        pair = across(same.astype(F32)) + beside
-    facts_ref[0] = jnp.where(
-        (jnp.max(place) < USUAL) & (jnp.max(pair) <= USUAL_PAIR), 0, 1
-    )
-    facts_ref[1] = jnp.sum((owner == me).astype(F32)).astype(I32)
-    facts_ref[2] = jnp.sum((owner == order[ways.slow % shards]).astype(F32)).astype(I32)
-    row_along, row_down = count((1, rows), 1), count((rows, 1), 0)
-    at_along, at_down = row_along, row_down
+    diagonal = line == lane
+    at_along, at_down = count((1, rows), 1), count((rows, 1), 0)
     for b in range(shards):
         shift = (order[b] - b) * own_rows
         low, high = b * own_rows, (b + 1) * own_rows
-        at_along = jnp.where((row_along >= low) & (row_along < high), row_along + shift, at_along)
-        at_down = jnp.where((row_down >= low) & (row_down < high), row_down + shift, at_down)
-    turned = lambda a: along(jnp.where(line == at_along, a, 0.0))
-    slot_along = along(jnp.where(line == lane, slot, 0.0))
-    slot = across(jnp.where(lane == at_down, slot_along, 0.0))
-    owner, place, beside = turned(owner), turned(place), turned(beside)
-    step = jnp.zeros_like(owner)
-    arrive, packed = step, place
+        at_along = jnp.where(
+            (lane[:1] >= low) & (lane[:1] < high), lane[:1] + shift, at_along
+        )
+        at_down = jnp.where(
+            (line[:, :1] >= low) & (line[:, :1] < high), line[:, :1] + shift, at_down
+        )
+    ids = across(jnp.where(lane == at_down, ids_ref[...].astype(F32), 0.0))
+    ids = along(jnp.where(diagonal, ids, 0.0))
+    slot = jnp.zeros_like(ids)
+    for v in range(variants):
+        slot = jnp.where(ids == float(v), slot_ref[v].astype(F32), slot)
+    slot_down = across(jnp.where(diagonal, slot, 0.0))
+    owner_of = lambda a: sum((a >= float(o * slots)).astype(F32) for o in range(1, shards))
+    owner, owner_down = owner_of(slot), owner_of(slot_down)
+    same = owner_down == owner
+    place = along((same & (at_down < at_along)).astype(F32))
+    packed, pair = place, jnp.zeros_like(place)
+    step = arrive = jnp.zeros_like(place)
+    paired = ways.direct and ways.fast == 2
+    if paired:
+        odd = sum((owner == float(o)).astype(F32) for o in range(1, shards, 2))
+        beside = along((owner_down == owner + 1.0 - 2.0 * odd).astype(F32))
+        pair = along(same.astype(F32)) + beside
     for b in range(shards):
         hit = owner == order[b]
         step = jnp.where(hit, float(b), step)
         arrive = jnp.where(hit, float(b % ways.slow if paired else b), arrive)
         if paired and b >= ways.slow:
             packed = jnp.where(hit, place + beside, packed)
+    crowded = (place >= float(USUAL)) | (pair > float(USUAL_PAIR))
+    facts_ref[0] = jnp.max(crowded.astype(F32)).astype(I32)
+    facts_ref[1] = jnp.sum((owner == me).astype(F32)).astype(I32)
+    facts_ref[2] = jnp.sum((owner == beside_me).astype(F32)).astype(I32)
     lines = {
         MINE: jnp.where(owner == me, place, -1.0),
-        NEXT: jnp.where(owner == order[ways.slow % shards], place, -1.0),
+        NEXT: jnp.where(owner == beside_me, place, -1.0),
         STEP: step,
         PLACE: place,
         ARRIVE: arrive,
@@ -171,7 +182,7 @@
     }
     for n, values in lines.items():
         marks_ref[n : n + 1] = values.astype(I32)
-    local = slot - me * slots
+    local = slot_down - me * slots
     for ref in (in_ref, out_ref):
         wide = ref.shape[1] // slots
         column = count(ref.shape, 1)
@@ -181,8 +192,10 @@
         copy.wait()
 
 
-def tables(ways, me, ids, variant_slot, x, shrink, slots, rank):
-    rows = ids.shape[0]
+def tables(ways, me, at, ids, variant_slot, x, shrink, expand, slots, rank):
+    rows = ids.shape[1]
+    shards = at.shape[0]
+    depth, width = expand.shape
     return pl.pallas_call(
         functools.partial(tables_kernel, ways, slots),
         out_shape=(
@@ -192,13 +205,14 @@
             jax.ShapeDtypeStruct((3,), I32),
             jax.ShapeDtypeStruct(x.shape, BF),
             jax.ShapeDtypeStruct(shrink.shape, BF),
+            jax.ShapeDtypeStruct((depth, width // 2), BF),
         ),
-        in_specs=[SCALARS, SCALARS, WHOLE, WHOLE, FAR, FAR],
-        out_specs=(WHOLE, WHOLE, WHOLE, SCALARS, WHOLE, WHOLE),
-        scratch_shapes=[pltpu.SemaphoreType.DMA((2,))],
+        in_specs=[SCALARS] * 4 + [WHOLE] + [FAR] * 3,
+        out_specs=(WHOLE, WHOLE, WHOLE, SCALARS, WHOLE, WHOLE, WHOLE),
+        scratch_shapes=[pltpu.SemaphoreType.DMA((2 + shards,))],
         compiler_params=params(52),
-        cost_estimate=cost(0, 4 * x.size + 4 * shrink.size),
-    )(ways.order, me, ids, variant_slot, x, shrink)
+        cost_estimate=cost(0, 4 * x.size + 4 * shrink.size + 2 * expand.size),
+    )(ways.order, me, at, variant_slot, ids, x, shrink, expand)
 
 
 def low_in_kernel(count, shrink_ref, mask_ref, *refs):
@@ -233,53 +247,34 @@
 
 
 def expand_kernel(
-    cap,
-    fast,
-    at_ref,
-    own_ref,
-    got_ref,
-    marks_ref,
-    cols_ref,
-    far_ref,
-    near_ref,
-    *refs,
+    cap, fast, at_ref, own_ref, got_ref, marks_ref, cols_ref, near_ref, far_ref, *out_refs
 ):
-    out_refs, held, sems = refs[:-2], refs[-2], refs[-1]
-    half = out_refs[0].shape[1]
-    count = at_ref.shape[0]
-    columns = [pl.ds(pl.multiple_of(at_ref[b] * half, half), half) for b in range(count)]
-    copies = []
-    for b in range(count):
-        put = held.at[:, pl.ds(b * half, half)]
-        copies.append(pltpu.make_async_copy(near_ref.at[:, columns[b]], put, sems.at[b]))
-        copies[b].start()
     low = (own_ref[...] + got_ref[...]).astype(BF)
     picked = dot(one_hot(cap, marks_ref[MINE : MINE + 1]), low).astype(BF)
     lhs = jnp.concatenate([dot(picked, cols_ref[kind]) for kind in range(2)], axis=0).astype(BF)
     tall = lhs.shape[0]
+    half = out_refs[0].shape[1]
+    count = at_ref.shape[0]
     for b in range(count):
-        copies[b].wait()
-        both = jnp.concatenate([held[:, pl.ds(b * half, half)], far_ref[:, columns[b]]], axis=0)
+        here = pl.ds(b * half, half)
+        columns = pl.ds(pl.multiple_of(at_ref[b] * half, half), half)
+        both = jnp.concatenate([near_ref[:, here], far_ref[:, columns]], axis=0)
         at = b % (count // fast)
         out_refs[b * fast // count][pl.ds(at * tall, tall)] = dot(lhs, both).astype(BF)
 
 
 def expand_rows(at, own, got, marks, cols, near, far, cap, fast):
-    depth, width = near.shape
+    depth, width = far.shape
     shards = at.shape[0]
     half = width // (2 * shards)
     out = jax.ShapeDtypeStruct((2 * cap * shards // fast, half), BF)
     return pl.pallas_call(
         functools.partial(expand_kernel, cap, fast),
         out_shape=(out,) * fast,
-        in_specs=[SCALARS] + [WHOLE] * 5 + [FAR],
-        scratch_shapes=[
-            pltpu.VMEM((depth, width // 2), BF),
-            pltpu.SemaphoreType.DMA((shards,)),
-        ],
-        compiler_params=params(52),
+        in_specs=[SCALARS] + [WHOLE] * 6,
+        compiler_params=params(16),
         cost_estimate=cost(8 * cap * depth * width, 4 * (depth + cap) * width),
-    )(at, own, got, marks, cols, far, near)
+    )(at, own, got, marks, cols, near, far)
 
 
 def base_kernel(side_ref, x_ref, gate_ref, up_ref, out_ref, held, sums, sems):
@@ -539,7 +534,6 @@
     own_rows, width = tokens.shape
     rows = own_rows * shards
     slots = shrink_gu.shape[0]
-    variants = variant_slot.shape[0]
     rank = shrink_down.shape[1]
     half_rank = expand_gu.shape[2]
     half = gate_weight.shape[1] // 2
@@ -553,13 +547,15 @@
     near = expand_gu.reshape(slots * 2 * half_rank, -1)
     token_parts, far = ways.gather(tokens, swap(near))
     shrink_in = shrink_gu.reshape(slots * 2 * rank, width)
-    marks, mask_in, slot_mask, facts, token_parts[0], shrink_in = tables(
+    marks, mask_in, slot_mask, facts, token_parts[0], shrink_in, near = tables(
         ways,
         me.reshape(1),
-        variant_ids,
-        variant_slot.reshape(1, variants),
+        at_here,
+        variant_ids.reshape(1, rows),
+        variant_slot,
         token_parts[0],
         shrink_in,
+        near,
         slots,
         rank,
     )

time: 78.4 us -> 77.6 us (0.990)
  Pallas kernels: 30.4 us -> 29 us
  waiting for transfers between devices: 10.7 us -> 11.5 us
    pallas_call x1, Pallas kernels: 2.87 us -> 1.16 us  [expand_rows(): pl.pallas_call(functools.partial(expand_kernel, cap, fast), out_shape=(ou...]
    unnamed x9 -> x10, local copies, waits for them, and re-layouts: 2.24 us -> 2.15 us
  transfers between devices with their start and end apart: 28 -> 28, of which waited for: 9 -> 10; matrix products, arithmetic and copies ran while one was open for 1% -> 0% of each run, Pallas kernels for 33% -> 34%
where the time goes in v5:
time: 77.6 us; the launch traced here: 77.4 us
  starting transfers between devices  33.3 us (43%)
  Pallas kernels  29 us (37%)
  waiting for transfers between devices  11.5 us (15%)
  local copies, waits for them, and re-layouts  2.15 us (3%)
  other arithmetic  0.91 us (1%)
    ppermute x9, starting transfers between devices, slow_steps(): got[-a % self.slow] = lax.ppermute(blocks[a], 'ff', self.back(a, 0))  13.4 us
    pallas_call x2, Pallas kernels, base_half(): pl.pallas_call(base_kernel, out_shape=jax.ShapeDtypeStruct((2, rows, half...  12.5 us
    pallas_call x2, Pallas kernels, down_base(): pl.pallas_call(functools.partial(down_kernel, start), out_shape=outs, in_...  8.17 us
    ppermute x3, starting transfers between devices, gather(): lax.ppermute(block, 'ff', self.back(-a, 0))  7.41 us
    ppermute x9, waiting for transfers between devices, slow_steps(): got[-a % self.slow] = lax.ppermute(blocks[a], 'ff', self.back(a, 0))  5.62 us
    ppermute x4, starting transfers between devices, gather(): lax.ppermute(part, 'ff', self.back(0, -c))  4.12 us
    pallas_call x1, Pallas kernels, tables(): pl.pallas_call(functools.partial(tables_kernel, ways, slots), out_shape=(...  3 us
    unnamed x10, local copies, waits for them, and re-layouts  2.15 us
  transfers between devices with their start and end apart: 28, of which 10 were waited for; matrix products, arithmetic and copies ran while one was open for 0% of the time, Pallas kernels for 34%

profile of v5, /device:TPU:0, one launch (start us, length us, event | category | flops | bytes accessed | tf_op | source)
XLA Modules:
  0.0 77.4 jit_solution(12036286715298202148)
XLA Ops:
  0.5 3.6 %collective-permute-start.40 = (bf16[8,4096]{1,0:T(8,128)(2,1)}, bf16[8,4096]{1,0:T(8,128)(2,1)S(1)}, u32[]{:S(2)}, u32[]{:S(2)}) collective-permute-start(bf16[8,4096]{1,0:T(8,128)(2,1)} %x_ref.1), channel_id=1, source_target_pairs={{0,8},{2,10},{4,12},{6,14},{8,0},{10,2},{12,4},{14,6},{1,9},{3,11}... | collective-permute-start | bytes 196616 | tf_op jit(solution)/shard_map/ppermute | solution.py:79
  4.0 1.6 %collective-permute-start.39 = (bf16[8,4096]{1,0:T(8,128)(2,1)}, bf16[8,4096]{1,0:T(8,128)(2,1)S(1)}, u32[]{:S(2)}, u32[]{:S(2)}) collective-permute-start(bf16[8,4096]{1,0:T(8,128)(2,1)} %x_ref.1), channel_id=1, source_target_pairs={{0,4},{2,6},{4,8},{6,10},{8,12},{10,14},{12,0},{14,2},{1,5},{3,7},... | collective-permute-start | bytes 196616 | tf_op jit(solution)/shard_map/ppermute | solution.py:79
  5.6 1.5 %collective-permute-start.42 = (bf16[8,4096]{1,0:T(8,128)(2,1)}, bf16[8,4096]{1,0:T(8,128)(2,1)S(1)}, u32[]{:S(2)}, u32[]{:S(2)}) collective-permute-start(bf16[8,4096]{1,0:T(8,128)(2,1)} %x_ref.1), channel_id=1, source_target_pairs={{0,2},{2,0},{4,6},{6,4},{8,10},{10,8},{12,14},{14,12},{1,3},{3,1},... | collective-permute-start | bytes 196616 | tf_op jit(solution)/shard_map/ppermute | solution.py:83
  7.1 2.2 %collective-permute-start.41 = (bf16[8,4096]{1,0:T(8,128)(2,1)}, bf16[8,4096]{1,0:T(8,128)(2,1)S(1)}, u32[]{:S(2)}, u32[]{:S(2)}) collective-permute-start(bf16[8,4096]{1,0:T(8,128)(2,1)} %x_ref.1), channel_id=1, source_target_pairs={{0,12},{2,14},{4,0},{6,2},{8,4},{10,6},{12,8},{14,10},{1,13},{3,15... | collective-permute-start | bytes 196616 | tf_op jit(solution)/shard_map/ppermute | solution.py:79
  10.1 1.6 %collective-permute-done.41.refs_5_ = bf16[8,4096]{1,0:T(8,128)(2,1)S(1)} collective-permute-done((bf16[8,4096]{1,0:T(8,128)(2,1)}, bf16[8,4096]{1,0:T(8,128)(2,1)S(1)}, u32[]{:S(2)}, u32[]{:S(2)}) %collective-permute-start.41) | collective-permute-done | bytes 65568 | tf_op jit(solution)/shard_map/ppermute | solution.py:79
  11.7 1.2 %collective-permute-start.45 = (bf16[8,4096]{1,0:T(8,128)(2,1)S(1)}, bf16[8,4096]{1,0:T(8,128)(2,1)S(1)}, u32[]{:S(2)}, u32[]{:S(2)}) collective-permute-start(bf16[8,4096]{1,0:T(8,128)(2,1)S(1)} %collective-permute-done.41.refs_5_), channel_id=1, source_target_pairs={{0,2},{2,0},{4,6},{6,4},{8,10},{10,8},{12,14},{14,12},{1,3},{3,1},... | collective-permute-start | bytes 196616 | tf_op jit(solution)/shard_map/ppermute | solution.py:83
  15.9 3.0 %shard_map.100 = (s32[8,64]{1,0:T(8,128)S(1)}, f32[64,128]{1,0:T(8,128)S(1)}, bf16[64,64]{1,0:T(8,128)(2,1)S(1)}, s32[3]{0:T(128)S(1)}, bf16[8,4096]{1,0:T(8,128...) custom-call(s32[8]{0:T(128)S(1)} %get-tuple-element.265.order_ref, s32[1]{0:T(128)} %bitcast.6.me_ref, ...), custom_call_target="tpu_custom_call" | custom-call | bytes 4325376 | tf_op jit(solution)/shard_map/pallas_call | solution.py:199
  21.3 55.4 %conditional.3 = (bf16[8,4096]{1,0:T(8,128)(2,1)S(1)}, f32[8,4096]{1,0:T(8,128)S(1)}, f32[8,4096]{1,0:T(8,128)S(1)}, f32[8,4096]{1,0:T(8,128)S(1)}) conditional(s32[]{:T(128)} %bitcast.10, (s32[]{:T(128)}, s32[8]{0:T(128)S(1)}, f32[64,128]{1,0:T(8,128)S(1)}, f32[64,128]{1,0:T(8,128)S(1)}, s32[8,64]{1,0:T(8,128)S(1)}, ...), branch_computations={%region_0.1_spmd, %region_1.2_spmd} | conditional | flops 3724640256 | bytes 92963672
  22.5 1.3 %collective-permute-start.19 = (bf16[128,1024]{1,0:T(8,128)(2,1)S(1)}, bf16[128,1024]{1,0:T(8,128)(2,1)S(1)}, u32[]{:S(2)}, u32[]{:S(2)}) collective-permute-start(bf16[128,1024]{1,0:T(8,128)(2,1)S(1)} %get-tuple-element.173), channel_id=1, source_target_pairs={{0,2},{2,0},{4,6},{6,4},{8,10},{10,8},{12,14},{14,12},{1,3},{3,1},... | collective-permute-start | bytes 786440 | tf_op jit(solution)/shard_map/cond/branch_1_fun/ppermute | solution.py:585
  23.7 6.3 %branch_1_fun.11 = bf16[2,64,1024]{2,1,0:T(8,128)(2,1)S(1)} custom-call(s32[1]{0:T(128)S(6)} %sub.32.side_ref, bf16[64,4096]{1,0:T(8,128)(2,1)S(1)} %get-tuple-element.180.x_ref, bf16[4096,2048]{1,0:T(8,128)(2,1)} %get-tuple-element.171.gate_ref, bf16[4096,2048]{1,0:T(8,128)(2,1)} %get-tuple-element.172.up_ref), custom_call_target="tpu_custom_call" | custom-call | flops 1073741824 | bytes 17301504 | tf_op jit(solution)/shard_map/cond/branch_1_fun/pallas_call | solution.py:304
  33.4 3.5 %collective-permute-start.22 = (bf16[48,1024]{1,0:T(8,128)(2,1)S(1)}, bf16[48,1024]{1,0:T(8,128)(2,1)S(1)}, u32[]{:S(2)}, u32[]{:S(2)}) collective-permute-start(bf16[48,1024]{1,0:T(8,128)(2,1)S(1)} %get-tuple-element.184), channel_id=1, source_target_pairs={{0,8},{2,10},{4,12},{6,14},{8,0},{10,2},{12,4},{14,6},{1,9},{3,11}... | collective-permute-start | bytes 294920 | tf_op jit(solution)/shard_map/cond/branch_1_fun/ppermute | solution.py:92
  36.9 6.2 %branch_1_fun.13.own_ref = f32[2,64,1024]{2,1,0:T(8,128)S(1)} custom-call(s32[1]{0:T(128)} %bitcast.3.side_ref.core_ref, bf16[64,4096]{1,0:T(8,128)(2,1)S(1)} %get-tuple-element.180.x_ref, bf16[4096,2048]{1,0:T(8,128)(2,1)} %get-tuple-element.171.gate_ref, bf16[4096,2048]{1,0:T(8,128)(2,1)} %get-tuple-element.172.up_ref), custom_call_target="tpu_custom_call" | custom-call | flops 1073741824 | bytes 17301504 | tf_op jit(solution)/shard_map/cond/branch_1_fun/pallas_call | solution.py:304
  45.2 1.3 %collective-permute-start.25 = (bf16[64,1024]{1,0:T(8,128)(2,1)S(1)}, bf16[64,1024]{1,0:T(8,128)(2,1)S(1)}, u32[]{:S(2)}, u32[]{:S(2)}) collective-permute-start(bf16[64,1024]{1,0:T(8,128)(2,1)S(1)} %get-tuple-element.191), channel_id=1, source_target_pairs={{0,2},{2,0},{4,6},{6,4},{8,10},{10,8},{12,14},{14,12},{1,3},{3,1},... | collective-permute-start | bytes 393224 | tf_op jit(solution)/shard_map/cond/branch_1_fun/ppermute | solution.py:606
  46.5 4.2 %branch_1_fun.15 = (f32[32,2048]{1,0:T(8,128)S(1)}, bf16[32,2048]{1,0:T(8,128)(2,1)S(1)}) custom-call(s32[1]{0:T(128)} %bitcast.3.side_ref.core_ref, bf16[64,1024]{1,0:T(8,128)(2,1)S(1)} %get-tuple-element.198.near_ref, bf16[64,1024]{1,0:T(8,128)(2,1)S(1)} %collective-permute-done.24.far_ref, bf16[2048,4096]{1,0:T(8,128)(2,1)} %get-tuple-element.187.weight_ref), custom_call_target="tpu_custom_call" | custom-call | flops 536870912 | bytes 8912896 | tf_op jit(solution)/shard_map/cond/branch_1_fun/pallas_call | solution.py:433
  51.1 1.2 %collective-permute-start.27 = (bf16[32,2048]{1,0:T(8,128)(2,1)S(1)}, bf16[32,2048]{1,0:T(8,128)(2,1)S(1)}, u32[]{:S(2)}, u32[]{:S(2)}) collective-permute-start(bf16[32,2048]{1,0:T(8,128)(2,1)S(1)} %get-tuple-element.201), channel_id=1, source_target_pairs={{0,2},{2,0},{4,6},{6,4},{8,10},{10,8},{12,14},{14,12},{1,3},{3,1},... | collective-permute-start | bytes 393224 | tf_op jit(solution)/shard_map/cond/branch_1_fun/ppermute | solution.py:609
  52.3 2.7 %collective-permute-start.28 = (bf16[32,1024]{1,0:T(8,128)(2,1)S(1)}, bf16[32,1024]{1,0:T(8,128)(2,1)S(1)}, u32[]{:S(2)}, u32[]{:S(2)}) collective-permute-start(bf16[32,1024]{1,0:T(8,128)(2,1)S(1)} %get-tuple-element.203), channel_id=1, source_target_pairs={{0,4},{2,6},{4,8},{6,10},{8,12},{10,14},{12,0},{14,2},{1,5},{3,7},... | collective-permute-start | bytes 196616 | tf_op jit(solution)/shard_map/cond/branch_1_fun/ppermute | solution.py:92
  55.7 1.8 %collective-permute-start.30 = (bf16[32,1024]{1,0:T(8,128)(2,1)S(1)}, bf16[32,1024]{1,0:T(8,128)(2,1)S(1)}, u32[]{:S(2)}, u32[]{:S(2)}) collective-permute-start(bf16[32,1024]{1,0:T(8,128)(2,1)S(1)} %get-tuple-element.205), channel_id=1, source_target_pairs={{0,12},{2,14},{4,0},{6,2},{8,4},{10,6},{12,8},{14,10},{1,13},{3,15... | collective-permute-start | bytes 196616 | tf_op jit(solution)/shard_map/cond/branch_1_fun/ppermute | solution.py:92
  57.5 4.0 %branch_1_fun.17 = (f32[32,2048]{1,0:T(8,128)S(1)}, bf16[32,2048]{1,0:T(8,128)(2,1)S(1)}) custom-call(s32[1]{0:T(128)} %bitcast.3.side_ref.core_ref, bf16[64,1024]{1,0:T(8,128)(2,1)S(1)} %get-tuple-element.198.near_ref, bf16[64,1024]{1,0:T(8,128)(2,1)S(1)} %collective-permute-done.24.far_ref, bf16[2048,4096]{1,0:T(8,128)(2,1)} %get-tuple-element.187.weight_ref), custom_call_target="tpu_custom_call" | custom-call | flops 536870912 | bytes 8912896 | tf_op jit(solution)/shard_map/cond/branch_1_fun/pallas_call | solution.py:433
  63.3 1.3 %collective-permute-start.33 = (f32[16,64]{1,0:T(8,128)S(1)}, f32[16,64]{1,0:T(8,128)S(1)}, u32[]{:S(2)}, u32[]{:S(2)}) collective-permute-start(f32[16,64]{1,0:T(8,128)S(1)} %branch_1_fun.18.refs_4_), channel_id=1, source_target_pairs={{0,2},{2,0},{4,6},{6,4},{8,10},{10,8},{12,14},{14,12},{1,3},{3,1},... | collective-permute-start | bytes 12296 | tf_op jit(solution)/shard_map/cond/branch_1_fun/ppermute | solution.py:627
  65.2 1.3 %collective-permute-done.34.refs_7_ = f32[16,64]{1,0:T(8,128)S(1)} collective-permute-done((f32[16,64]{1,0:T(8,128)S(1)}, f32[16,64]{1,0:T(8,128)S(1)}, u32[]{:S(2)}, u32[]{:S(2)}) %collective-permute-start.34) | collective-permute-done | bytes 4128 | tf_op jit(solution)/shard_map/cond/branch_1_fun/ppermute | solution.py:631
  67.6 1.9 %collective-permute-start.35 = (bf16[8,4096]{1,0:T(8,128)(2,1)S(1)}, bf16[8,4096]{1,0:T(8,128)(2,1)S(1)}, u32[]{:S(2)}, u32[]{:S(2)}) collective-permute-start(bf16[8,4096]{1,0:T(8,128)(2,1)S(1)} %get-tuple-element.221), channel_id=1, source_target_pairs={{0,4},{2,6},{4,8},{6,10},{8,12},{10,14},{12,0},{14,2},{1,5},{3,7},... | collective-permute-start | bytes 196616 | tf_op jit(solution)/shard_map/cond/branch_1_fun/ppermute | solution.py:92
  70.4 1.5 %collective-permute-start.37 = (bf16[8,4096]{1,0:T(8,128)(2,1)S(1)}, bf16[8,4096]{1,0:T(8,128)(2,1)S(1)}, u32[]{:S(2)}, u32[]{:S(2)}) collective-permute-start(bf16[8,4096]{1,0:T(8,128)(2,1)S(1)} %get-tuple-element.223), channel_id=1, source_target_pairs={{0,12},{2,14},{4,0},{6,2},{8,4},{10,6},{12,8},{14,10},{1,13},{3,15... | collective-permute-start | bytes 196616 | tf_op jit(solution)/shard_map/cond/branch_1_fun/ppermute | solution.py:92
  71.9 2.5 %collective-permute-done.35 = bf16[8,4096]{1,0:T(8,128)(2,1)S(1)} collective-permute-done((bf16[8,4096]{1,0:T(8,128)(2,1)S(1)}, bf16[8,4096]{1,0:T(8,128)(2,1)S(1)}, u32[]{:S(2)}, u32[]{:S(2)}) %collective-permute-start.35) | collective-permute-done | bytes 65568 | tf_op jit(solution)/shard_map/cond/branch_1_fun/ppermute | solution.py:92
  74.4 2.0 %collective-permute-done.36 = bf16[8,4096]{1,0:T(8,128)(2,1)S(1)} collective-permute-done((bf16[8,4096]{1,0:T(8,128)(2,1)S(1)}, bf16[8,4096]{1,0:T(8,128)(2,1)S(1)}, u32[]{:S(2)}, u32[]{:S(2)}) %collective-permute-start.36) | collective-permute-done | bytes 65568 | tf_op jit(solution)/shard_map/cond/branch_1_fun/ppermute | solution.py:92
  (65 shorter events, 19.2 us)
Async XLA Ops:
  0.0 12.9 %collective-permute-start.38 = (bf16[64,16384]{1,0:T(8,128)(2,1)}, bf16[64,16384]{1,0:T(8,128)(2,1)S(1)}, u32[]{:S(2)}, u32[]{:S(2)}) collective-permute-start(bf16[64,16384]{1,0:T(8,128)(2,1)} %bitcast.15), channel_id=1, source_target_pairs={{0,1},{1,0},{2,3},{3,2},{4,5},{5,4},{6,7},{7,6},{8,9},{9,8},{10,11... | collective-permute-start | bytes 6291464 | tf_op jit(solution)/shard_map/ppermute | solution.py:545
  0.5 9.1 %collective-permute-start.40 = (bf16[8,4096]{1,0:T(8,128)(2,1)}, bf16[8,4096]{1,0:T(8,128)(2,1)S(1)}, u32[]{:S(2)}, u32[]{:S(2)}) collective-permute-start(bf16[8,4096]{1,0:T(8,128)(2,1)} %x_ref.1), channel_id=1, source_target_pairs={{0,8},{2,10},{4,12},{6,14},{8,0},{10,2},{12,4},{14,6},{1,9},{3,11}... | collective-permute-start | bytes 196616 | tf_op jit(solution)/shard_map/ppermute | solution.py:79
  4.0 8.9 %collective-permute-start.39 = (bf16[8,4096]{1,0:T(8,128)(2,1)}, bf16[8,4096]{1,0:T(8,128)(2,1)S(1)}, u32[]{:S(2)}, u32[]{:S(2)}) collective-permute-start(bf16[8,4096]{1,0:T(8,128)(2,1)} %x_ref.1), channel_id=1, source_target_pairs={{0,4},{2,6},{4,8},{6,10},{8,12},{10,14},{12,0},{14,2},{1,5},{3,7},... | collective-permute-start | bytes 196616 | tf_op jit(solution)/shard_map/ppermute | solution.py:79
  5.6 13.3 %collective-permute-start.42 = (bf16[8,4096]{1,0:T(8,128)(2,1)}, bf16[8,4096]{1,0:T(8,128)(2,1)S(1)}, u32[]{:S(2)}, u32[]{:S(2)}) collective-permute-start(bf16[8,4096]{1,0:T(8,128)(2,1)} %x_ref.1), channel_id=1, source_target_pairs={{0,2},{2,0},{4,6},{6,4},{8,10},{10,8},{12,14},{14,12},{1,3},{3,1},... | collective-permute-start | bytes 196616 | tf_op jit(solution)/shard_map/ppermute | solution.py:83
  7.1 4.6 %collective-permute-start.41 = (bf16[8,4096]{1,0:T(8,128)(2,1)}, bf16[8,4096]{1,0:T(8,128)(2,1)S(1)}, u32[]{:S(2)}, u32[]{:S(2)}) collective-permute-start(bf16[8,4096]{1,0:T(8,128)(2,1)} %x_ref.1), channel_id=1, source_target_pairs={{0,12},{2,14},{4,0},{6,2},{8,4},{10,6},{12,8},{14,10},{1,13},{3,15... | collective-permute-start | bytes 196616 | tf_op jit(solution)/shard_map/ppermute | solution.py:79
  9.5 9.4 %collective-permute-start.44 = (bf16[8,4096]{1,0:T(8,128)(2,1)S(1)}, bf16[8,4096]{1,0:T(8,128)(2,1)S(1)}, u32[]{:S(2)}, u32[]{:S(2)}) collective-permute-start(bf16[8,4096]{1,0:T(8,128)(2,1)S(1)} %collective-permute-done.40.refs_4_), channel_id=1, source_target_pairs={{0,2},{2,0},{4,6},{6,4},{8,10},{10,8},{12,14},{14,12},{1,3},{3,1},... | collective-permute-start | bytes 196616 | tf_op jit(solution)/shard_map/ppermute | solution.py:83
  11.7 7.2 %collective-permute-start.45 = (bf16[8,4096]{1,0:T(8,128)(2,1)S(1)}, bf16[8,4096]{1,0:T(8,128)(2,1)S(1)}, u32[]{:S(2)}, u32[]{:S(2)}) collective-permute-start(bf16[8,4096]{1,0:T(8,128)(2,1)S(1)} %collective-permute-done.41.refs_5_), channel_id=1, source_target_pairs={{0,2},{2,0},{4,6},{6,4},{8,10},{10,8},{12,14},{14,12},{1,3},{3,1},... | collective-permute-start | bytes 196616 | tf_op jit(solution)/shard_map/ppermute | solution.py:83
  12.9 6.0 %collective-permute-start.43 = (bf16[8,4096]{1,0:T(8,128)(2,1)S(1)}, bf16[8,4096]{1,0:T(8,128)(2,1)S(1)}, u32[]{:S(2)}, u32[]{:S(2)}) collective-permute-start(bf16[8,4096]{1,0:T(8,128)(2,1)S(1)} %collective-permute-done.39.refs_3_), channel_id=1, source_target_pairs={{0,2},{2,0},{4,6},{6,4},{8,10},{10,8},{12,14},{14,12},{1,3},{3,1},... | collective-permute-start | bytes 196616 | tf_op jit(solution)/shard_map/ppermute | solution.py:83
  22.5 8.4 %collective-permute-start.19 = (bf16[128,1024]{1,0:T(8,128)(2,1)S(1)}, bf16[128,1024]{1,0:T(8,128)(2,1)S(1)}, u32[]{:S(2)}, u32[]{:S(2)}) collective-permute-start(bf16[128,1024]{1,0:T(8,128)(2,1)S(1)} %get-tuple-element.173), channel_id=1, source_target_pairs={{0,2},{2,0},{4,6},{6,4},{8,10},{10,8},{12,14},{14,12},{1,3},{3,1},... | collective-permute-start | bytes 786440 | tf_op jit(solution)/shard_map/cond/branch_1_fun/ppermute | solution.py:585
  30.9 20.2 %collective-permute-start.26 = (bf16[64,4096]{1,0:T(8,128)(2,1)S(1)}, bf16[64,4096]{1,0:T(8,128)(2,1)S(1)}, u32[]{:S(2)}, u32[]{:S(2)}) collective-permute-start(bf16[64,4096]{1,0:T(8,128)(2,1)S(1)} %bitcast.19), channel_id=1, source_target_pairs={{0,2},{2,0},{4,6},{6,4},{8,10},{10,8},{12,14},{14,12},{1,3},{3,1},... | collective-permute-start | bytes 1572872 | tf_op jit(solution)/shard_map/cond/branch_1_fun/ppermute | solution.py:591
  32.1 12.1 %collective-permute-start.20 = (bf16[2,64,1024]{2,1,0:T(8,128)(2,1)S(1)}, bf16[2,64,1024]{2,1,0:T(8,128)(2,1)S(1)}, u32[]{:S(2)}, u32[]{:S(2)}) collective-permute-start(bf16[2,64,1024]{2,1,0:T(8,128)(2,1)S(1)} %branch_1_fun.11), channel_id=1, source_target_pairs={{0,1},{1,0},{2,3},{3,2},{4,5},{5,4},{6,7},{7,6},{8,9},{9,8},{10,11... | collective-permute-start | bytes 786440 | tf_op jit(solution)/shard_map/cond/branch_1_fun/ppermute | solution.py:545
  32.9 10.2 %collective-permute-start.21 = (bf16[48,1024]{1,0:T(8,128)(2,1)S(1)}, bf16[48,1024]{1,0:T(8,128)(2,1)S(1)}, u32[]{:S(2)}, u32[]{:S(2)}) collective-permute-start(bf16[48,1024]{1,0:T(8,128)(2,1)S(1)} %get-tuple-element.183), channel_id=1, source_target_pairs={{0,4},{2,6},{4,8},{6,10},{8,12},{10,14},{12,0},{14,2},{1,5},{3,7},... | collective-permute-start | bytes 294920 | tf_op jit(solution)/shard_map/cond/branch_1_fun/ppermute | solution.py:92
  33.4 10.8 %collective-permute-start.22 = (bf16[48,1024]{1,0:T(8,128)(2,1)S(1)}, bf16[48,1024]{1,0:T(8,128)(2,1)S(1)}, u32[]{:S(2)}, u32[]{:S(2)}) collective-permute-start(bf16[48,1024]{1,0:T(8,128)(2,1)S(1)} %get-tuple-element.184), channel_id=1, source_target_pairs={{0,8},{2,10},{4,12},{6,14},{8,0},{10,2},{12,4},{14,6},{1,9},{3,11}... | collective-permute-start | bytes 294920 | tf_op jit(solution)/shard_map/cond/branch_1_fun/ppermute | solution.py:92
  36.9 7.4 %collective-permute-start.23 = (bf16[48,1024]{1,0:T(8,128)(2,1)S(1)}, bf16[48,1024]{1,0:T(8,128)(2,1)S(1)}, u32[]{:S(2)}, u32[]{:S(2)}) collective-permute-start(bf16[48,1024]{1,0:T(8,128)(2,1)S(1)} %get-tuple-element.185), channel_id=1, source_target_pairs={{0,12},{2,14},{4,0},{6,2},{8,4},{10,6},{12,8},{14,10},{1,13},{3,15... | collective-permute-start | bytes 294920 | tf_op jit(solution)/shard_map/cond/branch_1_fun/ppermute | solution.py:92
  45.2 5.9 %collective-permute-start.25 = (bf16[64,1024]{1,0:T(8,128)(2,1)S(1)}, bf16[64,1024]{1,0:T(8,128)(2,1)S(1)}, u32[]{:S(2)}, u32[]{:S(2)}) collective-permute-start(bf16[64,1024]{1,0:T(8,128)(2,1)S(1)} %get-tuple-element.191), channel_id=1, source_target_pairs={{0,2},{2,0},{4,6},{6,4},{8,10},{10,8},{12,14},{14,12},{1,3},{3,1},... | collective-permute-start | bytes 393224 | tf_op jit(solution)/shard_map/cond/branch_1_fun/ppermute | solution.py:606
  51.1 10.4 %collective-permute-start.27 = (bf16[32,2048]{1,0:T(8,128)(2,1)S(1)}, bf16[32,2048]{1,0:T(8,128)(2,1)S(1)}, u32[]{:S(2)}, u32[]{:S(2)}) collective-permute-start(bf16[32,2048]{1,0:T(8,128)(2,1)S(1)} %get-tuple-element.201), channel_id=1, source_target_pairs={{0,2},{2,0},{4,6},{6,4},{8,10},{10,8},{12,14},{14,12},{1,3},{3,1},... | collective-permute-start | bytes 393224 | tf_op jit(solution)/shard_map/cond/branch_1_fun/ppermute | solution.py:609
  52.3 9.1 %collective-permute-start.28 = (bf16[32,1024]{1,0:T(8,128)(2,1)S(1)}, bf16[32,1024]{1,0:T(8,128)(2,1)S(1)}, u32[]{:S(2)}, u32[]{:S(2)}) collective-permute-start(bf16[32,1024]{1,0:T(8,128)(2,1)S(1)} %get-tuple-element.203), channel_id=1, source_target_pairs={{0,4},{2,6},{4,8},{6,10},{8,12},{10,14},{12,0},{14,2},{1,5},{3,7},... | collective-permute-start | bytes 196616 | tf_op jit(solution)/shard_map/cond/branch_1_fun/ppermute | solution.py:92
  55.0 6.5 %collective-permute-start.29 = (bf16[32,1024]{1,0:T(8,128)(2,1)S(1)}, bf16[32,1024]{1,0:T(8,128)(2,1)S(1)}, u32[]{:S(2)}, u32[]{:S(2)}) collective-permute-start(bf16[32,1024]{1,0:T(8,128)(2,1)S(1)} %get-tuple-element.204), channel_id=1, source_target_pairs={{0,8},{2,10},{4,12},{6,14},{8,0},{10,2},{12,4},{14,6},{1,9},{3,11}... | collective-permute-start | bytes 196616 | tf_op jit(solution)/shard_map/cond/branch_1_fun/ppermute | solution.py:92
  55.7 5.8 %collective-permute-start.30 = (bf16[32,1024]{1,0:T(8,128)(2,1)S(1)}, bf16[32,1024]{1,0:T(8,128)(2,1)S(1)}, u32[]{:S(2)}, u32[]{:S(2)}) collective-permute-start(bf16[32,1024]{1,0:T(8,128)(2,1)S(1)} %get-tuple-element.205), channel_id=1, source_target_pairs={{0,12},{2,14},{4,0},{6,2},{8,4},{10,6},{12,8},{14,10},{1,13},{3,15... | collective-permute-start | bytes 196616 | tf_op jit(solution)/shard_map/cond/branch_1_fun/ppermute | solution.py:92
  61.5 5.5 %collective-permute-start.31 = (bf16[32,2048]{1,0:T(8,128)(2,1)S(1)}, bf16[32,2048]{1,0:T(8,128)(2,1)S(1)}, u32[]{:S(2)}, u32[]{:S(2)}) collective-permute-start(bf16[32,2048]{1,0:T(8,128)(2,1)S(1)} %get-tuple-element.212), channel_id=1, source_target_pairs={{0,2},{2,0},{4,6},{6,4},{8,10},{10,8},{12,14},{14,12},{1,3},{3,1},... | collective-permute-start | bytes 393224 | tf_op jit(solution)/shard_map/cond/branch_1_fun/ppermute | solution.py:616
  63.3 3.7 %collective-permute-start.33 = (f32[16,64]{1,0:T(8,128)S(1)}, f32[16,64]{1,0:T(8,128)S(1)}, u32[]{:S(2)}, u32[]{:S(2)}) collective-permute-start(f32[16,64]{1,0:T(8,128)S(1)} %branch_1_fun.18.refs_4_), channel_id=1, source_target_pairs={{0,2},{2,0},{4,6},{6,4},{8,10},{10,8},{12,14},{14,12},{1,3},{3,1},... | collective-permute-start | bytes 12296 | tf_op jit(solution)/shard_map/cond/branch_1_fun/ppermute | solution.py:627
  67.6 6.8 %collective-permute-start.35 = (bf16[8,4096]{1,0:T(8,128)(2,1)S(1)}, bf16[8,4096]{1,0:T(8,128)(2,1)S(1)}, u32[]{:S(2)}, u32[]{:S(2)}) collective-permute-start(bf16[8,4096]{1,0:T(8,128)(2,1)S(1)} %get-tuple-element.221), channel_id=1, source_target_pairs={{0,4},{2,6},{4,8},{6,10},{8,12},{10,14},{12,0},{14,2},{1,5},{3,7},... | collective-permute-start | bytes 196616 | tf_op jit(solution)/shard_map/cond/branch_1_fun/ppermute | solution.py:92
  69.5 7.0 %collective-permute-start.36 = (bf16[8,4096]{1,0:T(8,128)(2,1)S(1)}, bf16[8,4096]{1,0:T(8,128)(2,1)S(1)}, u32[]{:S(2)}, u32[]{:S(2)}) collective-permute-start(bf16[8,4096]{1,0:T(8,128)(2,1)S(1)} %get-tuple-element.222), channel_id=1, source_target_pairs={{0,8},{2,10},{4,12},{6,14},{8,0},{10,2},{12,4},{14,6},{1,9},{3,11}... | collective-permute-start | bytes 196616 | tf_op jit(solution)/shard_map/cond/branch_1_fun/ppermute | solution.py:92
  70.4 6.0 %collective-permute-start.37 = (bf16[8,4096]{1,0:T(8,128)(2,1)S(1)}, bf16[8,4096]{1,0:T(8,128)(2,1)S(1)}, u32[]{:S(2)}, u32[]{:S(2)}) collective-permute-start(bf16[8,4096]{1,0:T(8,128)(2,1)S(1)} %get-tuple-element.223), channel_id=1, source_target_pairs={{0,12},{2,14},{4,0},{6,2},{8,4},{10,6},{12,8},{14,10},{1,13},{3,15... | collective-permute-start | bytes 196616 | tf_op jit(solution)/shard_map/cond/branch_1_fun/ppermute | solution.py:92
  (9 other events, 33.5 us)

commit v6 on v5

--- a/solution.py
+++ b/solution.py
@@ -168,8 +168,9 @@
         arrive = jnp.where(hit, float(b % ways.slow if paired else b), arrive)
         if paired and b >= ways.slow:
             packed = jnp.where(hit, place + beside, packed)
-    crowded = (place >= float(USUAL)) | (pair > float(USUAL_PAIR))
-    facts_ref[0] = jnp.max(crowded.astype(F32)).astype(I32)
+    over = (place >= float(USUAL)).astype(F32)
+    far_over = (place >= float(USUAL_PAIR)) | (pair > float(USUAL_PAIR))
+    facts_ref[0] = jnp.max(jnp.where(far_over, 2.0, over)).astype(I32)
     facts_ref[1] = jnp.sum((owner == me).astype(F32)).astype(I32)
     facts_ref[2] = jnp.sum((owner == beside_me).astype(F32)).astype(I32)
     lines = {
@@ -584,9 +585,9 @@
         if split == 2:
             beside = lax.ppermute(made[1], "ff", ways.back(0, 1))
             base_there = base_half(there, held, gate_weight, up_weight, half, BF)
-            base_there, beside, expand = tied(base_there, beside, expand)
+            base_there, beside = tied(base_there, beside)
             made = pack(facts, made[0], beside, cap, room, ways.slow)
-            held, *made = tied(held, *made)
+            held, expand, *made = tied(held, expand, *made)
             delta = ways.slow_steps(made)
             expand_beside = lax.ppermute(expand, "ff", ways.back(0, 1))
         else:
@@ -639,14 +640,14 @@
         return ways.slow_steps(parts)
 
     most_room = 2 * most if split == 2 else most
-    if most <= USUAL:
+    if most <= USUAL_PAIR:
         parts = partial_sums(most, most_room)
     else:
-        parts = lax.cond(
-            most_facts[0] == 0,
-            lambda: partial_sums(USUAL, USUAL_PAIR if split == 2 else USUAL),
-            lambda: partial_sums(most, most_room),
-        )
+        rooms = [(USUAL, USUAL_PAIR), (USUAL_PAIR, USUAL_PAIR), (most, 2 * most)]
+        branches = [
+            functools.partial(partial_sums, cap, room if split == 2 else cap) for cap, room in rooms
+        ]
+        parts = lax.switch(most_facts[0], branches)
     return sum(part.astype(F32) for part in parts).astype(BF)
 
 

time: 77.6 us -> 77.6 us (level)
  transfers between devices with their start and end apart: 28 -> 28, of which waited for: 10 -> 9; matrix products, arithmetic and copies ran while one was open for 0% -> 0% of each run, Pallas kernels for 34% -> 33%
where the time goes in v6:
time: 77.6 us; the launch traced here: 77.4 us
  starting transfers between devices  33.3 us (43%)
  Pallas kernels  29 us (37%)
  waiting for transfers between devices  11.5 us (15%)
  local copies, waits for them, and re-layouts  2.15 us (3%)
  other arithmetic  0.91 us (1%)
    ppermute x9, starting transfers between devices, slow_steps(): got[-a % self.slow] = lax.ppermute(blocks[a], 'ff', self.back(a, 0))  13.4 us
    pallas_call x2, Pallas kernels, base_half(): pl.pallas_call(base_kernel, out_shape=jax.ShapeDtypeStruct((2, rows, half...  12.5 us
    pallas_call x2, Pallas kernels, down_base(): pl.pallas_call(functools.partial(down_kernel, start), out_shape=outs, in_...  8.17 us
    ppermute x3, starting transfers between devices, gather(): lax.ppermute(block, 'ff', self.back(-a, 0))  7.41 us
    ppermute x9, waiting for transfers between devices, slow_steps(): got[-a % self.slow] = lax.ppermute(blocks[a], 'ff', self.back(a, 0))  5.62 us
    ppermute x4, starting transfers between devices, gather(): lax.ppermute(part, 'ff', self.back(0, -c))  4.12 us
    pallas_call x1, Pallas kernels, tables(): pl.pallas_call(functools.partial(tables_kernel, ways, slots), out_shape=(...  3 us
    unnamed x10, local copies, waits for them, and re-layouts  2.15 us
  transfers between devices with their start and end apart: 28, of which 9 were waited for; matrix products, arithmetic and copies ran while one was open for 0% of the time, Pallas kernels for 33%

profile of v6, /device:TPU:0, one launch (start us, length us, event | category | flops | bytes accessed | tf_op | source)
XLA Modules:
  0.0 77.4 jit_solution(5344074229461532158)
XLA Ops:
  0.5 3.6 %collective-permute-start.59 = (bf16[8,4096]{1,0:T(8,128)(2,1)}, bf16[8,4096]{1,0:T(8,128)(2,1)S(1)}, u32[]{:S(2)}, u32[]{:S(2)}) collective-permute-start(bf16[8,4096]{1,0:T(8,128)(2,1)} %x_ref.1), channel_id=1, source_target_pairs={{0,8},{2,10},{4,12},{6,14},{8,0},{10,2},{12,4},{14,6},{1,9},{3,11}... | collective-permute-start | bytes 196616 | tf_op jit(solution)/shard_map/ppermute | solution.py:79
  4.0 1.6 %collective-permute-start.58 = (bf16[8,4096]{1,0:T(8,128)(2,1)}, bf16[8,4096]{1,0:T(8,128)(2,1)S(1)}, u32[]{:S(2)}, u32[]{:S(2)}) collective-permute-start(bf16[8,4096]{1,0:T(8,128)(2,1)} %x_ref.1), channel_id=1, source_target_pairs={{0,4},{2,6},{4,8},{6,10},{8,12},{10,14},{12,0},{14,2},{1,5},{3,7},... | collective-permute-start | bytes 196616 | tf_op jit(solution)/shard_map/ppermute | solution.py:79
  5.6 1.5 %collective-permute-start.61 = (bf16[8,4096]{1,0:T(8,128)(2,1)}, bf16[8,4096]{1,0:T(8,128)(2,1)S(1)}, u32[]{:S(2)}, u32[]{:S(2)}) collective-permute-start(bf16[8,4096]{1,0:T(8,128)(2,1)} %x_ref.1), channel_id=1, source_target_pairs={{0,2},{2,0},{4,6},{6,4},{8,10},{10,8},{12,14},{14,12},{1,3},{3,1},... | collective-permute-start | bytes 196616 | tf_op jit(solution)/shard_map/ppermute | solution.py:83
  7.1 2.2 %collective-permute-start.60 = (bf16[8,4096]{1,0:T(8,128)(2,1)}, bf16[8,4096]{1,0:T(8,128)(2,1)S(1)}, u32[]{:S(2)}, u32[]{:S(2)}) collective-permute-start(bf16[8,4096]{1,0:T(8,128)(2,1)} %x_ref.1), channel_id=1, source_target_pairs={{0,12},{2,14},{4,0},{6,2},{8,4},{10,6},{12,8},{14,10},{1,13},{3,15... | collective-permute-start | bytes 196616 | tf_op jit(solution)/shard_map/ppermute | solution.py:79
  10.1 1.6 %collective-permute-done.60.refs_5_ = bf16[8,4096]{1,0:T(8,128)(2,1)S(1)} collective-permute-done((bf16[8,4096]{1,0:T(8,128)(2,1)}, bf16[8,4096]{1,0:T(8,128)(2,1)S(1)}, u32[]{:S(2)}, u32[]{:S(2)}) %collective-permute-start.60) | collective-permute-done | bytes 65568 | tf_op jit(solution)/shard_map/ppermute | solution.py:79
  15.9 3.0 %shard_map.100 = (s32[8,64]{1,0:T(8,128)S(1)}, f32[64,128]{1,0:T(8,128)S(1)}, bf16[64,64]{1,0:T(8,128)(2,1)S(1)}, s32[3]{0:T(128)S(1)}, bf16[8,4096]{1,0:T(8,128...) custom-call(s32[8]{0:T(128)S(1)} %get-tuple-element.368.order_ref, s32[1]{0:T(128)} %bitcast.9.me_ref, ...), custom_call_target="tpu_custom_call" | custom-call | bytes 4325376 | tf_op jit(solution)/shard_map/pallas_call | solution.py:200
  21.3 55.4 %conditional.3 = (bf16[8,4096]{1,0:T(8,128)(2,1)S(1)}, f32[8,4096]{1,0:T(8,128)S(1)}, f32[8,4096]{1,0:T(8,128)S(1)}, f32[8,4096]{1,0:T(8,128)S(1)}) conditional(s32[]{:T(128)} %bitcast.13, (s32[]{:T(128)}, s32[8]{0:T(128)S(1)}, f32[64,128]{1,0:T(8,128)S(1)}, f32[64,128]{1,0:T(8,128)S(1)}, s32[8,64]{1,0:T(8,128)S(1)}, ...), branch_computations={%region_0.1_spmd, %region_1.2_spmd, %region_2.3_spmd} | conditional | flops 3724640256 | bytes 92963672
  22.5 1.3 %collective-permute-start = (bf16[128,1024]{1,0:T(8,128)(2,1)S(1)}, bf16[128,1024]{1,0:T(8,128)(2,1)S(1)}, u32[]{:S(2)}, u32[]{:S(2)}) collective-permute-start(bf16[128,1024]{1,0:T(8,128)(2,1)S(1)} %get-tuple-element.143), channel_id=1, source_target_pairs={{0,2},{2,0},{4,6},{6,4},{8,10},{10,8},{12,14},{14,12},{1,3},{3,1},... | collective-permute-start | bytes 786440 | tf_op jit(solution)/shard_map/cond/branch_0_fun/ppermute | solution.py:586
  23.7 6.3 %branch_0_fun.11 = bf16[2,64,1024]{2,1,0:T(8,128)(2,1)S(1)} custom-call(s32[1]{0:T(128)S(6)} %sub.33.side_ref, bf16[64,4096]{1,0:T(8,128)(2,1)S(1)} %get-tuple-element.149.x_ref, bf16[4096,2048]{1,0:T(8,128)(2,1)} %get-tuple-element.141.gate_ref, bf16[4096,2048]{1,0:T(8,128)(2,1)} %get-tuple-element.142.up_ref), custom_call_target="tpu_custom_call" | custom-call | flops 1073741824 | bytes 17301504 | tf_op jit(solution)/shard_map/cond/branch_0_fun/pallas_call | solution.py:305
  31.7 1.3 %collective-permute-start.7 = (bf16[64,4096]{1,0:T(8,128)(2,1)S(1)}, bf16[64,4096]{1,0:T(8,128)(2,1)S(1)}, u32[]{:S(2)}, u32[]{:S(2)}) collective-permute-start(bf16[64,4096]{1,0:T(8,128)(2,1)S(1)} %bitcast.19), channel_id=1, source_target_pairs={{0,2},{2,0},{4,6},{6,4},{8,10},{10,8},{12,14},{14,12},{1,3},{3,1},... | collective-permute-start | bytes 1572872 | tf_op jit(solution)/shard_map/cond/branch_0_fun/ppermute | solution.py:592
  33.4 3.5 %collective-permute-start.3 = (bf16[48,1024]{1,0:T(8,128)(2,1)S(1)}, bf16[48,1024]{1,0:T(8,128)(2,1)S(1)}, u32[]{:S(2)}, u32[]{:S(2)}) collective-permute-start(bf16[48,1024]{1,0:T(8,128)(2,1)S(1)} %get-tuple-element.153), channel_id=1, source_target_pairs={{0,8},{2,10},{4,12},{6,14},{8,0},{10,2},{12,4},{14,6},{1,9},{3,11}... | collective-permute-start | bytes 294920 | tf_op jit(solution)/shard_map/cond/branch_0_fun/ppermute | solution.py:92
  36.9 6.2 %branch_0_fun.13.own_ref = f32[2,64,1024]{2,1,0:T(8,128)S(1)} custom-call(s32[1]{0:T(128)} %bitcast.side_ref.core_ref, bf16[64,4096]{1,0:T(8,128)(2,1)S(1)} %get-tuple-element.149.x_ref, bf16[4096,2048]{1,0:T(8,128)(2,1)} %get-tuple-element.141.gate_ref, bf16[4096,2048]{1,0:T(8,128)(2,1)} %get-tuple-element.142.up_ref), custom_call_target="tpu_custom_call" | custom-call | flops 1073741824 | bytes 17301504 | tf_op jit(solution)/shard_map/cond/branch_0_fun/pallas_call | solution.py:305
  45.2 1.3 %collective-permute-start.6 = (bf16[64,1024]{1,0:T(8,128)(2,1)S(1)}, bf16[64,1024]{1,0:T(8,128)(2,1)S(1)}, u32[]{:S(2)}, u32[]{:S(2)}) collective-permute-start(bf16[64,1024]{1,0:T(8,128)(2,1)S(1)} %get-tuple-element.160), channel_id=1, source_target_pairs={{0,2},{2,0},{4,6},{6,4},{8,10},{10,8},{12,14},{14,12},{1,3},{3,1},... | collective-permute-start | bytes 393224 | tf_op jit(solution)/shard_map/cond/branch_0_fun/ppermute | solution.py:607
  46.5 4.2 %branch_0_fun.15 = (f32[32,2048]{1,0:T(8,128)S(1)}, bf16[32,2048]{1,0:T(8,128)(2,1)S(1)}) custom-call(s32[1]{0:T(128)} %bitcast.side_ref.core_ref, bf16[64,1024]{1,0:T(8,128)(2,1)S(1)} %get-tuple-element.167.near_ref, bf16[64,1024]{1,0:T(8,128)(2,1)S(1)} %collective-permute-done.5.far_ref, bf16[2048,4096]{1,0:T(8,128)(2,1)} %get-tuple-element.156.weight_ref), custom_call_target="tpu_custom_call" | custom-call | flops 536870912 | bytes 8912896 | tf_op jit(solution)/shard_map/cond/branch_0_fun/pallas_call | solution.py:434
  51.1 1.2 %collective-permute-start.8 = (bf16[32,2048]{1,0:T(8,128)(2,1)S(1)}, bf16[32,2048]{1,0:T(8,128)(2,1)S(1)}, u32[]{:S(2)}, u32[]{:S(2)}) collective-permute-start(bf16[32,2048]{1,0:T(8,128)(2,1)S(1)} %get-tuple-element.170), channel_id=1, source_target_pairs={{0,2},{2,0},{4,6},{6,4},{8,10},{10,8},{12,14},{14,12},{1,3},{3,1},... | collective-permute-start | bytes 393224 | tf_op jit(solution)/shard_map/cond/branch_0_fun/ppermute | solution.py:610
  52.3 2.7 %collective-permute-start.9 = (bf16[32,1024]{1,0:T(8,128)(2,1)S(1)}, bf16[32,1024]{1,0:T(8,128)(2,1)S(1)}, u32[]{:S(2)}, u32[]{:S(2)}) collective-permute-start(bf16[32,1024]{1,0:T(8,128)(2,1)S(1)} %get-tuple-element.172), channel_id=1, source_target_pairs={{0,4},{2,6},{4,8},{6,10},{8,12},{10,14},{12,0},{14,2},{1,5},{3,7},... | collective-permute-start | bytes 196616 | tf_op jit(solution)/shard_map/cond/branch_0_fun/ppermute | solution.py:92
  55.6 1.9 %collective-permute-start.11 = (bf16[32,1024]{1,0:T(8,128)(2,1)S(1)}, bf16[32,1024]{1,0:T(8,128)(2,1)S(1)}, u32[]{:S(2)}, u32[]{:S(2)}) collective-permute-start(bf16[32,1024]{1,0:T(8,128)(2,1)S(1)} %get-tuple-element.174), channel_id=1, source_target_pairs={{0,12},{2,14},{4,0},{6,2},{8,4},{10,6},{12,8},{14,10},{1,13},{3,15... | collective-permute-start | bytes 196616 | tf_op jit(solution)/shard_map/cond/branch_0_fun/ppermute | solution.py:92
  57.5 4.0 %branch_0_fun.17 = (f32[32,2048]{1,0:T(8,128)S(1)}, bf16[32,2048]{1,0:T(8,128)(2,1)S(1)}) custom-call(s32[1]{0:T(128)} %bitcast.side_ref.core_ref, bf16[64,1024]{1,0:T(8,128)(2,1)S(1)} %get-tuple-element.167.near_ref, bf16[64,1024]{1,0:T(8,128)(2,1)S(1)} %collective-permute-done.5.far_ref, bf16[2048,4096]{1,0:T(8,128)(2,1)} %get-tuple-element.156.weight_ref), custom_call_target="tpu_custom_call" | custom-call | flops 536870912 | bytes 8912896 | tf_op jit(solution)/shard_map/cond/branch_0_fun/pallas_call | solution.py:434
  63.3 1.3 %collective-permute-start.14 = (f32[16,64]{1,0:T(8,128)S(1)}, f32[16,64]{1,0:T(8,128)S(1)}, u32[]{:S(2)}, u32[]{:S(2)}) collective-permute-start(f32[16,64]{1,0:T(8,128)S(1)} %branch_0_fun.18.refs_4_), channel_id=1, source_target_pairs={{0,2},{2,0},{4,6},{6,4},{8,10},{10,8},{12,14},{14,12},{1,3},{3,1},... | collective-permute-start | bytes 12296 | tf_op jit(solution)/shard_map/cond/branch_0_fun/ppermute | solution.py:628
  65.2 1.3 %collective-permute-done.15.refs_7_ = f32[16,64]{1,0:T(8,128)S(1)} collective-permute-done((f32[16,64]{1,0:T(8,128)S(1)}, f32[16,64]{1,0:T(8,128)S(1)}, u32[]{:S(2)}, u32[]{:S(2)}) %collective-permute-start.15) | collective-permute-done | bytes 4128 | tf_op jit(solution)/shard_map/cond/branch_0_fun/ppermute | solution.py:632
  67.6 1.9 %collective-permute-start.16 = (bf16[8,4096]{1,0:T(8,128)(2,1)S(1)}, bf16[8,4096]{1,0:T(8,128)(2,1)S(1)}, u32[]{:S(2)}, u32[]{:S(2)}) collective-permute-start(bf16[8,4096]{1,0:T(8,128)(2,1)S(1)} %get-tuple-element.190), channel_id=1, source_target_pairs={{0,4},{2,6},{4,8},{6,10},{8,12},{10,14},{12,0},{14,2},{1,5},{3,7},... | collective-permute-start | bytes 196616 | tf_op jit(solution)/shard_map/cond/branch_0_fun/ppermute | solution.py:92
  70.5 1.5 %collective-permute-start.18 = (bf16[8,4096]{1,0:T(8,128)(2,1)S(1)}, bf16[8,4096]{1,0:T(8,128)(2,1)S(1)}, u32[]{:S(2)}, u32[]{:S(2)}) collective-permute-start(bf16[8,4096]{1,0:T(8,128)(2,1)S(1)} %get-tuple-element.192), channel_id=1, source_target_pairs={{0,12},{2,14},{4,0},{6,2},{8,4},{10,6},{12,8},{14,10},{1,13},{3,15... | collective-permute-start | bytes 196616 | tf_op jit(solution)/shard_map/cond/branch_0_fun/ppermute | solution.py:92
  71.9 2.5 %collective-permute-done.16 = bf16[8,4096]{1,0:T(8,128)(2,1)S(1)} collective-permute-done((bf16[8,4096]{1,0:T(8,128)(2,1)S(1)}, bf16[8,4096]{1,0:T(8,128)(2,1)S(1)}, u32[]{:S(2)}, u32[]{:S(2)}) %collective-permute-start.16) | collective-permute-done | bytes 65568 | tf_op jit(solution)/shard_map/cond/branch_0_fun/ppermute | solution.py:92
  74.4 2.1 %collective-permute-done.17 = bf16[8,4096]{1,0:T(8,128)(2,1)S(1)} collective-permute-done((bf16[8,4096]{1,0:T(8,128)(2,1)S(1)}, bf16[8,4096]{1,0:T(8,128)(2,1)S(1)}, u32[]{:S(2)}, u32[]{:S(2)}) %collective-permute-start.17) | collective-permute-done | bytes 65568 | tf_op jit(solution)/shard_map/cond/branch_0_fun/ppermute | solution.py:92
  (65 shorter events, 19.1 us)
Async XLA Ops:
  0.0 12.9 %collective-permute-start.57 = (bf16[64,16384]{1,0:T(8,128)(2,1)}, bf16[64,16384]{1,0:T(8,128)(2,1)S(1)}, u32[]{:S(2)}, u32[]{:S(2)}) collective-permute-start(bf16[64,16384]{1,0:T(8,128)(2,1)} %bitcast.25), channel_id=1, source_target_pairs={{0,1},{1,0},{2,3},{3,2},{4,5},{5,4},{6,7},{7,6},{8,9},{9,8},{10,11... | collective-permute-start | bytes 6291464 | tf_op jit(solution)/shard_map/ppermute | solution.py:546
  0.5 9.1 %collective-permute-start.59 = (bf16[8,4096]{1,0:T(8,128)(2,1)}, bf16[8,4096]{1,0:T(8,128)(2,1)S(1)}, u32[]{:S(2)}, u32[]{:S(2)}) collective-permute-start(bf16[8,4096]{1,0:T(8,128)(2,1)} %x_ref.1), channel_id=1, source_target_pairs={{0,8},{2,10},{4,12},{6,14},{8,0},{10,2},{12,4},{14,6},{1,9},{3,11}... | collective-permute-start | bytes 196616 | tf_op jit(solution)/shard_map/ppermute | solution.py:79
  4.0 8.9 %collective-permute-start.58 = (bf16[8,4096]{1,0:T(8,128)(2,1)}, bf16[8,4096]{1,0:T(8,128)(2,1)S(1)}, u32[]{:S(2)}, u32[]{:S(2)}) collective-permute-start(bf16[8,4096]{1,0:T(8,128)(2,1)} %x_ref.1), channel_id=1, source_target_pairs={{0,4},{2,6},{4,8},{6,10},{8,12},{10,14},{12,0},{14,2},{1,5},{3,7},... | collective-permute-start | bytes 196616 | tf_op jit(solution)/shard_map/ppermute | solution.py:79
  5.6 13.3 %collective-permute-start.61 = (bf16[8,4096]{1,0:T(8,128)(2,1)}, bf16[8,4096]{1,0:T(8,128)(2,1)S(1)}, u32[]{:S(2)}, u32[]{:S(2)}) collective-permute-start(bf16[8,4096]{1,0:T(8,128)(2,1)} %x_ref.1), channel_id=1, source_target_pairs={{0,2},{2,0},{4,6},{6,4},{8,10},{10,8},{12,14},{14,12},{1,3},{3,1},... | collective-permute-start | bytes 196616 | tf_op jit(solution)/shard_map/ppermute | solution.py:83
  7.1 4.6 %collective-permute-start.60 = (bf16[8,4096]{1,0:T(8,128)(2,1)}, bf16[8,4096]{1,0:T(8,128)(2,1)S(1)}, u32[]{:S(2)}, u32[]{:S(2)}) collective-permute-start(bf16[8,4096]{1,0:T(8,128)(2,1)} %x_ref.1), channel_id=1, source_target_pairs={{0,12},{2,14},{4,0},{6,2},{8,4},{10,6},{12,8},{14,10},{1,13},{3,15... | collective-permute-start | bytes 196616 | tf_op jit(solution)/shard_map/ppermute | solution.py:79
  9.5 9.4 %collective-permute-start.63 = (bf16[8,4096]{1,0:T(8,128)(2,1)S(1)}, bf16[8,4096]{1,0:T(8,128)(2,1)S(1)}, u32[]{:S(2)}, u32[]{:S(2)}) collective-permute-start(bf16[8,4096]{1,0:T(8,128)(2,1)S(1)} %collective-permute-done.59.refs_4_), channel_id=1, source_target_pairs={{0,2},{2,0},{4,6},{6,4},{8,10},{10,8},{12,14},{14,12},{1,3},{3,1},... | collective-permute-start | bytes 196616 | tf_op jit(solution)/shard_map/ppermute | solution.py:83
  11.7 7.2 %collective-permute-start.64 = (bf16[8,4096]{1,0:T(8,128)(2,1)S(1)}, bf16[8,4096]{1,0:T(8,128)(2,1)S(1)}, u32[]{:S(2)}, u32[]{:S(2)}) collective-permute-start(bf16[8,4096]{1,0:T(8,128)(2,1)S(1)} %collective-permute-done.60.refs_5_), channel_id=1, source_target_pairs={{0,2},{2,0},{4,6},{6,4},{8,10},{10,8},{12,14},{14,12},{1,3},{3,1},... | collective-permute-start | bytes 196616 | tf_op jit(solution)/shard_map/ppermute | solution.py:83
  12.9 6.0 %collective-permute-start.62 = (bf16[8,4096]{1,0:T(8,128)(2,1)S(1)}, bf16[8,4096]{1,0:T(8,128)(2,1)S(1)}, u32[]{:S(2)}, u32[]{:S(2)}) collective-permute-start(bf16[8,4096]{1,0:T(8,128)(2,1)S(1)} %collective-permute-done.58.refs_3_), channel_id=1, source_target_pairs={{0,2},{2,0},{4,6},{6,4},{8,10},{10,8},{12,14},{14,12},{1,3},{3,1},... | collective-permute-start | bytes 196616 | tf_op jit(solution)/shard_map/ppermute | solution.py:83
  22.5 8.4 %collective-permute-start = (bf16[128,1024]{1,0:T(8,128)(2,1)S(1)}, bf16[128,1024]{1,0:T(8,128)(2,1)S(1)}, u32[]{:S(2)}, u32[]{:S(2)}) collective-permute-start(bf16[128,1024]{1,0:T(8,128)(2,1)S(1)} %get-tuple-element.143), channel_id=1, source_target_pairs={{0,2},{2,0},{4,6},{6,4},{8,10},{10,8},{12,14},{14,12},{1,3},{3,1},... | collective-permute-start | bytes 786440 | tf_op jit(solution)/shard_map/cond/branch_0_fun/ppermute | solution.py:586
  31.7 19.4 %collective-permute-start.7 = (bf16[64,4096]{1,0:T(8,128)(2,1)S(1)}, bf16[64,4096]{1,0:T(8,128)(2,1)S(1)}, u32[]{:S(2)}, u32[]{:S(2)}) collective-permute-start(bf16[64,4096]{1,0:T(8,128)(2,1)S(1)} %bitcast.19), channel_id=1, source_target_pairs={{0,2},{2,0},{4,6},{6,4},{8,10},{10,8},{12,14},{14,12},{1,3},{3,1},... | collective-permute-start | bytes 1572872 | tf_op jit(solution)/shard_map/cond/branch_0_fun/ppermute | solution.py:592
  33.0 11.3 %collective-permute-start.1 = (bf16[2,64,1024]{2,1,0:T(8,128)(2,1)S(1)}, bf16[2,64,1024]{2,1,0:T(8,128)(2,1)S(1)}, u32[]{:S(2)}, u32[]{:S(2)}) collective-permute-start(bf16[2,64,1024]{2,1,0:T(8,128)(2,1)S(1)} %branch_0_fun.11), channel_id=1, source_target_pairs={{0,1},{1,0},{2,3},{3,2},{4,5},{5,4},{6,7},{7,6},{8,9},{9,8},{10,11... | collective-permute-start | bytes 786440 | tf_op jit(solution)/shard_map/cond/branch_0_fun/ppermute | solution.py:546
  33.0 10.2 %collective-permute-start.2 = (bf16[48,1024]{1,0:T(8,128)(2,1)S(1)}, bf16[48,1024]{1,0:T(8,128)(2,1)S(1)}, u32[]{:S(2)}, u32[]{:S(2)}) collective-permute-start(bf16[48,1024]{1,0:T(8,128)(2,1)S(1)} %get-tuple-element.152), channel_id=1, source_target_pairs={{0,4},{2,6},{4,8},{6,10},{8,12},{10,14},{12,0},{14,2},{1,5},{3,7},... | collective-permute-start | bytes 294920 | tf_op jit(solution)/shard_map/cond/branch_0_fun/ppermute | solution.py:92
  33.4 10.8 %collective-permute-start.3 = (bf16[48,1024]{1,0:T(8,128)(2,1)S(1)}, bf16[48,1024]{1,0:T(8,128)(2,1)S(1)}, u32[]{:S(2)}, u32[]{:S(2)}) collective-permute-start(bf16[48,1024]{1,0:T(8,128)(2,1)S(1)} %get-tuple-element.153), channel_id=1, source_target_pairs={{0,8},{2,10},{4,12},{6,14},{8,0},{10,2},{12,4},{14,6},{1,9},{3,11}... | collective-permute-start | bytes 294920 | tf_op jit(solution)/shard_map/cond/branch_0_fun/ppermute | solution.py:92
  36.9 7.3 %collective-permute-start.4 = (bf16[48,1024]{1,0:T(8,128)(2,1)S(1)}, bf16[48,1024]{1,0:T(8,128)(2,1)S(1)}, u32[]{:S(2)}, u32[]{:S(2)}) collective-permute-start(bf16[48,1024]{1,0:T(8,128)(2,1)S(1)} %get-tuple-element.154), channel_id=1, source_target_pairs={{0,12},{2,14},{4,0},{6,2},{8,4},{10,6},{12,8},{14,10},{1,13},{3,15... | collective-permute-start | bytes 294920 | tf_op jit(solution)/shard_map/cond/branch_0_fun/ppermute | solution.py:92
  45.2 5.9 %collective-permute-start.6 = (bf16[64,1024]{1,0:T(8,128)(2,1)S(1)}, bf16[64,1024]{1,0:T(8,128)(2,1)S(1)}, u32[]{:S(2)}, u32[]{:S(2)}) collective-permute-start(bf16[64,1024]{1,0:T(8,128)(2,1)S(1)} %get-tuple-element.160), channel_id=1, source_target_pairs={{0,2},{2,0},{4,6},{6,4},{8,10},{10,8},{12,14},{14,12},{1,3},{3,1},... | collective-permute-start | bytes 393224 | tf_op jit(solution)/shard_map/cond/branch_0_fun/ppermute | solution.py:607
  51.1 10.4 %collective-permute-start.8 = (bf16[32,2048]{1,0:T(8,128)(2,1)S(1)}, bf16[32,2048]{1,0:T(8,128)(2,1)S(1)}, u32[]{:S(2)}, u32[]{:S(2)}) collective-permute-start(bf16[32,2048]{1,0:T(8,128)(2,1)S(1)} %get-tuple-element.170), channel_id=1, source_target_pairs={{0,2},{2,0},{4,6},{6,4},{8,10},{10,8},{12,14},{14,12},{1,3},{3,1},... | collective-permute-start | bytes 393224 | tf_op jit(solution)/shard_map/cond/branch_0_fun/ppermute | solution.py:610
  52.3 9.1 %collective-permute-start.9 = (bf16[32,1024]{1,0:T(8,128)(2,1)S(1)}, bf16[32,1024]{1,0:T(8,128)(2,1)S(1)}, u32[]{:S(2)}, u32[]{:S(2)}) collective-permute-start(bf16[32,1024]{1,0:T(8,128)(2,1)S(1)} %get-tuple-element.172), channel_id=1, source_target_pairs={{0,4},{2,6},{4,8},{6,10},{8,12},{10,14},{12,0},{14,2},{1,5},{3,7},... | collective-permute-start | bytes 196616 | tf_op jit(solution)/shard_map/cond/branch_0_fun/ppermute | solution.py:92
  55.0 6.5 %collective-permute-start.10 = (bf16[32,1024]{1,0:T(8,128)(2,1)S(1)}, bf16[32,1024]{1,0:T(8,128)(2,1)S(1)}, u32[]{:S(2)}, u32[]{:S(2)}) collective-permute-start(bf16[32,1024]{1,0:T(8,128)(2,1)S(1)} %get-tuple-element.173), channel_id=1, source_target_pairs={{0,8},{2,10},{4,12},{6,14},{8,0},{10,2},{12,4},{14,6},{1,9},{3,11}... | collective-permute-start | bytes 196616 | tf_op jit(solution)/shard_map/cond/branch_0_fun/ppermute | solution.py:92
  55.6 5.9 %collective-permute-start.11 = (bf16[32,1024]{1,0:T(8,128)(2,1)S(1)}, bf16[32,1024]{1,0:T(8,128)(2,1)S(1)}, u32[]{:S(2)}, u32[]{:S(2)}) collective-permute-start(bf16[32,1024]{1,0:T(8,128)(2,1)S(1)} %get-tuple-element.174), channel_id=1, source_target_pairs={{0,12},{2,14},{4,0},{6,2},{8,4},{10,6},{12,8},{14,10},{1,13},{3,15... | collective-permute-start | bytes 196616 | tf_op jit(solution)/shard_map/cond/branch_0_fun/ppermute | solution.py:92
  61.5 5.5 %collective-permute-start.12 = (bf16[32,2048]{1,0:T(8,128)(2,1)S(1)}, bf16[32,2048]{1,0:T(8,128)(2,1)S(1)}, u32[]{:S(2)}, u32[]{:S(2)}) collective-permute-start(bf16[32,2048]{1,0:T(8,128)(2,1)S(1)} %get-tuple-element.181), channel_id=1, source_target_pairs={{0,2},{2,0},{4,6},{6,4},{8,10},{10,8},{12,14},{14,12},{1,3},{3,1},... | collective-permute-start | bytes 393224 | tf_op jit(solution)/shard_map/cond/branch_0_fun/ppermute | solution.py:617
  63.3 3.7 %collective-permute-start.14 = (f32[16,64]{1,0:T(8,128)S(1)}, f32[16,64]{1,0:T(8,128)S(1)}, u32[]{:S(2)}, u32[]{:S(2)}) collective-permute-start(f32[16,64]{1,0:T(8,128)S(1)} %branch_0_fun.18.refs_4_), channel_id=1, source_target_pairs={{0,2},{2,0},{4,6},{6,4},{8,10},{10,8},{12,14},{14,12},{1,3},{3,1},... | collective-permute-start | bytes 12296 | tf_op jit(solution)/shard_map/cond/branch_0_fun/ppermute | solution.py:628
  67.6 6.8 %collective-permute-start.16 = (bf16[8,4096]{1,0:T(8,128)(2,1)S(1)}, bf16[8,4096]{1,0:T(8,128)(2,1)S(1)}, u32[]{:S(2)}, u32[]{:S(2)}) collective-permute-start(bf16[8,4096]{1,0:T(8,128)(2,1)S(1)} %get-tuple-element.190), channel_id=1, source_target_pairs={{0,4},{2,6},{4,8},{6,10},{8,12},{10,14},{12,0},{14,2},{1,5},{3,7},... | collective-permute-start | bytes 196616 | tf_op jit(solution)/shard_map/cond/branch_0_fun/ppermute | solution.py:92
  69.5 7.0 %collective-permute-start.17 = (bf16[8,4096]{1,0:T(8,128)(2,1)S(1)}, bf16[8,4096]{1,0:T(8,128)(2,1)S(1)}, u32[]{:S(2)}, u32[]{:S(2)}) collective-permute-start(bf16[8,4096]{1,0:T(8,128)(2,1)S(1)} %get-tuple-element.191), channel_id=1, source_target_pairs={{0,8},{2,10},{4,12},{6,14},{8,0},{10,2},{12,4},{14,6},{1,9},{3,11}... | collective-permute-start | bytes 196616 | tf_op jit(solution)/shard_map/cond/branch_0_fun/ppermute | solution.py:92
  70.5 6.0 %collective-permute-start.18 = (bf16[8,4096]{1,0:T(8,128)(2,1)S(1)}, bf16[8,4096]{1,0:T(8,128)(2,1)S(1)}, u32[]{:S(2)}, u32[]{:S(2)}) collective-permute-start(bf16[8,4096]{1,0:T(8,128)(2,1)S(1)} %get-tuple-element.192), channel_id=1, source_target_pairs={{0,12},{2,14},{4,0},{6,2},{8,4},{10,6},{12,8},{14,10},{1,13},{3,15... | collective-permute-start | bytes 196616 | tf_op jit(solution)/shard_map/cond/branch_0_fun/ppermute | solution.py:92
  (9 other events, 34.3 us)

commit v7 on v6

--- a/solution.py
+++ b/solution.py
@@ -72,16 +72,16 @@
         S, F = self.slow, self.fast
         return [(s * F + f, (s - a) % S * F + (f - c) % F) for s in range(S) for f in range(F)]
 
-    def gather(self, block, other):
+    def gather(self, block, *others):
         if not self.direct:
-            return list(lax.all_gather(block, "ff")), other
+            return list(lax.all_gather(block, "ff")), *others
         got = [block] + [
             lax.ppermute(block, "ff", self.back(-a, 0)) for a in range(1, self.slow)
         ]
-        other, got[1] = tied(other, got[1])
+        got[1], *others = tied(got[1], *others)
         for c in range(1, self.fast):
             got += [lax.ppermute(part, "ff", self.back(0, -c)) for part in got[: self.slow]]
-        return got, other
+        return got, *others
 
     def spread(self, blocks):
         return lax.all_to_all(blocks, "ff", 0, 0, tiled=True)
@@ -99,8 +99,7 @@
     order_ref,
     me_ref,
     at_ref,
-    slot_ref,
-    ids_ref,
+    named_ref,
     x_ref,
     shrink_ref,
     expand_ref,
@@ -125,7 +124,7 @@
         copies.append(pltpu.make_async_copy(expand_ref.at[:, columns], put, sems.at[2 + b]))
     for copy in copies:
         copy.start()
-    rows, variants = ids_ref.shape[1], slot_ref.shape[0]
+    rows, size = in_ref.shape[0], named_ref.shape[1]
     own_rows = rows // shards
     me = me_ref[0].astype(F32)
     order = [order_ref[b].astype(F32) for b in range(shards)]
@@ -145,11 +144,13 @@
         at_down = jnp.where(
             (line[:, :1] >= low) & (line[:, :1] < high), line[:, :1] + shift, at_down
         )
-    ids = across(jnp.where(lane == at_down, ids_ref[...].astype(F32), 0.0))
+    named = named_ref[...].astype(F32)
+    ids = across(jnp.where(count((rows, size), 1) == at_down, named, 0.0))
     ids = along(jnp.where(diagonal, ids, 0.0))
-    slot = jnp.zeros_like(ids)
-    for v in range(variants):
-        slot = jnp.where(ids == float(v), slot_ref[v].astype(F32), slot)
+    variants = size - rows
+    of_variant = count((variants, size), 1) == count((variants, size), 0) + rows
+    slots_down = across(jnp.where(of_variant, named, 0.0))
+    slot = along(jnp.where(count((variants, rows), 0) == ids, slots_down, 0.0))
     slot_down = across(jnp.where(diagonal, slot, 0.0))
     owner_of = lambda a: sum((a >= float(o * slots)).astype(F32) for o in range(1, shards))
     owner, owner_down = owner_of(slot), owner_of(slot_down)
@@ -193,8 +194,7 @@
         copy.wait()
 
 
-def tables(ways, me, at, ids, variant_slot, x, shrink, expand, slots, rank):
-    rows = ids.shape[1]
+def tables(ways, me, at, named, x, shrink, expand, rows, slots, rank):
     shards = at.shape[0]
     depth, width = expand.shape
     return pl.pallas_call(
@@ -208,12 +208,12 @@
             jax.ShapeDtypeStruct(shrink.shape, BF),
             jax.ShapeDtypeStruct((depth, width // 2), BF),
         ),
-        in_specs=[SCALARS] * 4 + [WHOLE] + [FAR] * 3,
+        in_specs=[SCALARS] * 3 + [WHOLE] + [FAR] * 3,
         out_specs=(WHOLE, WHOLE, WHOLE, SCALARS, WHOLE, WHOLE, WHOLE),
         scratch_shapes=[pltpu.SemaphoreType.DMA((2 + shards,))],
         compiler_params=params(52),
         cost_estimate=cost(0, 4 * x.size + 4 * shrink.size + 2 * expand.size),
-    )(ways.order, me, at, variant_slot, ids, x, shrink, expand)
+    )(ways.order, me, at, named, x, shrink, expand)
 
 
 def low_in_kernel(count, shrink_ref, mask_ref, *refs):
@@ -546,17 +546,18 @@
     swap = lambda a: lax.ppermute(a, "var", [(0, 1), (1, 0)])
 
     near = expand_gu.reshape(slots * 2 * half_rank, -1)
-    token_parts, far = ways.gather(tokens, swap(near))
+    named = jnp.concatenate([variant_ids[:, 0], variant_slot]).reshape(1, -1)
+    token_parts, far, named = ways.gather(tokens, swap(near), named)
     shrink_in = shrink_gu.reshape(slots * 2 * rank, width)
     marks, mask_in, slot_mask, facts, token_parts[0], shrink_in, near = tables(
         ways,
         me.reshape(1),
         at_here,
-        variant_ids.reshape(1, rows),
-        variant_slot,
+        named,
         token_parts[0],
         shrink_in,
         near,
+        rows,
         slots,
         rank,
     )

time: 77.6 us -> 76.2 us (0.982)
  local copies, waits for them, and re-layouts: 2.15 us -> 0.84 us
    unnamed x10 -> x6, local copies, waits for them, and re-layouts: 2.15 us -> 0.84 us
  transfers between devices with their start and end apart: 28 -> 28, of which waited for: 9 -> 9; matrix products, arithmetic and copies ran while one was open for 0% -> 1% of each run, Pallas kernels for 33% -> 33%
where the time goes in v7:
time: 76.2 us; the launch traced here: 76 us
  starting transfers between devices  33.2 us (44%)
  Pallas kernels  28.9 us (38%)
  waiting for transfers between devices  10.8 us (14%)
  other arithmetic  1.66 us (2%)
  local copies, waits for them, and re-layouts  0.84 us (1%)
    ppermute x9, starting transfers between devices, slow_steps(): got[-a % self.slow] = lax.ppermute(blocks[a], 'ff', self.back(a, 0))  13.4 us
    pallas_call x2, Pallas kernels, base_half(): pl.pallas_call(base_kernel, out_shape=jax.ShapeDtypeStruct((2, rows, half...  12.5 us
    pallas_call x2, Pallas kernels, down_base(): pl.pallas_call(functools.partial(down_kernel, start), out_shape=outs, in_...  8.17 us
    ppermute x3, starting transfers between devices, gather(): lax.ppermute(block, 'ff', self.back(-a, 0))  7.41 us
    ppermute x9, waiting for transfers between devices, slow_steps(): got[-a % self.slow] = lax.ppermute(blocks[a], 'ff', self.back(a, 0))  5.62 us
    ppermute x4, starting transfers between devices, gather(): lax.ppermute(part, 'ff', self.back(0, -c))  4.05 us
    pallas_call x1, Pallas kernels, tables(): pl.pallas_call(functools.partial(tables_kernel, ways, slots), out_shape=(...  2.89 us
  transfers between devices with their start and end apart: 28, of which 9 were waited for; matrix products, arithmetic and copies ran while one was open for 1% of the time, Pallas kernels for 33%

profile of v7, /device:TPU:0, one launch (start us, length us, event | category | flops | bytes accessed | tf_op | source)
XLA Modules:
  0.0 76.0 jit_solution(928128730064913969)
XLA Ops:
  0.5 3.6 %collective-permute-start.59 = (bf16[8,4096]{1,0:T(8,128)(2,1)}, bf16[8,4096]{1,0:T(8,128)(2,1)S(1)}, u32[]{:S(2)}, u32[]{:S(2)}) collective-permute-start(bf16[8,4096]{1,0:T(8,128)(2,1)} %x_ref.1), channel_id=1, source_target_pairs={{0,8},{2,10},{4,12},{6,14},{8,0},{10,2},{12,4},{14,6},{1,9},{3,11}... | collective-permute-start | bytes 196616 | tf_op jit(solution)/shard_map/ppermute | solution.py:79
  4.0 1.6 %collective-permute-start.57 = (bf16[8,4096]{1,0:T(8,128)(2,1)}, bf16[8,4096]{1,0:T(8,128)(2,1)S(1)}, u32[]{:S(2)}, u32[]{:S(2)}) collective-permute-start(bf16[8,4096]{1,0:T(8,128)(2,1)} %x_ref.1), channel_id=1, source_target_pairs={{0,4},{2,6},{4,8},{6,10},{8,12},{10,14},{12,0},{14,2},{1,5},{3,7},... | collective-permute-start | bytes 196616 | tf_op jit(solution)/shard_map/ppermute | solution.py:79
  5.6 1.5 %collective-permute-start.61 = (bf16[8,4096]{1,0:T(8,128)(2,1)}, bf16[8,4096]{1,0:T(8,128)(2,1)S(1)}, u32[]{:S(2)}, u32[]{:S(2)}) collective-permute-start(bf16[8,4096]{1,0:T(8,128)(2,1)} %x_ref.1), channel_id=1, source_target_pairs={{0,2},{2,0},{4,6},{6,4},{8,10},{10,8},{12,14},{14,12},{1,3},{3,1},... | collective-permute-start | bytes 196616 | tf_op jit(solution)/shard_map/ppermute | solution.py:83
  7.1 2.2 %collective-permute-start.60 = (bf16[8,4096]{1,0:T(8,128)(2,1)}, bf16[8,4096]{1,0:T(8,128)(2,1)S(1)}, u32[]{:S(2)}, u32[]{:S(2)}) collective-permute-start(bf16[8,4096]{1,0:T(8,128)(2,1)} %x_ref.1), channel_id=1, source_target_pairs={{0,12},{2,14},{4,0},{6,2},{8,4},{10,6},{12,8},{14,10},{1,13},{3,15... | collective-permute-start | bytes 196616 | tf_op jit(solution)/shard_map/ppermute | solution.py:79
  11.7 1.2 %collective-permute-start.64 = (bf16[8,4096]{1,0:T(8,128)(2,1)S(1)}, bf16[8,4096]{1,0:T(8,128)(2,1)S(1)}, u32[]{:S(2)}, u32[]{:S(2)}) collective-permute-start(bf16[8,4096]{1,0:T(8,128)(2,1)S(1)} %collective-permute-done.60.refs_5_), channel_id=1, source_target_pairs={{0,2},{2,0},{4,6},{6,4},{8,10},{10,8},{12,14},{14,12},{1,3},{3,1},... | collective-permute-start | bytes 196616 | tf_op jit(solution)/shard_map/ppermute | solution.py:83
  14.6 2.9 %shard_map.100 = (s32[8,64]{1,0:T(8,128)S(1)}, f32[64,128]{1,0:T(8,128)S(1)}, bf16[64,64]{1,0:T(8,128)(2,1)S(1)}, s32[3]{0:T(128)S(1)}, bf16[8,4096]{1,0:T(8,128...) custom-call(s32[8]{0:T(128)S(1)} %get-tuple-element.370.order_ref, s32[1]{0:T(128)} %bitcast.9.me_ref, ...), custom_call_target="tpu_custom_call" | custom-call | bytes 4325376 | tf_op jit(solution)/shard_map/pallas_call | solution.py:200
  19.9 55.4 %conditional.3 = (bf16[8,4096]{1,0:T(8,128)(2,1)S(1)}, f32[8,4096]{1,0:T(8,128)S(1)}, f32[8,4096]{1,0:T(8,128)S(1)}, f32[8,4096]{1,0:T(8,128)S(1)}) conditional(s32[]{:T(128)} %bitcast.14, (s32[]{:T(128)}, s32[8]{0:T(128)S(1)}, f32[64,128]{1,0:T(8,128)S(1)}, f32[64,128]{1,0:T(8,128)S(1)}, s32[8,64]{1,0:T(8,128)S(1)}, ...), branch_computations={%region_0.1_spmd, %region_1.2_spmd, %region_2.3_spmd} | conditional | flops 3724640256 | bytes 92963672
  21.0 1.3 %collective-permute-start = (bf16[128,1024]{1,0:T(8,128)(2,1)S(1)}, bf16[128,1024]{1,0:T(8,128)(2,1)S(1)}, u32[]{:S(2)}, u32[]{:S(2)}) collective-permute-start(bf16[128,1024]{1,0:T(8,128)(2,1)S(1)} %get-tuple-element.143), channel_id=1, source_target_pairs={{0,2},{2,0},{4,6},{6,4},{8,10},{10,8},{12,14},{14,12},{1,3},{3,1},... | collective-permute-start | bytes 786440 | tf_op jit(solution)/shard_map/cond/branch_0_fun/ppermute | solution.py:587
  22.3 6.3 %branch_0_fun.11 = bf16[2,64,1024]{2,1,0:T(8,128)(2,1)S(1)} custom-call(s32[1]{0:T(128)S(6)} %sub.33.side_ref, bf16[64,4096]{1,0:T(8,128)(2,1)S(1)} %get-tuple-element.149.x_ref, bf16[4096,2048]{1,0:T(8,128)(2,1)} %get-tuple-element.141.gate_ref, bf16[4096,2048]{1,0:T(8,128)(2,1)} %get-tuple-element.142.up_ref), custom_call_target="tpu_custom_call" | custom-call | flops 1073741824 | bytes 17301504 | tf_op jit(solution)/shard_map/cond/branch_0_fun/pallas_call | solution.py:305
  30.3 1.3 %collective-permute-start.7 = (bf16[64,4096]{1,0:T(8,128)(2,1)S(1)}, bf16[64,4096]{1,0:T(8,128)(2,1)S(1)}, u32[]{:S(2)}, u32[]{:S(2)}) collective-permute-start(bf16[64,4096]{1,0:T(8,128)(2,1)S(1)} %bitcast.20), channel_id=1, source_target_pairs={{0,2},{2,0},{4,6},{6,4},{8,10},{10,8},{12,14},{14,12},{1,3},{3,1},... | collective-permute-start | bytes 1572872 | tf_op jit(solution)/shard_map/cond/branch_0_fun/ppermute | solution.py:593
  32.0 3.5 %collective-permute-start.3 = (bf16[48,1024]{1,0:T(8,128)(2,1)S(1)}, bf16[48,1024]{1,0:T(8,128)(2,1)S(1)}, u32[]{:S(2)}, u32[]{:S(2)}) collective-permute-start(bf16[48,1024]{1,0:T(8,128)(2,1)S(1)} %get-tuple-element.153), channel_id=1, source_target_pairs={{0,8},{2,10},{4,12},{6,14},{8,0},{10,2},{12,4},{14,6},{1,9},{3,11}... | collective-permute-start | bytes 294920 | tf_op jit(solution)/shard_map/cond/branch_0_fun/ppermute | solution.py:92
  35.5 6.2 %branch_0_fun.13.own_ref = f32[2,64,1024]{2,1,0:T(8,128)S(1)} custom-call(s32[1]{0:T(128)} %bitcast.side_ref.core_ref, bf16[64,4096]{1,0:T(8,128)(2,1)S(1)} %get-tuple-element.149.x_ref, bf16[4096,2048]{1,0:T(8,128)(2,1)} %get-tuple-element.141.gate_ref, bf16[4096,2048]{1,0:T(8,128)(2,1)} %get-tuple-element.142.up_ref), custom_call_target="tpu_custom_call" | custom-call | flops 1073741824 | bytes 17301504 | tf_op jit(solution)/shard_map/cond/branch_0_fun/pallas_call | solution.py:305
  43.8 1.3 %collective-permute-start.6 = (bf16[64,1024]{1,0:T(8,128)(2,1)S(1)}, bf16[64,1024]{1,0:T(8,128)(2,1)S(1)}, u32[]{:S(2)}, u32[]{:S(2)}) collective-permute-start(bf16[64,1024]{1,0:T(8,128)(2,1)S(1)} %get-tuple-element.160), channel_id=1, source_target_pairs={{0,2},{2,0},{4,6},{6,4},{8,10},{10,8},{12,14},{14,12},{1,3},{3,1},... | collective-permute-start | bytes 393224 | tf_op jit(solution)/shard_map/cond/branch_0_fun/ppermute | solution.py:608
  45.1 4.2 %branch_0_fun.15 = (f32[32,2048]{1,0:T(8,128)S(1)}, bf16[32,2048]{1,0:T(8,128)(2,1)S(1)}) custom-call(s32[1]{0:T(128)} %bitcast.side_ref.core_ref, bf16[64,1024]{1,0:T(8,128)(2,1)S(1)} %get-tuple-element.167.near_ref, bf16[64,1024]{1,0:T(8,128)(2,1)S(1)} %collective-permute-done.5.far_ref, bf16[2048,4096]{1,0:T(8,128)(2,1)} %get-tuple-element.156.weight_ref), custom_call_target="tpu_custom_call" | custom-call | flops 536870912 | bytes 8912896 | tf_op jit(solution)/shard_map/cond/branch_0_fun/pallas_call | solution.py:434
  49.7 1.2 %collective-permute-start.8 = (bf16[32,2048]{1,0:T(8,128)(2,1)S(1)}, bf16[32,2048]{1,0:T(8,128)(2,1)S(1)}, u32[]{:S(2)}, u32[]{:S(2)}) collective-permute-start(bf16[32,2048]{1,0:T(8,128)(2,1)S(1)} %get-tuple-element.170), channel_id=1, source_target_pairs={{0,2},{2,0},{4,6},{6,4},{8,10},{10,8},{12,14},{14,12},{1,3},{3,1},... | collective-permute-start | bytes 393224 | tf_op jit(solution)/shard_map/cond/branch_0_fun/ppermute | solution.py:611
  50.9 2.7 %collective-permute-start.9 = (bf16[32,1024]{1,0:T(8,128)(2,1)S(1)}, bf16[32,1024]{1,0:T(8,128)(2,1)S(1)}, u32[]{:S(2)}, u32[]{:S(2)}) collective-permute-start(bf16[32,1024]{1,0:T(8,128)(2,1)S(1)} %get-tuple-element.172), channel_id=1, source_target_pairs={{0,4},{2,6},{4,8},{6,10},{8,12},{10,14},{12,0},{14,2},{1,5},{3,7},... | collective-permute-start | bytes 196616 | tf_op jit(solution)/shard_map/cond/branch_0_fun/ppermute | solution.py:92
  54.2 1.9 %collective-permute-start.11 = (bf16[32,1024]{1,0:T(8,128)(2,1)S(1)}, bf16[32,1024]{1,0:T(8,128)(2,1)S(1)}, u32[]{:S(2)}, u32[]{:S(2)}) collective-permute-start(bf16[32,1024]{1,0:T(8,128)(2,1)S(1)} %get-tuple-element.174), channel_id=1, source_target_pairs={{0,12},{2,14},{4,0},{6,2},{8,4},{10,6},{12,8},{14,10},{1,13},{3,15... | collective-permute-start | bytes 196616 | tf_op jit(solution)/shard_map/cond/branch_0_fun/ppermute | solution.py:92
  56.0 4.0 %branch_0_fun.17 = (f32[32,2048]{1,0:T(8,128)S(1)}, bf16[32,2048]{1,0:T(8,128)(2,1)S(1)}) custom-call(s32[1]{0:T(128)} %bitcast.side_ref.core_ref, bf16[64,1024]{1,0:T(8,128)(2,1)S(1)} %get-tuple-element.167.near_ref, bf16[64,1024]{1,0:T(8,128)(2,1)S(1)} %collective-permute-done.5.far_ref, bf16[2048,4096]{1,0:T(8,128)(2,1)} %get-tuple-element.156.weight_ref), custom_call_target="tpu_custom_call" | custom-call | flops 536870912 | bytes 8912896 | tf_op jit(solution)/shard_map/cond/branch_0_fun/pallas_call | solution.py:434
  61.9 1.3 %collective-permute-start.14 = (f32[16,64]{1,0:T(8,128)S(1)}, f32[16,64]{1,0:T(8,128)S(1)}, u32[]{:S(2)}, u32[]{:S(2)}) collective-permute-start(f32[16,64]{1,0:T(8,128)S(1)} %branch_0_fun.18.refs_4_), channel_id=1, source_target_pairs={{0,2},{2,0},{4,6},{6,4},{8,10},{10,8},{12,14},{14,12},{1,3},{3,1},... | collective-permute-start | bytes 12296 | tf_op jit(solution)/shard_map/cond/branch_0_fun/ppermute | solution.py:629
  63.8 1.3 %collective-permute-done.15.refs_7_ = f32[16,64]{1,0:T(8,128)S(1)} collective-permute-done((f32[16,64]{1,0:T(8,128)S(1)}, f32[16,64]{1,0:T(8,128)S(1)}, u32[]{:S(2)}, u32[]{:S(2)}) %collective-permute-start.15) | collective-permute-done | bytes 4128 | tf_op jit(solution)/shard_map/cond/branch_0_fun/ppermute | solution.py:633
  66.2 1.9 %collective-permute-start.16 = (bf16[8,4096]{1,0:T(8,128)(2,1)S(1)}, bf16[8,4096]{1,0:T(8,128)(2,1)S(1)}, u32[]{:S(2)}, u32[]{:S(2)}) collective-permute-start(bf16[8,4096]{1,0:T(8,128)(2,1)S(1)} %get-tuple-element.190), channel_id=1, source_target_pairs={{0,4},{2,6},{4,8},{6,10},{8,12},{10,14},{12,0},{14,2},{1,5},{3,7},... | collective-permute-start | bytes 196616 | tf_op jit(solution)/shard_map/cond/branch_0_fun/ppermute | solution.py:92
  69.0 1.5 %collective-permute-start.18 = (bf16[8,4096]{1,0:T(8,128)(2,1)S(1)}, bf16[8,4096]{1,0:T(8,128)(2,1)S(1)}, u32[]{:S(2)}, u32[]{:S(2)}) collective-permute-start(bf16[8,4096]{1,0:T(8,128)(2,1)S(1)} %get-tuple-element.192), channel_id=1, source_target_pairs={{0,12},{2,14},{4,0},{6,2},{8,4},{10,6},{12,8},{14,10},{1,13},{3,15... | collective-permute-start | bytes 196616 | tf_op jit(solution)/shard_map/cond/branch_0_fun/ppermute | solution.py:92
  70.5 2.5 %collective-permute-done.16 = bf16[8,4096]{1,0:T(8,128)(2,1)S(1)} collective-permute-done((bf16[8,4096]{1,0:T(8,128)(2,1)S(1)}, bf16[8,4096]{1,0:T(8,128)(2,1)S(1)}, u32[]{:S(2)}, u32[]{:S(2)}) %collective-permute-start.16) | collective-permute-done | bytes 65568 | tf_op jit(solution)/shard_map/cond/branch_0_fun/ppermute | solution.py:92
  73.0 2.1 %collective-permute-done.17 = bf16[8,4096]{1,0:T(8,128)(2,1)S(1)} collective-permute-done((bf16[8,4096]{1,0:T(8,128)(2,1)S(1)}, bf16[8,4096]{1,0:T(8,128)(2,1)S(1)}, u32[]{:S(2)}, u32[]{:S(2)}) %collective-permute-start.17) | collective-permute-done | bytes 65568 | tf_op jit(solution)/shard_map/cond/branch_0_fun/ppermute | solution.py:92
  (62 shorter events, 18.2 us)
Async XLA Ops:
  0.0 12.9 %collective-permute-start.58 = (bf16[64,16384]{1,0:T(8,128)(2,1)}, bf16[64,16384]{1,0:T(8,128)(2,1)S(1)}, u32[]{:S(2)}, u32[]{:S(2)}) collective-permute-start(bf16[64,16384]{1,0:T(8,128)(2,1)} %bitcast.26), channel_id=1, source_target_pairs={{0,1},{1,0},{2,3},{3,2},{4,5},{5,4},{6,7},{7,6},{8,9},{9,8},{10,11... | collective-permute-start | bytes 6291464 | tf_op jit(solution)/shard_map/ppermute | solution.py:546
  0.5 9.8 %collective-permute-start.59 = (bf16[8,4096]{1,0:T(8,128)(2,1)}, bf16[8,4096]{1,0:T(8,128)(2,1)S(1)}, u32[]{:S(2)}, u32[]{:S(2)}) collective-permute-start(bf16[8,4096]{1,0:T(8,128)(2,1)} %x_ref.1), channel_id=1, source_target_pairs={{0,8},{2,10},{4,12},{6,14},{8,0},{10,2},{12,4},{14,6},{1,9},{3,11}... | collective-permute-start | bytes 196616 | tf_op jit(solution)/shard_map/ppermute | solution.py:79
  4.0 8.9 %collective-permute-start.57 = (bf16[8,4096]{1,0:T(8,128)(2,1)}, bf16[8,4096]{1,0:T(8,128)(2,1)S(1)}, u32[]{:S(2)}, u32[]{:S(2)}) collective-permute-start(bf16[8,4096]{1,0:T(8,128)(2,1)} %x_ref.1), channel_id=1, source_target_pairs={{0,4},{2,6},{4,8},{6,10},{8,12},{10,14},{12,0},{14,2},{1,5},{3,7},... | collective-permute-start | bytes 196616 | tf_op jit(solution)/shard_map/ppermute | solution.py:79
  5.6 11.9 %collective-permute-start.61 = (bf16[8,4096]{1,0:T(8,128)(2,1)}, bf16[8,4096]{1,0:T(8,128)(2,1)S(1)}, u32[]{:S(2)}, u32[]{:S(2)}) collective-permute-start(bf16[8,4096]{1,0:T(8,128)(2,1)} %x_ref.1), channel_id=1, source_target_pairs={{0,2},{2,0},{4,6},{6,4},{8,10},{10,8},{12,14},{14,12},{1,3},{3,1},... | collective-permute-start | bytes 196616 | tf_op jit(solution)/shard_map/ppermute | solution.py:83
  7.1 4.6 %collective-permute-start.60 = (bf16[8,4096]{1,0:T(8,128)(2,1)}, bf16[8,4096]{1,0:T(8,128)(2,1)S(1)}, u32[]{:S(2)}, u32[]{:S(2)}) collective-permute-start(bf16[8,4096]{1,0:T(8,128)(2,1)} %x_ref.1), channel_id=1, source_target_pairs={{0,12},{2,14},{4,0},{6,2},{8,4},{10,6},{12,8},{14,10},{1,13},{3,15... | collective-permute-start | bytes 196616 | tf_op jit(solution)/shard_map/ppermute | solution.py:79
  10.3 7.3 %collective-permute-start.63 = (bf16[8,4096]{1,0:T(8,128)(2,1)S(1)}, bf16[8,4096]{1,0:T(8,128)(2,1)S(1)}, u32[]{:S(2)}, u32[]{:S(2)}) collective-permute-start(bf16[8,4096]{1,0:T(8,128)(2,1)S(1)} %collective-permute-done.59.refs_4_), channel_id=1, source_target_pairs={{0,2},{2,0},{4,6},{6,4},{8,10},{10,8},{12,14},{14,12},{1,3},{3,1},... | collective-permute-start | bytes 196616 | tf_op jit(solution)/shard_map/ppermute | solution.py:83
  11.7 5.8 %collective-permute-start.64 = (bf16[8,4096]{1,0:T(8,128)(2,1)S(1)}, bf16[8,4096]{1,0:T(8,128)(2,1)S(1)}, u32[]{:S(2)}, u32[]{:S(2)}) collective-permute-start(bf16[8,4096]{1,0:T(8,128)(2,1)S(1)} %collective-permute-done.60.refs_5_), channel_id=1, source_target_pairs={{0,2},{2,0},{4,6},{6,4},{8,10},{10,8},{12,14},{14,12},{1,3},{3,1},... | collective-permute-start | bytes 196616 | tf_op jit(solution)/shard_map/ppermute | solution.py:83
  12.9 4.6 %collective-permute-start.62 = (bf16[8,4096]{1,0:T(8,128)(2,1)S(1)}, bf16[8,4096]{1,0:T(8,128)(2,1)S(1)}, u32[]{:S(2)}, u32[]{:S(2)}) collective-permute-start(bf16[8,4096]{1,0:T(8,128)(2,1)S(1)} %collective-permute-done.57.refs_3_), channel_id=1, source_target_pairs={{0,2},{2,0},{4,6},{6,4},{8,10},{10,8},{12,14},{14,12},{1,3},{3,1},... | collective-permute-start | bytes 196616 | tf_op jit(solution)/shard_map/ppermute | solution.py:83
  21.0 8.4 %collective-permute-start = (bf16[128,1024]{1,0:T(8,128)(2,1)S(1)}, bf16[128,1024]{1,0:T(8,128)(2,1)S(1)}, u32[]{:S(2)}, u32[]{:S(2)}) collective-permute-start(bf16[128,1024]{1,0:T(8,128)(2,1)S(1)} %get-tuple-element.143), channel_id=1, source_target_pairs={{0,2},{2,0},{4,6},{6,4},{8,10},{10,8},{12,14},{14,12},{1,3},{3,1},... | collective-permute-start | bytes 786440 | tf_op jit(solution)/shard_map/cond/branch_0_fun/ppermute | solution.py:587
  30.3 19.4 %collective-permute-start.7 = (bf16[64,4096]{1,0:T(8,128)(2,1)S(1)}, bf16[64,4096]{1,0:T(8,128)(2,1)S(1)}, u32[]{:S(2)}, u32[]{:S(2)}) collective-permute-start(bf16[64,4096]{1,0:T(8,128)(2,1)S(1)} %bitcast.20), channel_id=1, source_target_pairs={{0,2},{2,0},{4,6},{6,4},{8,10},{10,8},{12,14},{14,12},{1,3},{3,1},... | collective-permute-start | bytes 1572872 | tf_op jit(solution)/shard_map/cond/branch_0_fun/ppermute | solution.py:593
  31.6 11.3 %collective-permute-start.1 = (bf16[2,64,1024]{2,1,0:T(8,128)(2,1)S(1)}, bf16[2,64,1024]{2,1,0:T(8,128)(2,1)S(1)}, u32[]{:S(2)}, u32[]{:S(2)}) collective-permute-start(bf16[2,64,1024]{2,1,0:T(8,128)(2,1)S(1)} %branch_0_fun.11), channel_id=1, source_target_pairs={{0,1},{1,0},{2,3},{3,2},{4,5},{5,4},{6,7},{7,6},{8,9},{9,8},{10,11... | collective-permute-start | bytes 786440 | tf_op jit(solution)/shard_map/cond/branch_0_fun/ppermute | solution.py:546
  31.6 10.2 %collective-permute-start.2 = (bf16[48,1024]{1,0:T(8,128)(2,1)S(1)}, bf16[48,1024]{1,0:T(8,128)(2,1)S(1)}, u32[]{:S(2)}, u32[]{:S(2)}) collective-permute-start(bf16[48,1024]{1,0:T(8,128)(2,1)S(1)} %get-tuple-element.152), channel_id=1, source_target_pairs={{0,4},{2,6},{4,8},{6,10},{8,12},{10,14},{12,0},{14,2},{1,5},{3,7},... | collective-permute-start | bytes 294920 | tf_op jit(solution)/shard_map/cond/branch_0_fun/ppermute | solution.py:92
  32.0 10.8 %collective-permute-start.3 = (bf16[48,1024]{1,0:T(8,128)(2,1)S(1)}, bf16[48,1024]{1,0:T(8,128)(2,1)S(1)}, u32[]{:S(2)}, u32[]{:S(2)}) collective-permute-start(bf16[48,1024]{1,0:T(8,128)(2,1)S(1)} %get-tuple-element.153), channel_id=1, source_target_pairs={{0,8},{2,10},{4,12},{6,14},{8,0},{10,2},{12,4},{14,6},{1,9},{3,11}... | collective-permute-start | bytes 294920 | tf_op jit(solution)/shard_map/cond/branch_0_fun/ppermute | solution.py:92
  35.5 7.4 %collective-permute-start.4 = (bf16[48,1024]{1,0:T(8,128)(2,1)S(1)}, bf16[48,1024]{1,0:T(8,128)(2,1)S(1)}, u32[]{:S(2)}, u32[]{:S(2)}) collective-permute-start(bf16[48,1024]{1,0:T(8,128)(2,1)S(1)} %get-tuple-element.154), channel_id=1, source_target_pairs={{0,12},{2,14},{4,0},{6,2},{8,4},{10,6},{12,8},{14,10},{1,13},{3,15... | collective-permute-start | bytes 294920 | tf_op jit(solution)/shard_map/cond/branch_0_fun/ppermute | solution.py:92
  43.8 5.9 %collective-permute-start.6 = (bf16[64,1024]{1,0:T(8,128)(2,1)S(1)}, bf16[64,1024]{1,0:T(8,128)(2,1)S(1)}, u32[]{:S(2)}, u32[]{:S(2)}) collective-permute-start(bf16[64,1024]{1,0:T(8,128)(2,1)S(1)} %get-tuple-element.160), channel_id=1, source_target_pairs={{0,2},{2,0},{4,6},{6,4},{8,10},{10,8},{12,14},{14,12},{1,3},{3,1},... | collective-permute-start | bytes 393224 | tf_op jit(solution)/shard_map/cond/branch_0_fun/ppermute | solution.py:608
  49.7 10.4 %collective-permute-start.8 = (bf16[32,2048]{1,0:T(8,128)(2,1)S(1)}, bf16[32,2048]{1,0:T(8,128)(2,1)S(1)}, u32[]{:S(2)}, u32[]{:S(2)}) collective-permute-start(bf16[32,2048]{1,0:T(8,128)(2,1)S(1)} %get-tuple-element.170), channel_id=1, source_target_pairs={{0,2},{2,0},{4,6},{6,4},{8,10},{10,8},{12,14},{14,12},{1,3},{3,1},... | collective-permute-start | bytes 393224 | tf_op jit(solution)/shard_map/cond/branch_0_fun/ppermute | solution.py:611
  50.9 9.1 %collective-permute-start.9 = (bf16[32,1024]{1,0:T(8,128)(2,1)S(1)}, bf16[32,1024]{1,0:T(8,128)(2,1)S(1)}, u32[]{:S(2)}, u32[]{:S(2)}) collective-permute-start(bf16[32,1024]{1,0:T(8,128)(2,1)S(1)} %get-tuple-element.172), channel_id=1, source_target_pairs={{0,4},{2,6},{4,8},{6,10},{8,12},{10,14},{12,0},{14,2},{1,5},{3,7},... | collective-permute-start | bytes 196616 | tf_op jit(solution)/shard_map/cond/branch_0_fun/ppermute | solution.py:92
  53.6 6.5 %collective-permute-start.10 = (bf16[32,1024]{1,0:T(8,128)(2,1)S(1)}, bf16[32,1024]{1,0:T(8,128)(2,1)S(1)}, u32[]{:S(2)}, u32[]{:S(2)}) collective-permute-start(bf16[32,1024]{1,0:T(8,128)(2,1)S(1)} %get-tuple-element.173), channel_id=1, source_target_pairs={{0,8},{2,10},{4,12},{6,14},{8,0},{10,2},{12,4},{14,6},{1,9},{3,11}... | collective-permute-start | bytes 196616 | tf_op jit(solution)/shard_map/cond/branch_0_fun/ppermute | solution.py:92
  54.2 5.9 %collective-permute-start.11 = (bf16[32,1024]{1,0:T(8,128)(2,1)S(1)}, bf16[32,1024]{1,0:T(8,128)(2,1)S(1)}, u32[]{:S(2)}, u32[]{:S(2)}) collective-permute-start(bf16[32,1024]{1,0:T(8,128)(2,1)S(1)} %get-tuple-element.174), channel_id=1, source_target_pairs={{0,12},{2,14},{4,0},{6,2},{8,4},{10,6},{12,8},{14,10},{1,13},{3,15... | collective-permute-start | bytes 196616 | tf_op jit(solution)/shard_map/cond/branch_0_fun/ppermute | solution.py:92
  60.1 5.5 %collective-permute-start.12 = (bf16[32,2048]{1,0:T(8,128)(2,1)S(1)}, bf16[32,2048]{1,0:T(8,128)(2,1)S(1)}, u32[]{:S(2)}, u32[]{:S(2)}) collective-permute-start(bf16[32,2048]{1,0:T(8,128)(2,1)S(1)} %get-tuple-element.181), channel_id=1, source_target_pairs={{0,2},{2,0},{4,6},{6,4},{8,10},{10,8},{12,14},{14,12},{1,3},{3,1},... | collective-permute-start | bytes 393224 | tf_op jit(solution)/shard_map/cond/branch_0_fun/ppermute | solution.py:618
  61.9 3.7 %collective-permute-start.14 = (f32[16,64]{1,0:T(8,128)S(1)}, f32[16,64]{1,0:T(8,128)S(1)}, u32[]{:S(2)}, u32[]{:S(2)}) collective-permute-start(f32[16,64]{1,0:T(8,128)S(1)} %branch_0_fun.18.refs_4_), channel_id=1, source_target_pairs={{0,2},{2,0},{4,6},{6,4},{8,10},{10,8},{12,14},{14,12},{1,3},{3,1},... | collective-permute-start | bytes 12296 | tf_op jit(solution)/shard_map/cond/branch_0_fun/ppermute | solution.py:629
  66.2 6.8 %collective-permute-start.16 = (bf16[8,4096]{1,0:T(8,128)(2,1)S(1)}, bf16[8,4096]{1,0:T(8,128)(2,1)S(1)}, u32[]{:S(2)}, u32[]{:S(2)}) collective-permute-start(bf16[8,4096]{1,0:T(8,128)(2,1)S(1)} %get-tuple-element.190), channel_id=1, source_target_pairs={{0,4},{2,6},{4,8},{6,10},{8,12},{10,14},{12,0},{14,2},{1,5},{3,7},... | collective-permute-start | bytes 196616 | tf_op jit(solution)/shard_map/cond/branch_0_fun/ppermute | solution.py:92
  68.1 7.0 %collective-permute-start.17 = (bf16[8,4096]{1,0:T(8,128)(2,1)S(1)}, bf16[8,4096]{1,0:T(8,128)(2,1)S(1)}, u32[]{:S(2)}, u32[]{:S(2)}) collective-permute-start(bf16[8,4096]{1,0:T(8,128)(2,1)S(1)} %get-tuple-element.191), channel_id=1, source_target_pairs={{0,8},{2,10},{4,12},{6,14},{8,0},{10,2},{12,4},{14,6},{1,9},{3,11}... | collective-permute-start | bytes 196616 | tf_op jit(solution)/shard_map/cond/branch_0_fun/ppermute | solution.py:92
  69.0 6.0 %collective-permute-start.18 = (bf16[8,4096]{1,0:T(8,128)(2,1)S(1)}, bf16[8,4096]{1,0:T(8,128)(2,1)S(1)}, u32[]{:S(2)}, u32[]{:S(2)}) collective-permute-start(bf16[8,4096]{1,0:T(8,128)(2,1)S(1)} %get-tuple-element.192), channel_id=1, source_target_pairs={{0,12},{2,14},{4,0},{6,2},{8,4},{10,6},{12,8},{14,10},{1,13},{3,15... | collective-permute-start | bytes 196616 | tf_op jit(solution)/shard_map/cond/branch_0_fun/ppermute | solution.py:92
  (7 other events, 33.0 us)

commit v8 on v7

--- a/solution.py
+++ b/solution.py
@@ -12,6 +12,8 @@
 MINE, NEXT, STEP, PLACE, ARRIVE, PACKED = range(6)
 USUAL = 16
 USUAL_PAIR = 24
+CROWDED = 24
+CROWDED_PAIR = 32
 BF = jnp.bfloat16
 F32 = jnp.float32
 I32 = jnp.int32
@@ -169,9 +171,9 @@
         arrive = jnp.where(hit, float(b % ways.slow if paired else b), arrive)
         if paired and b >= ways.slow:
             packed = jnp.where(hit, place + beside, packed)
-    over = (place >= float(USUAL)).astype(F32)
-    far_over = (place >= float(USUAL_PAIR)) | (pair > float(USUAL_PAIR))
-    facts_ref[0] = jnp.max(jnp.where(far_over, 2.0, over)).astype(I32)
+    over = (place >= float(USUAL)) | (pair > float(USUAL_PAIR))
+    far_over = (place >= float(CROWDED)) | (pair > float(CROWDED_PAIR))
+    facts_ref[0] = jnp.max(jnp.where(far_over, 2.0, over.astype(F32))).astype(I32)
     facts_ref[1] = jnp.sum((owner == me).astype(F32)).astype(I32)
     facts_ref[2] = jnp.sum((owner == beside_me).astype(F32)).astype(I32)
     lines = {
@@ -641,10 +643,10 @@
         return ways.slow_steps(parts)
 
     most_room = 2 * most if split == 2 else most
-    if most <= USUAL_PAIR:
+    if most <= CROWDED:
         parts = partial_sums(most, most_room)
     else:
-        rooms = [(USUAL, USUAL_PAIR), (USUAL_PAIR, USUAL_PAIR), (most, 2 * most)]
+        rooms = [(USUAL, USUAL_PAIR), (CROWDED, CROWDED_PAIR), (most, 2 * most)]
         branches = [
             functools.partial(partial_sums, cap, room if split == 2 else cap) for cap, room in rooms
         ]

time: 76.2 us -> 76.2 us (level)
  no operation moved by 1% of the time
where the time goes in v8:
time: 76.2 us; the launch traced here: 76 us
  starting transfers between devices  33.2 us (44%)
  Pallas kernels  28.9 us (38%)
  waiting for transfers between devices  10.8 us (14%)
  other arithmetic  1.66 us (2%)
  local copies, waits for them, and re-layouts  0.84 us (1%)
    ppermute x9, starting transfers between devices, slow_steps(): got[-a % self.slow] = lax.ppermute(blocks[a], 'ff', self.back(a, 0))  13.4 us
    pallas_call x2, Pallas kernels, base_half(): pl.pallas_call(base_kernel, out_shape=jax.ShapeDtypeStruct((2, rows, half...  12.5 us
    pallas_call x2, Pallas kernels, down_base(): pl.pallas_call(functools.partial(down_kernel, start), out_shape=outs, in_...  8.17 us
    ppermute x3, starting transfers between devices, gather(): lax.ppermute(block, 'ff', self.back(-a, 0))  7.41 us
    ppermute x9, waiting for transfers between devices, slow_steps(): got[-a % self.slow] = lax.ppermute(blocks[a], 'ff', self.back(a, 0))  5.62 us
    ppermute x4, starting transfers between devices, gather(): lax.ppermute(part, 'ff', self.back(0, -c))  4.05 us
    pallas_call x1, Pallas kernels, tables(): pl.pallas_call(functools.partial(tables_kernel, ways, slots), out_shape=(...  2.89 us
  transfers between devices with their start and end apart: 28, of which 9 were waited for; matrix products, arithmetic and copies ran while one was open for 1% of the time, Pallas kernels for 33%

profile of v8, /device:TPU:0, one launch (start us, length us, event | category | flops | bytes accessed | tf_op | source)
XLA Modules:
  0.0 76.0 jit_solution(17295741347188682440)
XLA Ops:
  0.5 3.6 %collective-permute-start.59 = (bf16[8,4096]{1,0:T(8,128)(2,1)}, bf16[8,4096]{1,0:T(8,128)(2,1)S(1)}, u32[]{:S(2)}, u32[]{:S(2)}) collective-permute-start(bf16[8,4096]{1,0:T(8,128)(2,1)} %x_ref.1), channel_id=1, source_target_pairs={{0,8},{2,10},{4,12},{6,14},{8,0},{10,2},{12,4},{14,6},{1,9},{3,11}... | collective-permute-start | bytes 196616 | tf_op jit(solution)/shard_map/ppermute | solution.py:81
  4.0 1.6 %collective-permute-start.57 = (bf16[8,4096]{1,0:T(8,128)(2,1)}, bf16[8,4096]{1,0:T(8,128)(2,1)S(1)}, u32[]{:S(2)}, u32[]{:S(2)}) collective-permute-start(bf16[8,4096]{1,0:T(8,128)(2,1)} %x_ref.1), channel_id=1, source_target_pairs={{0,4},{2,6},{4,8},{6,10},{8,12},{10,14},{12,0},{14,2},{1,5},{3,7},... | collective-permute-start | bytes 196616 | tf_op jit(solution)/shard_map/ppermute | solution.py:81
  5.6 1.5 %collective-permute-start.61 = (bf16[8,4096]{1,0:T(8,128)(2,1)}, bf16[8,4096]{1,0:T(8,128)(2,1)S(1)}, u32[]{:S(2)}, u32[]{:S(2)}) collective-permute-start(bf16[8,4096]{1,0:T(8,128)(2,1)} %x_ref.1), channel_id=1, source_target_pairs={{0,2},{2,0},{4,6},{6,4},{8,10},{10,8},{12,14},{14,12},{1,3},{3,1},... | collective-permute-start | bytes 196616 | tf_op jit(solution)/shard_map/ppermute | solution.py:85
  7.1 2.2 %collective-permute-start.60 = (bf16[8,4096]{1,0:T(8,128)(2,1)}, bf16[8,4096]{1,0:T(8,128)(2,1)S(1)}, u32[]{:S(2)}, u32[]{:S(2)}) collective-permute-start(bf16[8,4096]{1,0:T(8,128)(2,1)} %x_ref.1), channel_id=1, source_target_pairs={{0,12},{2,14},{4,0},{6,2},{8,4},{10,6},{12,8},{14,10},{1,13},{3,15... | collective-permute-start | bytes 196616 | tf_op jit(solution)/shard_map/ppermute | solution.py:81
  11.7 1.2 %collective-permute-start.64 = (bf16[8,4096]{1,0:T(8,128)(2,1)S(1)}, bf16[8,4096]{1,0:T(8,128)(2,1)S(1)}, u32[]{:S(2)}, u32[]{:S(2)}) collective-permute-start(bf16[8,4096]{1,0:T(8,128)(2,1)S(1)} %collective-permute-done.60.refs_5_), channel_id=1, source_target_pairs={{0,2},{2,0},{4,6},{6,4},{8,10},{10,8},{12,14},{14,12},{1,3},{3,1},... | collective-permute-start | bytes 196616 | tf_op jit(solution)/shard_map/ppermute | solution.py:85
  14.6 2.9 %shard_map.100 = (s32[8,64]{1,0:T(8,128)S(1)}, f32[64,128]{1,0:T(8,128)S(1)}, bf16[64,64]{1,0:T(8,128)(2,1)S(1)}, s32[3]{0:T(128)S(1)}, bf16[8,4096]{1,0:T(8,128...) custom-call(s32[8]{0:T(128)S(1)} %get-tuple-element.370.order_ref, s32[1]{0:T(128)} %bitcast.9.me_ref, ...), custom_call_target="tpu_custom_call" | custom-call | bytes 4325376 | tf_op jit(solution)/shard_map/pallas_call | solution.py:202
  19.9 55.4 %conditional.3 = (bf16[8,4096]{1,0:T(8,128)(2,1)S(1)}, f32[8,4096]{1,0:T(8,128)S(1)}, f32[8,4096]{1,0:T(8,128)S(1)}, f32[8,4096]{1,0:T(8,128)S(1)}) conditional(s32[]{:T(128)} %bitcast.14, (s32[]{:T(128)}, s32[8]{0:T(128)S(1)}, f32[64,128]{1,0:T(8,128)S(1)}, f32[64,128]{1,0:T(8,128)S(1)}, s32[8,64]{1,0:T(8,128)S(1)}, ...), branch_computations={%region_0.1_spmd, %region_1.2_spmd, %region_2.3_spmd} | conditional | flops 3724640256 | bytes 92963672
  21.0 1.3 %collective-permute-start = (bf16[128,1024]{1,0:T(8,128)(2,1)S(1)}, bf16[128,1024]{1,0:T(8,128)(2,1)S(1)}, u32[]{:S(2)}, u32[]{:S(2)}) collective-permute-start(bf16[128,1024]{1,0:T(8,128)(2,1)S(1)} %get-tuple-element.143), channel_id=1, source_target_pairs={{0,2},{2,0},{4,6},{6,4},{8,10},{10,8},{12,14},{14,12},{1,3},{3,1},... | collective-permute-start | bytes 786440 | tf_op jit(solution)/shard_map/cond/branch_0_fun/ppermute | solution.py:589
  22.3 6.3 %branch_0_fun.11 = bf16[2,64,1024]{2,1,0:T(8,128)(2,1)S(1)} custom-call(s32[1]{0:T(128)S(6)} %sub.33.side_ref, bf16[64,4096]{1,0:T(8,128)(2,1)S(1)} %get-tuple-element.149.x_ref, bf16[4096,2048]{1,0:T(8,128)(2,1)} %get-tuple-element.141.gate_ref, bf16[4096,2048]{1,0:T(8,128)(2,1)} %get-tuple-element.142.up_ref), custom_call_target="tpu_custom_call" | custom-call | flops 1073741824 | bytes 17301504 | tf_op jit(solution)/shard_map/cond/branch_0_fun/pallas_call | solution.py:307
  30.3 1.3 %collective-permute-start.7 = (bf16[64,4096]{1,0:T(8,128)(2,1)S(1)}, bf16[64,4096]{1,0:T(8,128)(2,1)S(1)}, u32[]{:S(2)}, u32[]{:S(2)}) collective-permute-start(bf16[64,4096]{1,0:T(8,128)(2,1)S(1)} %bitcast.20), channel_id=1, source_target_pairs={{0,2},{2,0},{4,6},{6,4},{8,10},{10,8},{12,14},{14,12},{1,3},{3,1},... | collective-permute-start | bytes 1572872 | tf_op jit(solution)/shard_map/cond/branch_0_fun/ppermute | solution.py:595
  32.0 3.5 %collective-permute-start.3 = (bf16[48,1024]{1,0:T(8,128)(2,1)S(1)}, bf16[48,1024]{1,0:T(8,128)(2,1)S(1)}, u32[]{:S(2)}, u32[]{:S(2)}) collective-permute-start(bf16[48,1024]{1,0:T(8,128)(2,1)S(1)} %get-tuple-element.153), channel_id=1, source_target_pairs={{0,8},{2,10},{4,12},{6,14},{8,0},{10,2},{12,4},{14,6},{1,9},{3,11}... | collective-permute-start | bytes 294920 | tf_op jit(solution)/shard_map/cond/branch_0_fun/ppermute | solution.py:94
  35.5 6.2 %branch_0_fun.13.own_ref = f32[2,64,1024]{2,1,0:T(8,128)S(1)} custom-call(s32[1]{0:T(128)} %bitcast.side_ref.core_ref, bf16[64,4096]{1,0:T(8,128)(2,1)S(1)} %get-tuple-element.149.x_ref, bf16[4096,2048]{1,0:T(8,128)(2,1)} %get-tuple-element.141.gate_ref, bf16[4096,2048]{1,0:T(8,128)(2,1)} %get-tuple-element.142.up_ref), custom_call_target="tpu_custom_call" | custom-call | flops 1073741824 | bytes 17301504 | tf_op jit(solution)/shard_map/cond/branch_0_fun/pallas_call | solution.py:307
  43.8 1.3 %collective-permute-start.6 = (bf16[64,1024]{1,0:T(8,128)(2,1)S(1)}, bf16[64,1024]{1,0:T(8,128)(2,1)S(1)}, u32[]{:S(2)}, u32[]{:S(2)}) collective-permute-start(bf16[64,1024]{1,0:T(8,128)(2,1)S(1)} %get-tuple-element.160), channel_id=1, source_target_pairs={{0,2},{2,0},{4,6},{6,4},{8,10},{10,8},{12,14},{14,12},{1,3},{3,1},... | collective-permute-start | bytes 393224 | tf_op jit(solution)/shard_map/cond/branch_0_fun/ppermute | solution.py:610
  45.1 4.2 %branch_0_fun.15 = (f32[32,2048]{1,0:T(8,128)S(1)}, bf16[32,2048]{1,0:T(8,128)(2,1)S(1)}) custom-call(s32[1]{0:T(128)} %bitcast.side_ref.core_ref, bf16[64,1024]{1,0:T(8,128)(2,1)S(1)} %get-tuple-element.167.near_ref, bf16[64,1024]{1,0:T(8,128)(2,1)S(1)} %collective-permute-done.5.far_ref, bf16[2048,4096]{1,0:T(8,128)(2,1)} %get-tuple-element.156.weight_ref), custom_call_target="tpu_custom_call" | custom-call | flops 536870912 | bytes 8912896 | tf_op jit(solution)/shard_map/cond/branch_0_fun/pallas_call | solution.py:436
  49.7 1.2 %collective-permute-start.8 = (bf16[32,2048]{1,0:T(8,128)(2,1)S(1)}, bf16[32,2048]{1,0:T(8,128)(2,1)S(1)}, u32[]{:S(2)}, u32[]{:S(2)}) collective-permute-start(bf16[32,2048]{1,0:T(8,128)(2,1)S(1)} %get-tuple-element.170), channel_id=1, source_target_pairs={{0,2},{2,0},{4,6},{6,4},{8,10},{10,8},{12,14},{14,12},{1,3},{3,1},... | collective-permute-start | bytes 393224 | tf_op jit(solution)/shard_map/cond/branch_0_fun/ppermute | solution.py:613
  50.9 2.7 %collective-permute-start.9 = (bf16[32,1024]{1,0:T(8,128)(2,1)S(1)}, bf16[32,1024]{1,0:T(8,128)(2,1)S(1)}, u32[]{:S(2)}, u32[]{:S(2)}) collective-permute-start(bf16[32,1024]{1,0:T(8,128)(2,1)S(1)} %get-tuple-element.172), channel_id=1, source_target_pairs={{0,4},{2,6},{4,8},{6,10},{8,12},{10,14},{12,0},{14,2},{1,5},{3,7},... | collective-permute-start | bytes 196616 | tf_op jit(solution)/shard_map/cond/branch_0_fun/ppermute | solution.py:94
  54.2 1.9 %collective-permute-start.11 = (bf16[32,1024]{1,0:T(8,128)(2,1)S(1)}, bf16[32,1024]{1,0:T(8,128)(2,1)S(1)}, u32[]{:S(2)}, u32[]{:S(2)}) collective-permute-start(bf16[32,1024]{1,0:T(8,128)(2,1)S(1)} %get-tuple-element.174), channel_id=1, source_target_pairs={{0,12},{2,14},{4,0},{6,2},{8,4},{10,6},{12,8},{14,10},{1,13},{3,15... | collective-permute-start | bytes 196616 | tf_op jit(solution)/shard_map/cond/branch_0_fun/ppermute | solution.py:94
  56.0 4.0 %branch_0_fun.17 = (f32[32,2048]{1,0:T(8,128)S(1)}, bf16[32,2048]{1,0:T(8,128)(2,1)S(1)}) custom-call(s32[1]{0:T(128)} %bitcast.side_ref.core_ref, bf16[64,1024]{1,0:T(8,128)(2,1)S(1)} %get-tuple-element.167.near_ref, bf16[64,1024]{1,0:T(8,128)(2,1)S(1)} %collective-permute-done.5.far_ref, bf16[2048,4096]{1,0:T(8,128)(2,1)} %get-tuple-element.156.weight_ref), custom_call_target="tpu_custom_call" | custom-call | flops 536870912 | bytes 8912896 | tf_op jit(solution)/shard_map/cond/branch_0_fun/pallas_call | solution.py:436
  61.9 1.3 %collective-permute-start.14 = (f32[16,64]{1,0:T(8,128)S(1)}, f32[16,64]{1,0:T(8,128)S(1)}, u32[]{:S(2)}, u32[]{:S(2)}) collective-permute-start(f32[16,64]{1,0:T(8,128)S(1)} %branch_0_fun.18.refs_4_), channel_id=1, source_target_pairs={{0,2},{2,0},{4,6},{6,4},{8,10},{10,8},{12,14},{14,12},{1,3},{3,1},... | collective-permute-start | bytes 12296 | tf_op jit(solution)/shard_map/cond/branch_0_fun/ppermute | solution.py:631
  63.8 1.3 %collective-permute-done.15.refs_7_ = f32[16,64]{1,0:T(8,128)S(1)} collective-permute-done((f32[16,64]{1,0:T(8,128)S(1)}, f32[16,64]{1,0:T(8,128)S(1)}, u32[]{:S(2)}, u32[]{:S(2)}) %collective-permute-start.15) | collective-permute-done | bytes 4128 | tf_op jit(solution)/shard_map/cond/branch_0_fun/ppermute | solution.py:635
  66.2 1.9 %collective-permute-start.16 = (bf16[8,4096]{1,0:T(8,128)(2,1)S(1)}, bf16[8,4096]{1,0:T(8,128)(2,1)S(1)}, u32[]{:S(2)}, u32[]{:S(2)}) collective-permute-start(bf16[8,4096]{1,0:T(8,128)(2,1)S(1)} %get-tuple-element.190), channel_id=1, source_target_pairs={{0,4},{2,6},{4,8},{6,10},{8,12},{10,14},{12,0},{14,2},{1,5},{3,7},... | collective-permute-start | bytes 196616 | tf_op jit(solution)/shard_map/cond/branch_0_fun/ppermute | solution.py:94
  69.0 1.5 %collective-permute-start.18 = (bf16[8,4096]{1,0:T(8,128)(2,1)S(1)}, bf16[8,4096]{1,0:T(8,128)(2,1)S(1)}, u32[]{:S(2)}, u32[]{:S(2)}) collective-permute-start(bf16[8,4096]{1,0:T(8,128)(2,1)S(1)} %get-tuple-element.192), channel_id=1, source_target_pairs={{0,12},{2,14},{4,0},{6,2},{8,4},{10,6},{12,8},{14,10},{1,13},{3,15... | collective-permute-start | bytes 196616 | tf_op jit(solution)/shard_map/cond/branch_0_fun/ppermute | solution.py:94
  70.5 2.5 %collective-permute-done.16 = bf16[8,4096]{1,0:T(8,128)(2,1)S(1)} collective-permute-done((bf16[8,4096]{1,0:T(8,128)(2,1)S(1)}, bf16[8,4096]{1,0:T(8,128)(2,1)S(1)}, u32[]{:S(2)}, u32[]{:S(2)}) %collective-permute-start.16) | collective-permute-done | bytes 65568 | tf_op jit(solution)/shard_map/cond/branch_0_fun/ppermute | solution.py:94
  73.0 2.1 %collective-permute-done.17 = bf16[8,4096]{1,0:T(8,128)(2,1)S(1)} collective-permute-done((bf16[8,4096]{1,0:T(8,128)(2,1)S(1)}, bf16[8,4096]{1,0:T(8,128)(2,1)S(1)}, u32[]{:S(2)}, u32[]{:S(2)}) %collective-permute-start.17) | collective-permute-done | bytes 65568 | tf_op jit(solution)/shard_map/cond/branch_0_fun/ppermute | solution.py:94
  (62 shorter events, 18.2 us)
Async XLA Ops:
  0.0 12.9 %collective-permute-start.58 = (bf16[64,16384]{1,0:T(8,128)(2,1)}, bf16[64,16384]{1,0:T(8,128)(2,1)S(1)}, u32[]{:S(2)}, u32[]{:S(2)}) collective-permute-start(bf16[64,16384]{1,0:T(8,128)(2,1)} %bitcast.26), channel_id=1, source_target_pairs={{0,1},{1,0},{2,3},{3,2},{4,5},{5,4},{6,7},{7,6},{8,9},{9,8},{10,11... | collective-permute-start | bytes 6291464 | tf_op jit(solution)/shard_map/ppermute | solution.py:548
  0.5 9.8 %collective-permute-start.59 = (bf16[8,4096]{1,0:T(8,128)(2,1)}, bf16[8,4096]{1,0:T(8,128)(2,1)S(1)}, u32[]{:S(2)}, u32[]{:S(2)}) collective-permute-start(bf16[8,4096]{1,0:T(8,128)(2,1)} %x_ref.1), channel_id=1, source_target_pairs={{0,8},{2,10},{4,12},{6,14},{8,0},{10,2},{12,4},{14,6},{1,9},{3,11}... | collective-permute-start | bytes 196616 | tf_op jit(solution)/shard_map/ppermute | solution.py:81
  4.0 8.9 %collective-permute-start.57 = (bf16[8,4096]{1,0:T(8,128)(2,1)}, bf16[8,4096]{1,0:T(8,128)(2,1)S(1)}, u32[]{:S(2)}, u32[]{:S(2)}) collective-permute-start(bf16[8,4096]{1,0:T(8,128)(2,1)} %x_ref.1), channel_id=1, source_target_pairs={{0,4},{2,6},{4,8},{6,10},{8,12},{10,14},{12,0},{14,2},{1,5},{3,7},... | collective-permute-start | bytes 196616 | tf_op jit(solution)/shard_map/ppermute | solution.py:81
  5.6 11.9 %collective-permute-start.61 = (bf16[8,4096]{1,0:T(8,128)(2,1)}, bf16[8,4096]{1,0:T(8,128)(2,1)S(1)}, u32[]{:S(2)}, u32[]{:S(2)}) collective-permute-start(bf16[8,4096]{1,0:T(8,128)(2,1)} %x_ref.1), channel_id=1, source_target_pairs={{0,2},{2,0},{4,6},{6,4},{8,10},{10,8},{12,14},{14,12},{1,3},{3,1},... | collective-permute-start | bytes 196616 | tf_op jit(solution)/shard_map/ppermute | solution.py:85
  7.1 4.6 %collective-permute-start.60 = (bf16[8,4096]{1,0:T(8,128)(2,1)}, bf16[8,4096]{1,0:T(8,128)(2,1)S(1)}, u32[]{:S(2)}, u32[]{:S(2)}) collective-permute-start(bf16[8,4096]{1,0:T(8,128)(2,1)} %x_ref.1), channel_id=1, source_target_pairs={{0,12},{2,14},{4,0},{6,2},{8,4},{10,6},{12,8},{14,10},{1,13},{3,15... | collective-permute-start | bytes 196616 | tf_op jit(solution)/shard_map/ppermute | solution.py:81
  10.3 7.3 %collective-permute-start.63 = (bf16[8,4096]{1,0:T(8,128)(2,1)S(1)}, bf16[8,4096]{1,0:T(8,128)(2,1)S(1)}, u32[]{:S(2)}, u32[]{:S(2)}) collective-permute-start(bf16[8,4096]{1,0:T(8,128)(2,1)S(1)} %collective-permute-done.59.refs_4_), channel_id=1, source_target_pairs={{0,2},{2,0},{4,6},{6,4},{8,10},{10,8},{12,14},{14,12},{1,3},{3,1},... | collective-permute-start | bytes 196616 | tf_op jit(solution)/shard_map/ppermute | solution.py:85
  11.7 5.8 %collective-permute-start.64 = (bf16[8,4096]{1,0:T(8,128)(2,1)S(1)}, bf16[8,4096]{1,0:T(8,128)(2,1)S(1)}, u32[]{:S(2)}, u32[]{:S(2)}) collective-permute-start(bf16[8,4096]{1,0:T(8,128)(2,1)S(1)} %collective-permute-done.60.refs_5_), channel_id=1, source_target_pairs={{0,2},{2,0},{4,6},{6,4},{8,10},{10,8},{12,14},{14,12},{1,3},{3,1},... | collective-permute-start | bytes 196616 | tf_op jit(solution)/shard_map/ppermute | solution.py:85
  12.9 4.6 %collective-permute-start.62 = (bf16[8,4096]{1,0:T(8,128)(2,1)S(1)}, bf16[8,4096]{1,0:T(8,128)(2,1)S(1)}, u32[]{:S(2)}, u32[]{:S(2)}) collective-permute-start(bf16[8,4096]{1,0:T(8,128)(2,1)S(1)} %collective-permute-done.57.refs_3_), channel_id=1, source_target_pairs={{0,2},{2,0},{4,6},{6,4},{8,10},{10,8},{12,14},{14,12},{1,3},{3,1},... | collective-permute-start | bytes 196616 | tf_op jit(solution)/shard_map/ppermute | solution.py:85
  21.0 8.4 %collective-permute-start = (bf16[128,1024]{1,0:T(8,128)(2,1)S(1)}, bf16[128,1024]{1,0:T(8,128)(2,1)S(1)}, u32[]{:S(2)}, u32[]{:S(2)}) collective-permute-start(bf16[128,1024]{1,0:T(8,128)(2,1)S(1)} %get-tuple-element.143), channel_id=1, source_target_pairs={{0,2},{2,0},{4,6},{6,4},{8,10},{10,8},{12,14},{14,12},{1,3},{3,1},... | collective-permute-start | bytes 786440 | tf_op jit(solution)/shard_map/cond/branch_0_fun/ppermute | solution.py:589
  30.3 19.4 %collective-permute-start.7 = (bf16[64,4096]{1,0:T(8,128)(2,1)S(1)}, bf16[64,4096]{1,0:T(8,128)(2,1)S(1)}, u32[]{:S(2)}, u32[]{:S(2)}) collective-permute-start(bf16[64,4096]{1,0:T(8,128)(2,1)S(1)} %bitcast.20), channel_id=1, source_target_pairs={{0,2},{2,0},{4,6},{6,4},{8,10},{10,8},{12,14},{14,12},{1,3},{3,1},... | collective-permute-start | bytes 1572872 | tf_op jit(solution)/shard_map/cond/branch_0_fun/ppermute | solution.py:595
  31.6 11.3 %collective-permute-start.1 = (bf16[2,64,1024]{2,1,0:T(8,128)(2,1)S(1)}, bf16[2,64,1024]{2,1,0:T(8,128)(2,1)S(1)}, u32[]{:S(2)}, u32[]{:S(2)}) collective-permute-start(bf16[2,64,1024]{2,1,0:T(8,128)(2,1)S(1)} %branch_0_fun.11), channel_id=1, source_target_pairs={{0,1},{1,0},{2,3},{3,2},{4,5},{5,4},{6,7},{7,6},{8,9},{9,8},{10,11... | collective-permute-start | bytes 786440 | tf_op jit(solution)/shard_map/cond/branch_0_fun/ppermute | solution.py:548
  31.6 10.2 %collective-permute-start.2 = (bf16[48,1024]{1,0:T(8,128)(2,1)S(1)}, bf16[48,1024]{1,0:T(8,128)(2,1)S(1)}, u32[]{:S(2)}, u32[]{:S(2)}) collective-permute-start(bf16[48,1024]{1,0:T(8,128)(2,1)S(1)} %get-tuple-element.152), channel_id=1, source_target_pairs={{0,4},{2,6},{4,8},{6,10},{8,12},{10,14},{12,0},{14,2},{1,5},{3,7},... | collective-permute-start | bytes 294920 | tf_op jit(solution)/shard_map/cond/branch_0_fun/ppermute | solution.py:94
  32.0 10.8 %collective-permute-start.3 = (bf16[48,1024]{1,0:T(8,128)(2,1)S(1)}, bf16[48,1024]{1,0:T(8,128)(2,1)S(1)}, u32[]{:S(2)}, u32[]{:S(2)}) collective-permute-start(bf16[48,1024]{1,0:T(8,128)(2,1)S(1)} %get-tuple-element.153), channel_id=1, source_target_pairs={{0,8},{2,10},{4,12},{6,14},{8,0},{10,2},{12,4},{14,6},{1,9},{3,11}... | collective-permute-start | bytes 294920 | tf_op jit(solution)/shard_map/cond/branch_0_fun/ppermute | solution.py:94
  35.5 7.4 %collective-permute-start.4 = (bf16[48,1024]{1,0:T(8,128)(2,1)S(1)}, bf16[48,1024]{1,0:T(8,128)(2,1)S(1)}, u32[]{:S(2)}, u32[]{:S(2)}) collective-permute-start(bf16[48,1024]{1,0:T(8,128)(2,1)S(1)} %get-tuple-element.154), channel_id=1, source_target_pairs={{0,12},{2,14},{4,0},{6,2},{8,4},{10,6},{12,8},{14,10},{1,13},{3,15... | collective-permute-start | bytes 294920 | tf_op jit(solution)/shard_map/cond/branch_0_fun/ppermute | solution.py:94
  43.8 5.9 %collective-permute-start.6 = (bf16[64,1024]{1,0:T(8,128)(2,1)S(1)}, bf16[64,1024]{1,0:T(8,128)(2,1)S(1)}, u32[]{:S(2)}, u32[]{:S(2)}) collective-permute-start(bf16[64,1024]{1,0:T(8,128)(2,1)S(1)} %get-tuple-element.160), channel_id=1, source_target_pairs={{0,2},{2,0},{4,6},{6,4},{8,10},{10,8},{12,14},{14,12},{1,3},{3,1},... | collective-permute-start | bytes 393224 | tf_op jit(solution)/shard_map/cond/branch_0_fun/ppermute | solution.py:610
  49.7 10.4 %collective-permute-start.8 = (bf16[32,2048]{1,0:T(8,128)(2,1)S(1)}, bf16[32,2048]{1,0:T(8,128)(2,1)S(1)}, u32[]{:S(2)}, u32[]{:S(2)}) collective-permute-start(bf16[32,2048]{1,0:T(8,128)(2,1)S(1)} %get-tuple-element.170), channel_id=1, source_target_pairs={{0,2},{2,0},{4,6},{6,4},{8,10},{10,8},{12,14},{14,12},{1,3},{3,1},... | collective-permute-start | bytes 393224 | tf_op jit(solution)/shard_map/cond/branch_0_fun/ppermute | solution.py:613
  50.9 9.1 %collective-permute-start.9 = (bf16[32,1024]{1,0:T(8,128)(2,1)S(1)}, bf16[32,1024]{1,0:T(8,128)(2,1)S(1)}, u32[]{:S(2)}, u32[]{:S(2)}) collective-permute-start(bf16[32,1024]{1,0:T(8,128)(2,1)S(1)} %get-tuple-element.172), channel_id=1, source_target_pairs={{0,4},{2,6},{4,8},{6,10},{8,12},{10,14},{12,0},{14,2},{1,5},{3,7},... | collective-permute-start | bytes 196616 | tf_op jit(solution)/shard_map/cond/branch_0_fun/ppermute | solution.py:94
  53.6 6.5 %collective-permute-start.10 = (bf16[32,1024]{1,0:T(8,128)(2,1)S(1)}, bf16[32,1024]{1,0:T(8,128)(2,1)S(1)}, u32[]{:S(2)}, u32[]{:S(2)}) collective-permute-start(bf16[32,1024]{1,0:T(8,128)(2,1)S(1)} %get-tuple-element.173), channel_id=1, source_target_pairs={{0,8},{2,10},{4,12},{6,14},{8,0},{10,2},{12,4},{14,6},{1,9},{3,11}... | collective-permute-start | bytes 196616 | tf_op jit(solution)/shard_map/cond/branch_0_fun/ppermute | solution.py:94
  54.2 5.9 %collective-permute-start.11 = (bf16[32,1024]{1,0:T(8,128)(2,1)S(1)}, bf16[32,1024]{1,0:T(8,128)(2,1)S(1)}, u32[]{:S(2)}, u32[]{:S(2)}) collective-permute-start(bf16[32,1024]{1,0:T(8,128)(2,1)S(1)} %get-tuple-element.174), channel_id=1, source_target_pairs={{0,12},{2,14},{4,0},{6,2},{8,4},{10,6},{12,8},{14,10},{1,13},{3,15... | collective-permute-start | bytes 196616 | tf_op jit(solution)/shard_map/cond/branch_0_fun/ppermute | solution.py:94
  60.1 5.5 %collective-permute-start.12 = (bf16[32,2048]{1,0:T(8,128)(2,1)S(1)}, bf16[32,2048]{1,0:T(8,128)(2,1)S(1)}, u32[]{:S(2)}, u32[]{:S(2)}) collective-permute-start(bf16[32,2048]{1,0:T(8,128)(2,1)S(1)} %get-tuple-element.181), channel_id=1, source_target_pairs={{0,2},{2,0},{4,6},{6,4},{8,10},{10,8},{12,14},{14,12},{1,3},{3,1},... | collective-permute-start | bytes 393224 | tf_op jit(solution)/shard_map/cond/branch_0_fun/ppermute | solution.py:620
  61.9 3.7 %collective-permute-start.14 = (f32[16,64]{1,0:T(8,128)S(1)}, f32[16,64]{1,0:T(8,128)S(1)}, u32[]{:S(2)}, u32[]{:S(2)}) collective-permute-start(f32[16,64]{1,0:T(8,128)S(1)} %branch_0_fun.18.refs_4_), channel_id=1, source_target_pairs={{0,2},{2,0},{4,6},{6,4},{8,10},{10,8},{12,14},{14,12},{1,3},{3,1},... | collective-permute-start | bytes 12296 | tf_op jit(solution)/shard_map/cond/branch_0_fun/ppermute | solution.py:631
  66.2 6.8 %collective-permute-start.16 = (bf16[8,4096]{1,0:T(8,128)(2,1)S(1)}, bf16[8,4096]{1,0:T(8,128)(2,1)S(1)}, u32[]{:S(2)}, u32[]{:S(2)}) collective-permute-start(bf16[8,4096]{1,0:T(8,128)(2,1)S(1)} %get-tuple-element.190), channel_id=1, source_target_pairs={{0,4},{2,6},{4,8},{6,10},{8,12},{10,14},{12,0},{14,2},{1,5},{3,7},... | collective-permute-start | bytes 196616 | tf_op jit(solution)/shard_map/cond/branch_0_fun/ppermute | solution.py:94
  68.1 7.0 %collective-permute-start.17 = (bf16[8,4096]{1,0:T(8,128)(2,1)S(1)}, bf16[8,4096]{1,0:T(8,128)(2,1)S(1)}, u32[]{:S(2)}, u32[]{:S(2)}) collective-permute-start(bf16[8,4096]{1,0:T(8,128)(2,1)S(1)} %get-tuple-element.191), channel_id=1, source_target_pairs={{0,8},{2,10},{4,12},{6,14},{8,0},{10,2},{12,4},{14,6},{1,9},{3,11}... | collective-permute-start | bytes 196616 | tf_op jit(solution)/shard_map/cond/branch_0_fun/ppermute | solution.py:94
  69.0 6.0 %collective-permute-start.18 = (bf16[8,4096]{1,0:T(8,128)(2,1)S(1)}, bf16[8,4096]{1,0:T(8,128)(2,1)S(1)}, u32[]{:S(2)}, u32[]{:S(2)}) collective-permute-start(bf16[8,4096]{1,0:T(8,128)(2,1)S(1)} %get-tuple-element.192), channel_id=1, source_target_pairs={{0,12},{2,14},{4,0},{6,2},{8,4},{10,6},{12,8},{14,10},{1,13},{3,15... | collective-permute-start | bytes 196616 | tf_op jit(solution)/shard_map/cond/branch_0_fun/ppermute | solution.py:94
  (7 other events, 33.0 us)
